TPU v7x, 128 devices: a whole 4x4x4 slice. The times are simulated.
128 devices in a mesh: blk: 16 (over x_hi, z, core), near: 8 (over x_lo, y).
Axes of the slice: x: 4 (x_hi: 2, x_lo: 2; x = x_hi * 2 + x_lo), y: 4, z: 4, core: 2. Of those that a mesh axis runs over, the one named last changes fastest.
Arguments:
- rhs_block: bfloat16 [16, 16, 256, 256], P('blk', 'near'), may hold values from -18 to 18
- far_u: bfloat16 [256, 16, 16, 32, 256], P('blk', None, 'near'), may hold values from -0.09375 to 0.09375
- far_w: bfloat16 [256, 16, 16, 32, 256], P('blk', None, 'near'), may hold values from -0.375 to 0.375
- far_ranks: int32 [256, 16, 16], P('blk', None, 'near'), may hold values from 8 to 32
- near_tiles: bfloat16 [16, 16, 8, 256, 256], P('blk', 'near'), may hold values from -6 to 6
- near_cols: int32 [16, 16, 8], P('blk'), may hold values from 0 to 15, as said below
- near_count: int32 [16, 16], P('blk'), may hold values from 1 to 8, as said below
Outputs:
- second_basis: bfloat16 [16, 16, 256, 256], P('blk', 'near')
- second_image: float32 [16, 16, 256, 256], P('blk', 'near')
- coefficients: float32 [2, 256], replicated
Inputs may be any that keep to these rules, and one draw needn't show every extreme that they name: `near_cols`: slot 0 of every block row is the row's own block; the slots of one row name distinct blocks of its panel. `near_count`: some block row has all 8 slots live.
All inputs are finite; a program needn't handle non-finite values.
Results may differ from a plain program's by a relative error of at most 0.015.
Values may be sent and summed in bfloat16 or wider, within the bound.
No kernel may reach another device: no remote copies, remote signals or barrier semaphores. Data moves between devices by JAX's collectives and lax.ppermute only.
A program may use at most 128 MiB of HBM per device.

v0:
```python
import jax
import jax.numpy as jnp
from jax import lax
from jax.sharding import PartitionSpec as P


def body(rhs_block, far_u, far_w, far_ranks, near_tiles, near_cols, near_count):
    panel_count = lax.axis_size("blk")
    slice_count = lax.axis_size("near")
    my_panel = lax.axis_index("blk")
    my_slice = lax.axis_index("near")
    per_dev = rhs_block.shape[1]
    block_size = rhs_block.shape[2]
    total_rows = per_dev * block_size * panel_count * slice_count
    slots = near_cols.shape[2]
    rank = far_u.shape[3]
    all_cols = near_cols[0]
    slot_live = jnp.arange(slots, dtype=jnp.int32)[None, :] < near_count[0][:, None]
    mine = my_slice * per_dev + jnp.arange(per_dev, dtype=jnp.int32)
    is_near = jnp.any((all_cols[:, :, None] == mine[None, None, :]) & slot_live[:, :, None], axis=1)
    same_panel = jnp.arange(panel_count, dtype=jnp.int32) == my_panel
    near_pair = same_panel[None, :, None] & is_near[:, None, :]
    ranked = jnp.arange(rank, dtype=jnp.int32)[None, None, None, :] < far_ranks[..., None]
    keep = (ranked & jnp.logical_not(near_pair)[..., None]).astype(jnp.float32)
    my_cols = lax.dynamic_slice_in_dim(all_cols, my_slice * per_dev, per_dev, 0)
    my_count = lax.dynamic_slice_in_dim(near_count[0], my_slice * per_dev, per_dev, 0)
    my_live = jnp.arange(slots, dtype=jnp.int32)[None, :] < my_count[:, None]
    tiles = near_tiles[0]

    def apply_matrix(field):
        coded = jnp.einsum(
            "imprs,mpsc->imprc",
            far_w,
            lax.all_gather(field, "blk", axis=0, tiled=True),
            preferred_element_type=jnp.float32,
        )
        coded = (coded * keep[..., None]).astype(jnp.bfloat16)
        far_total = jnp.einsum("imprs,imprc->isc", far_u, coded, preferred_element_type=jnp.float32)
        far_mine = lax.psum_scatter(
            far_total.astype(jnp.bfloat16), "near", scatter_dimension=0, tiled=True
        ).astype(jnp.float32)
        panel_field = lax.all_gather(field, "near", axis=1, tiled=True)[0]
        sources = panel_field[my_cols]
        sources = jnp.where(my_live[:, :, None, None], sources, jnp.zeros_like(sources))
        near_part = jnp.einsum("pkst,pktc->psc", tiles, sources, preferred_element_type=jnp.float32)
        return (far_mine + near_part)[None]

    start = rhs_block.astype(jnp.float32)
    mean_start = lax.psum(jnp.sum(start * start, axis=(0, 1, 2)), ("blk", "near")) / total_rows
    first = (start * lax.rsqrt(mean_start + 1e-06)).astype(jnp.bfloat16)
    image = apply_matrix(first)
    first_f = first.astype(jnp.float32)
    proj = lax.psum(jnp.sum(first_f * image, axis=(0, 1, 2)), ("blk", "near")) / total_rows
    rest = image - proj * first_f
    mean_rest = lax.psum(jnp.sum(rest * rest, axis=(0, 1, 2)), ("blk", "near")) / total_rows
    second_basis = (rest * lax.rsqrt(mean_rest + 1e-06)).astype(jnp.bfloat16)
    second_image = apply_matrix(second_basis)
    coefficients = jnp.stack([proj, jnp.sqrt(mean_rest + 1e-06)])
    return (second_basis, second_image, coefficients)


def solution(mesh):
    placed = (
        P("blk", "near", None, None),
        P("blk", None, "near", None, None),
        P("blk", None, "near", None, None),
        P("blk", None, "near"),
        P("blk", "near", None, None, None),
        P("blk", None, None),
        P("blk", None),
    )
    return jax.shard_map(
        body,
        mesh=mesh,
        in_specs=placed,
        out_specs=(P("blk", "near", None, None), P("blk", "near", None, None), P()),
        check_vma=False,
    )
```

profile of v0, /device:TPU:0, one launch (start us, length us, event | category | flops | bytes accessed | tf_op | source)
XLA Modules:
  0.0 493.9 jit_solution(5304383496619594118)
XLA Ops:
  7.2 0.0 copy-start
  7.2 0.0 all-gather.5.cloned.1.call-start
  7.2 1.2 copy.32
  8.5 0.1 fusion.68
  8.6 68.2 %psum.21 = f32[256]{0:T(256)S(1)} all-reduce(f32[256]{0:T(256)S(1)} %fusion.68), channel_id=1, replica_groups=mesh['blk'=16,'near'=8] {'blk','near'}, use_global_device_ids=true, to_apply=%region_1.0 | all-reduce | flops 256 | bytes 2048 | tf_op jit(solution)/shard_map/psum | solution.py:49
  76.8 0.1 fusion.69
  76.9 0.8 copy.33
  77.8 0.0 all-gather.5.cloned.1.call-update
  77.8 0.0 all-gather.7.cloned.1.call-start
  77.8 0.8 copy.38
  78.7 0.0 all-gather.7.cloned.1.call-update
  78.7 0.0 reduce-scatter.3.cloned.1.call-start
  78.8 0.7 iota_compare_fusion
  79.4 0.8 and_reduce_fusion
  80.2 0.1 copy.35
  80.3 0.9 copy.34
  81.2 0.1 and_not_fusion
  81.3 0.7 and_convert_fusion
  82.0 47.5 %all-gather.5.cloned.1.call-done = bf16[16,2,256,256]{3,2,1,0:T(8,128)(2,1)} async-done(((bf16[1,2,256,256]{3,2,1,0:T(8,128)(2,1)}), bf16[16,2,256,256]{3,2,1,0:T(8,128)(2,1)}) %all-gather.5.cloned.1.call-update) | async-done | bytes 4194320 | tf_op jit(solution)/shard_map/all_gather | solution.py:34
  129.5 8.1 %fusion.1 = bf16[16,16,2,32,256]{4,3,2,1,0:T(8,128)(2,1)} fusion(bf16[16,16,2,32,256]{4,3,2,1,0:T(8,128)(2,1)} %param.9, f32[16,16,2,32]{3,2,1,0:T(2,128)S(1)} %and_convert_fusion, bf16[16,2,256,256]{3,2,1,0:T(8,128)(2,1)} %all-gather.5.cloned.1.call-done), kind=kOutput, calls=%fused_computation.5 | convolution fusion | flops 2155872256 | bytes 21037056 | tf_op jit(solution)/shard_map/imprs,mpsc->imprc/dot_general | solution.py:31
  137.7 0.0 copy-start.1
  137.7 0.0 copy-start.2
  137.7 9.7 %fusion.26 = bf16[16,256,256]{1,2,0:T(8,128)(2,1)} fusion(bf16[16,16,2,32,256]{4,3,2,1,0:T(8,128)(2,1)} %param.8, bf16[16,16,2,32,256]{4,3,2,1,0:T(8,128)(2,1)} %fusion.1), kind=kOutput, calls=%fused_computation.24 | convolution fusion | flops 2148532224 | bytes 18874368 | tf_op jit(solution)/shard_map/imprs,imprc->isc/dot_general | solution.py:38
  147.4 0.0 reduce-scatter.3.cloned.1.call-update
  147.4 0.0 all-gather.9.cloned.1.call-start
  147.4 0.0 copy-done.1
  147.4 0.1 constant_dynamic-slice_fusion
  147.5 0.1 copy.39
  147.6 0.1 reshape.114
  147.7 0.0 copy-done.2
  147.7 0.1 dynamic-slice_bitcast_fusion
  147.8 0.1 iota_compare_fusion.1
  147.9 23.1 %all-gather.7.cloned.1.call-done = bf16[1,16,256,256]{3,2,0,1:T(8,128)(2,1)} async-done(((bf16[1,2,256,256]{3,2,0,1:T(8,128)(2,1)}), bf16[1,16,256,256]{3,2,0,1:T(8,128)(2,1)}) %all-gather.7.cloned.1.call-update) | async-done | bytes 2097168 | tf_op jit(solution)/shard_map/all_gather | solution.py:42
  171.0 3.6 gather_fusion
  174.5 4.0 copy.40
  178.5 37.1 %reduce-scatter.3.cloned.1.call-done = bf16[2,256,256]{1,2,0:T(8,128)(2,1)} async-done(((bf16[16,256,256]{1,2,0:T(8,128)(2,1)}), bf16[2,256,256]{1,2,0:T(8,128)(2,1)}) %reduce-scatter.3.cloned.1.call-update) | async-done | bytes 262160 | tf_op jit(solution)/shard_map/reduce_scatter | solution.py:39
  215.6 0.0 copy-done
  215.6 2.4 fusion.70
  218.0 63.9 %psum.22 = f32[256]{0:T(256)S(1)} all-reduce(f32[256]{0:T(256)S(1)} %get-tuple-element.14), channel_id=1, replica_groups=mesh['blk'=16,'near'=8] {'blk','near'}, use_global_device_ids=true, to_apply=%region_5.6 | all-reduce | flops 256 | bytes 2048 | tf_op jit(solution)/shard_map/psum | solution.py:53
  281.9 0.3 multiply_reduce_fusion
  282.2 62.5 %psum.23 = f32[256]{0:T(256)S(1)} all-reduce(f32[256]{0:T(256)S(1)} %multiply_reduce_fusion), channel_id=1, replica_groups=mesh['blk'=16,'near'=8] {'blk','near'}, use_global_device_ids=true, to_apply=%region_7.8 | all-reduce | flops 256 | bytes 2048 | tf_op jit(solution)/shard_map/psum | solution.py:55
  344.7 0.2 multiply_convert_fusion
  344.9 0.8 copy.48
  345.7 0.0 all-gather.9.cloned.1.call-update
  345.7 0.0 all-gather.11.cloned.1.call-start
  345.8 0.8 copy.46
  346.6 0.0 all-gather.11.cloned.1.call-update
  346.6 0.2 reduce-scatter.5.cloned.1.call-start
  346.9 51.3 %all-gather.9.cloned.1.call-done = bf16[16,2,256,256]{3,2,1,0:T(8,128)(2,1)} async-done(((bf16[1,2,256,256]{3,2,1,0:T(8,128)(2,1)}), bf16[16,2,256,256]{3,2,1,0:T(8,128)(2,1)}) %all-gather.9.cloned.1.call-update) | async-done | bytes 4194320 | tf_op jit(solution)/shard_map/all_gather | solution.py:34
  398.2 8.1 %fusion = bf16[16,16,2,32,256]{4,3,2,1,0:T(8,128)(2,1)} fusion(bf16[16,16,2,32,256]{4,3,2,1,0:T(8,128)(2,1)} %param.9, f32[16,16,2,32]{3,2,1,0:T(2,128)S(1)} %and_convert_fusion, bf16[16,2,256,256]{3,2,1,0:T(8,128)(2,1)} %all-gather.9.cloned.1.call-done), kind=kOutput, calls=%fused_computation.3 | convolution fusion | flops 2155872256 | bytes 21037056 | tf_op jit(solution)/shard_map/imprs,mpsc->imprc/dot_general | solution.py:31
  406.3 9.6 %fusion.31 = bf16[16,256,256]{1,2,0:T(8,128)(2,1)} fusion(bf16[16,16,2,32,256]{4,3,2,1,0:T(8,128)(2,1)} %param.8, bf16[16,16,2,32,256]{4,3,2,1,0:T(8,128)(2,1)} %fusion), kind=kOutput, calls=%fused_computation.25 | convolution fusion | flops 2148532224 | bytes 18874368 | tf_op jit(solution)/shard_map/imprs,imprc->isc/dot_general | solution.py:38
  416.0 0.0 reduce-scatter.5.cloned.1.call-update
  416.0 0.6 pad_maximum_fusion
  416.6 22.8 %all-gather.11.cloned.1.call-done = bf16[1,16,256,256]{3,2,0,1:T(8,128)(2,1)} async-done(((bf16[1,2,256,256]{3,2,0,1:T(8,128)(2,1)}), bf16[1,16,256,256]{3,2,0,1:T(8,128)(2,1)}) %all-gather.11.cloned.1.call-update) | async-done | bytes 2097168 | tf_op jit(solution)/shard_map/all_gather | solution.py:42
  439.4 3.6 gather_fusion.1
  443.0 4.0 copy.47
  446.9 36.8 %reduce-scatter.5.cloned.1.call-done = bf16[2,256,256]{1,2,0:T(8,128)(2,1)} async-done(((bf16[16,256,256]{1,2,0:T(8,128)(2,1)}), bf16[2,256,256]{1,2,0:T(8,128)(2,1)}) %reduce-scatter.5.cloned.1.call-update) | async-done | bytes 262160 | tf_op jit(solution)/shard_map/reduce_scatter | solution.py:39
  483.7 2.3 fusion.51
  486.1 1.0 copy.49
  (7 shorter events, 0.0 us)
Async XLA Ops:
  7.2 208.4 %copy-start = (bf16[1,2,8,256,256]{4,3,2,1,0:T(8,128)(2,1)S(1)}, bf16[1,2,8,256,256]{4,3,2,1,0:T(8,128)(2,1)}, u32[]{:S(2)}) copy-start(bf16[1,2,8,256,256]{4,3,2,1,0:T(8,128)(2,1)} %param.11) | copy-start | bytes 6291460
  7.2 122.3 %all-gather.5.cloned.1.call-start = ((), (), s32[]{:S(2)}) async-start(), calls=%async_computation.2 | async-start | bytes 4456448 | tf_op jit(solution)/shard_map/all_gather | solution.py:34
  77.8 93.2 %all-gather.7.cloned.1.call-start = ((), (), s32[]{:S(2)}) async-start(), calls=%async_computation.4 | async-start | bytes 2359296 | tf_op jit(solution)/shard_map/all_gather | solution.py:42
  78.7 136.9 %reduce-scatter.3.cloned.1.call-start = ((), (), s32[]{:S(2)}) async-start(), calls=%async_computation.3 | async-start | bytes 2359296 | tf_op jit(solution)/shard_map/reduce_scatter | solution.py:39
  137.7 9.8 %copy-start.1 = (s32[1,16,8]{1,2,0:T(8,128)S(1)}, s32[1,16,8]{1,2,0:T(8,128)}, u32[]{:S(2)}) copy-start(s32[1,16,8]{1,2,0:T(8,128)} %param.12) | copy-start | bytes 1540
  137.7 10.0 %copy-start.2 = (s32[1,16]{1,0:T(1,128)S(1)}, s32[1,16]{1,0:T(1,128)}, u32[]{:S(2)}) copy-start(s32[1,16]{1,0:T(1,128)} %param.13) | copy-start | bytes 196
  147.4 250.8 %all-gather.9.cloned.1.call-start = ((), (), s32[]{:S(2)}) async-start(), calls=%async_computation.5 | async-start | bytes 4456448 | tf_op jit(solution)/shard_map/all_gather | solution.py:34
  345.7 93.7 %all-gather.11.cloned.1.call-start = ((), (), s32[]{:S(2)}) async-start(), calls=%async_computation.7 | async-start | bytes 2359296 | tf_op jit(solution)/shard_map/all_gather | solution.py:42
  346.6 137.1 %reduce-scatter.5.cloned.1.call-start = ((), (), s32[]{:S(2)}) async-start(), calls=%async_computation.6 | async-start | bytes 2359296 | tf_op jit(solution)/shard_map/reduce_scatter | solution.py:39
Sparse Core Ops, SparseCore 0:
  77.9 51.5 all-gather.4
  131.7 39.1 all-gather.6
  173.4 42.1 reduce-scatter.2
  345.8 52.3 all-gather.8
  400.3 39.0 all-gather.10
  441.7 42.0 reduce-scatter.4
where the time goes:
time: 495 us; the launch traced here: 494 us
  waiting for transfers between devices  219 us (44%)
  blocking collectives  195 us (39%)
  matrix products  40.4 us (8%)
  local copies, waits for them, and re-layouts  21.9 us (4%)
  between operations  14.2 us (3%)
    all_gather x2, waiting for transfers between devices, apply_matrix(): lax.all_gather(field, 'blk', axis=0, tiled=True)  98.9 us
    reduce_scatter x2, waiting for transfers between devices, apply_matrix(): lax.psum_scatter(far_total.astype(jnp.bfloat16), 'near', scatter_dimensio...  73.9 us
    psum x1, blocking collectives, body(): lax.psum(jnp.sum(start * start, axis=(0, 1, 2)), ('blk', 'near'))  68.2 us
    psum x1, blocking collectives, body(): lax.psum(jnp.sum(first_f * image, axis=(0, 1, 2)), ('blk', 'near'))  63.9 us
    psum x1, blocking collectives, body(): lax.psum(jnp.sum(rest * rest, axis=(0, 1, 2)), ('blk', 'near')) / total_rows  62.5 us
    all_gather x2, waiting for transfers between devices, apply_matrix(): panel_field = lax.all_gather(field, 'near', axis=1, tiled=True)[0]  45.9 us
    dot_general x2, matrix products, apply_matrix(): jnp.einsum('imprs,imprc->isc', far_u, coded, preferred_element_type=jnp.f...  19.3 us
    dot_general x2, matrix products, apply_matrix(): jnp.einsum('imprs,mpsc->imprc', far_w, lax.all_gather(field, 'blk', axis=...  16.3 us
  transfers between devices with their start and end apart: 6, of which 6 were waited for; matrix products, arithmetic and copies ran while one was open for 11% of the time, Pallas kernels for 0%

commit v1 on v0

v1 whole, which is shorter than its diff:
```python
import functools

import jax
import jax.numpy as jnp
from jax import lax
from jax.experimental import pallas as pl
from jax.experimental.pallas import tpu as pltpu
from jax.sharding import PartitionSpec as P

EPS = 1e-06
EXTRA = 16
MIB = 1 << 20


def put_sums(sums, width):
    rows = []
    for value in sums:
        high = value.astype(jnp.bfloat16)
        left = value - high.astype(jnp.float32)
        middle = left.astype(jnp.bfloat16)
        low = (left - middle.astype(jnp.float32)).astype(jnp.bfloat16)
        rows += [high, middle, low]
    rows.append(jnp.zeros((EXTRA - len(rows), width), jnp.bfloat16))
    return jnp.concatenate(rows, axis=0)


def get_sums(rows):
    return (
        rows[0:1] + rows[1:2] + rows[2:3],
        rows[3:4] + rows[4:5] + rows[5:6],
    )


def whole(shape):
    return pl.BlockSpec(shape, lambda *_: (0,) * len(shape))


def start_kernel(x_ref, own_ref, out_ref):
    copies, rows, width = out_ref.shape
    per_dev, size, _ = x_ref.shape
    square = jnp.zeros((1, width), jnp.float32)
    cross = jnp.zeros((1, width), jnp.float32)
    for p in range(per_dev):
        x = x_ref[p]
        x_f = x.astype(jnp.float32)
        image = jnp.dot(own_ref[p, 0], x, preferred_element_type=jnp.float32)
        square += jnp.sum(x_f * x_f, axis=0, keepdims=True)
        cross += jnp.sum(x_f * image, axis=0, keepdims=True)
        for k in range(copies):
            out_ref[k, p * size : (p + 1) * size, :] = x
    extra = put_sums((square, cross), width)
    for k in range(copies):
        out_ref[k, per_dev * size :, :] = extra


def far_kernel(
    place_ref, rank_ref, w_ref, u_ref, p00, p10, p01, p11, out_ref, coded_ref, sums_ref,
    *, zs, per_dev, targets, rank, size,
):
    step = pl.program_id(0)
    half = 2 * zs
    width = out_ref.shape[2]
    blocks = per_dev * size
    xh, core = place_ref[0], place_ref[1]

    @pl.when(step == 0)
    def _():
        sums_ref[...] = jnp.zeros_like(sums_ref)

    def code(side, mine, other):
        z = step - side * zs
        pair = (jnp.where(side == 1, 1 - xh, xh) * zs + z) * 2
        row = lax.broadcasted_iota(jnp.int32, (rank, width), 0)
        for turn, source in ((0, mine), (1, other)):
            which = core if turn == 0 else 1 - core
            panel = pair + which
            sums_ref[...] += source[0, blocks:, :].astype(jnp.float32)
            for p in range(per_dev):
                w = w_ref[:, which, p].reshape(targets * rank, size)
                field = source[0, p * size : (p + 1) * size, :]
                value = jnp.dot(w, field, preferred_element_type=jnp.float32)
                for i in range(targets):
                    live = rank_ref[panel * per_dev + p, i]
                    part = value[i * rank : (i + 1) * rank]
                    part = jnp.where(row < live, part, 0.0).astype(jnp.bfloat16)
                    coded_ref[i, panel, p * rank : (p + 1) * rank, :] = part

    @pl.when(step < zs)
    def _():
        code(0, p00, p01)

    @pl.when((step >= zs) & (step < half))
    def _():
        code(1, p10, p11)

    @pl.when(step >= half)
    def _():
        first = (step - half) * per_dev
        for p in range(per_dev):
            u = u_ref[p].reshape(-1, size)
            value = coded_ref[first + p].reshape(-1, width)
            total = lax.dot_general(
                u, value, (((0,), (0,)), ((), ())), preferred_element_type=jnp.float32
            )
            out_ref[0, p * size : (p + 1) * size, :] = total.astype(jnp.bfloat16)
        out_ref[0, blocks:, :] = put_sums(get_sums(sums_ref[...]), width)


def row_image(cols_ref, count_ref, far_ref, tiles_ref, panel_ref, p, total_ref):
    size = tiles_ref.shape[2]
    senders = far_ref.shape[0]
    total = far_ref[0, p * size : (p + 1) * size, :].astype(jnp.float32)
    for s in range(1, senders):
        total += far_ref[s, p * size : (p + 1) * size, :].astype(jnp.float32)
    total_ref[...] = total
    for k in range(tiles_ref.shape[1]):

        @pl.when(k < count_ref[p])
        def _():
            total_ref[...] += jnp.dot(
                tiles_ref[p, k], panel_ref[cols_ref[p, k]], preferred_element_type=jnp.float32
            )

    return total_ref[...]


def far_sums(far_ref):
    senders, rows, _ = far_ref.shape
    total = far_ref[0, rows - EXTRA :, :].astype(jnp.float32)
    for s in range(1, senders):
        total += far_ref[s, rows - EXTRA :, :].astype(jnp.float32)
    return get_sums(total)


def middle_kernel(
    cols_ref, count_ref, far_ref, tiles_ref, panel_ref, x_ref,
    image_ref, z_ref, out_ref, sums_ref, total_ref, *, total_rows,
):
    copies, _, width = out_ref.shape
    per_dev, size, _ = x_ref.shape
    square_x, cross_x = far_sums(far_ref)
    guess = cross_x / (square_x + EPS * total_rows)
    sums_ref[0:1, :] = square_x
    sums_ref[1:2, :] = guess
    cross = jnp.zeros((1, width), jnp.float32)
    square = jnp.zeros((1, width), jnp.float32)
    for p in range(per_dev):
        image = row_image(cols_ref, count_ref, far_ref, tiles_ref, panel_ref, p, total_ref)
        image_ref[p] = image
        x = x_ref[p].astype(jnp.float32)
        moved = image - guess * x
        cross += jnp.sum(x * moved, axis=0, keepdims=True)
        square += jnp.sum(moved * moved, axis=0, keepdims=True)
        z = moved.astype(jnp.bfloat16)
        z_ref[p] = z
        for k in range(copies):
            out_ref[k, p * size : (p + 1) * size, :] = z
    extra = put_sums((cross, square), width)
    for k in range(copies):
        out_ref[k, per_dev * size :, :] = extra


def last_kernel(
    cols_ref, count_ref, far_ref, tiles_ref, panel_ref, x_ref, image_ref, sums_ref,
    basis_ref, out_ref, coef_ref, total_ref, *, total_rows,
):
    per_dev = x_ref.shape[0]
    cross, square = far_sums(far_ref)
    cross, square = cross / total_rows, square / total_rows
    mean_x = sums_ref[0:1, :] / total_rows
    guess = sums_ref[1:2, :]
    scale = lax.rsqrt(mean_x + EPS)
    proj = scale * scale * (cross + guess * mean_x)
    off = proj - guess
    mean_rest = scale * scale * (square - 2.0 * off * cross + off * off * mean_x)
    mean_rest = jnp.maximum(mean_rest, 0.0) + EPS
    factor = scale * lax.rsqrt(mean_rest)
    coef_ref[0:1, :] = proj
    coef_ref[1:2, :] = jnp.sqrt(mean_rest)
    for p in range(per_dev):
        image = image_ref[p]
        x = x_ref[p].astype(jnp.float32)
        basis_ref[p] = ((image - guess * x - off * x) * factor).astype(jnp.bfloat16)
        second = row_image(cols_ref, count_ref, far_ref, tiles_ref, panel_ref, p, total_ref)
        out_ref[p] = (second - off * image) * factor


def body(rhs_block, far_u, far_w, far_ranks, near_tiles, near_cols, near_count):
    panel_count = lax.axis_size("blk")
    slice_count = lax.axis_size("near")
    my_panel = lax.axis_index("blk")
    my_slice = lax.axis_index("near")
    per_dev, size, width = rhs_block.shape[1:]
    total_rows = float(per_dev * size * panel_count * slice_count)
    slots = near_cols.shape[2]
    targets = far_u.shape[0]
    rank = far_u.shape[3]
    zs = panel_count // 4
    rows = per_dev * size + EXTRA
    bf16, f32 = jnp.bfloat16, jnp.float32

    x = rhs_block[0]
    tiles = near_tiles[0]
    place = jnp.stack([my_panel // (2 * zs), my_panel % 2]).astype(jnp.int32)
    slot_live = jnp.arange(slots, dtype=jnp.int32)[None, :] < near_count[0][:, None]
    mine = my_slice * per_dev + jnp.arange(per_dev, dtype=jnp.int32)
    is_near = jnp.any((near_cols[0][:, :, None] == mine) & slot_live[:, :, None], axis=1)
    same = jnp.arange(panel_count, dtype=jnp.int32) == my_panel
    near_pair = same[:, None, None] & is_near.T[None]
    ranks = jnp.where(near_pair, 0, far_ranks.transpose(1, 2, 0)).reshape(-1, targets)
    my_cols = lax.dynamic_slice_in_dim(near_cols[0], my_slice * per_dev, per_dev, 0)
    my_count = lax.dynamic_slice_in_dim(near_count[0], my_slice * per_dev, per_dev, 0)

    z_groups = [[h * 2 * zs + z * 2 + c for z in range(zs)] for h in range(2) for c in range(2)]
    flip_x = [(i, (i + 2 * zs) % panel_count) for i in range(panel_count)]
    flip_core = [(i, i ^ 1) for i in range(panel_count)]

    def gather_panels(payload):
        crossed = lax.ppermute(payload[0], "blk", flip_x)
        here = lax.all_to_all(payload, "blk", 0, 0, tiled=True, axis_index_groups=z_groups)
        here_other = lax.ppermute(here, "blk", flip_core)
        crossed = jnp.broadcast_to(crossed[None], payload.shape)
        there = lax.all_to_all(crossed, "blk", 0, 0, tiled=True, axis_index_groups=z_groups)
        there_other = lax.ppermute(there, "blk", flip_core)
        return here, there, here_other, there_other

    def far_products(gathered):
        half = 2 * zs
        own = lambda j, *_: (jnp.minimum(j, zs - 1), 0, 0)
        far = lambda j, *_: (jnp.clip(j - zs, 0, zs - 1), 0, 0)

        def w_block(j, place_ref, rank_ref):
            j = jnp.minimum(j, half - 1)
            side = j // zs
            xh = place_ref[0]
            return (0, jnp.where(side == 1, 1 - xh, xh) * zs + j % zs, 0, 0, 0)

        last = lambda j, *_: (jnp.maximum(j - half, 0), 0, 0)
        u_block = lambda j, *_: (jnp.maximum(j - half, 0), 0, 0, 0, 0)
        return pl.pallas_call(
            functools.partial(
                far_kernel, zs=zs, per_dev=per_dev, targets=targets, rank=rank, size=size
            ),
            out_shape=jax.ShapeDtypeStruct((slice_count, rows, width), bf16),
            grid_spec=pltpu.PrefetchScalarGridSpec(
                num_scalar_prefetch=2,
                grid=(half + slice_count,),
                in_specs=[
                    pl.BlockSpec((targets, 2, per_dev, rank, size), w_block),
                    pl.BlockSpec((per_dev, panel_count, per_dev, rank, size), u_block),
                    pl.BlockSpec((1, rows, width), own),
                    pl.BlockSpec((1, rows, width), far),
                    pl.BlockSpec((1, rows, width), own),
                    pl.BlockSpec((1, rows, width), far),
                ],
                out_specs=pl.BlockSpec((1, rows, width), last),
                scratch_shapes=[
                    pltpu.VMEM((targets, panel_count, per_dev * rank, width), bf16),
                    pltpu.VMEM((EXTRA, width), f32),
                ],
            ),
            compiler_params=pltpu.CompilerParams(vmem_limit_bytes=40 * MIB),
            cost_estimate=pl.CostEstimate(
                flops=4 * targets * panel_count * per_dev * rank * size * width,
                bytes_accessed=24 * MIB,
                transcendentals=0,
            ),
        )(place, ranks, far_w, far_u, *gathered)

    def scatter_panel(parts):
        return lax.all_to_all(parts, "near", 0, 0, tiled=True)

    smem = pl.BlockSpec(memory_space=pltpu.SMEM)
    vmem = pl.BlockSpec(memory_space=pltpu.VMEM)
    params = pltpu.CompilerParams(vmem_limit_bytes=40 * MIB)
    work = [pltpu.VMEM((size, width), f32)]

    payload = pl.pallas_call(
        start_kernel,
        grid=(1,),
        out_shape=jax.ShapeDtypeStruct((zs, rows, width), bf16),
        in_specs=[whole(x.shape), whole((per_dev, 1, size, size))],
        out_specs=whole((zs, rows, width)),
        compiler_params=params,
    )(x, tiles)
    panel_x = lax.all_gather(x, "near", axis=0, tiled=True)
    far_x = scatter_panel(far_products(gather_panels(payload)))
    image, z, payload, sums = pl.pallas_call(
        functools.partial(middle_kernel, total_rows=total_rows),
        out_shape=(
            jax.ShapeDtypeStruct((per_dev, size, width), f32),
            jax.ShapeDtypeStruct((per_dev, size, width), bf16),
            jax.ShapeDtypeStruct((zs, rows, width), bf16),
            jax.ShapeDtypeStruct((2, width), f32),
        ),
        in_specs=[smem, smem, vmem, vmem, vmem, vmem],
        out_specs=(vmem, vmem, vmem, vmem),
        scratch_shapes=work,
        compiler_params=params,
    )(my_cols, my_count, far_x, tiles, panel_x, x)
    panel_z = lax.all_gather(z, "near", axis=0, tiled=True)
    far_z = scatter_panel(far_products(gather_panels(payload)))
    second_basis, second_image, coefficients = pl.pallas_call(
        functools.partial(last_kernel, total_rows=total_rows),
        out_shape=(
            jax.ShapeDtypeStruct((per_dev, size, width), bf16),
            jax.ShapeDtypeStruct((per_dev, size, width), f32),
            jax.ShapeDtypeStruct((2, width), f32),
        ),
        in_specs=[smem, smem, vmem, vmem, vmem, vmem, vmem, vmem],
        out_specs=(vmem, vmem, vmem),
        scratch_shapes=work,
        compiler_params=params,
    )(my_cols, my_count, far_z, tiles, panel_z, x, image, sums)
    return second_basis[None], second_image[None], coefficients


def solution(mesh):
    placed = (
        P("blk", "near", None, None),
        P("blk", None, "near", None, None),
        P("blk", None, "near", None, None),
        P("blk", None, "near"),
        P("blk", "near", None, None, None),
        P("blk", None, None),
        P("blk", None),
    )
    return jax.shard_map(
        body,
        mesh=mesh,
        in_specs=placed,
        out_specs=(P("blk", "near", None, None), P("blk", "near", None, None), P()),
        check_vma=False,
    )
```

time: 495 us -> 222 us (0.45)
  blocking collectives: 195 us -> 0 us
  waiting for transfers between devices: 219 us -> 110 us
  Pallas kernels: 0 us -> 43.5 us
  matrix products: 40.4 us -> 0 us
  starting transfers between devices: 0.43 us -> 34.6 us
  local copies, waits for them, and re-layouts: 21.9 us -> 16.3 us
    psum x3 -> x0, blocking collectives: 195 us -> none  [the longest x1 68.2 us: body(): lax.psum(jnp.sum(start * start, axis=(0, 1, 2)), ('blk', 'near'))]
    all_gather x4 -> x2, waiting for transfers between devices: 145 us -> 19.2 us  [the longest x1 15.3 us: body(): panel_x = lax.all_gather(x, 'near', axis=0, tiled=True)]
    reduce_scatter x2 -> x0, waiting for transfers between devices: 73.9 us -> none  [apply_matrix(): lax.psum_scatter(far_total.astype(jnp.bfloat16), 'near', scatter_dimensio...]
    all_to_all x0 -> x6, waiting for transfers between devices: none -> 71.4 us  [the longest x2 35.2 us: scatter_panel(): return lax.all_to_all(parts, 'near', 0, 0, tiled=True)]
    pallas_call x0 -> x5, Pallas kernels: none -> 43.5 us  [the longest x2 32.6 us: far_products(): pl.pallas_call(functools.partial(far_kernel, zs=zs, per_dev=per_dev, targ...]
    dot_general x6 -> x0, matrix products: 40.4 us -> none  [the longest x2 19.3 us: apply_matrix(): jnp.einsum('imprs,imprc->isc', far_u, coded, preferred_element_type=jnp.f...]
    all_to_all x0 -> x6, starting transfers between devices: none -> 29.2 us  [the longest x2 12.4 us: scatter_panel(): return lax.all_to_all(parts, 'near', 0, 0, tiled=True)]
    ppermute x0 -> x6, waiting for transfers between devices: none -> 18.3 us  [the longest x2 13 us: gather_panels(): crossed = lax.ppermute(payload[0], 'blk', flip_x)]
  transfers between devices with their start and end apart: 6 -> 14, of which waited for: 6 -> 12; matrix products, arithmetic and copies ran while one was open for 11% -> 1% of each run, Pallas kernels for 0% -> 15%
where the time goes in v1:
time: 222 us; the launch traced here: 219 us
  waiting for transfers between devices  110 us (50%)
  Pallas kernels  43.5 us (20%)
  starting transfers between devices  34.6 us (16%)
  local copies, waits for them, and re-layouts  16.3 us (7%)
  between operations  14.2 us (6%)
    all_to_all x2, waiting for transfers between devices, scatter_panel(): return lax.all_to_all(parts, 'near', 0, 0, tiled=True)  35.2 us
    pallas_call x2, Pallas kernels, far_products(): pl.pallas_call(functools.partial(far_kernel, zs=zs, per_dev=per_dev, targ...  32.6 us
    all_to_all x2, waiting for transfers between devices, gather_panels(): lax.all_to_all(crossed, 'blk', 0, 0, tiled=True, axis_index_groups=z_groups)  26.4 us
    all_gather x1, waiting for transfers between devices, body(): panel_x = lax.all_gather(x, 'near', axis=0, tiled=True)  15.3 us
    ppermute x2, waiting for transfers between devices, gather_panels(): crossed = lax.ppermute(payload[0], 'blk', flip_x)  13 us
    all_to_all x2, starting transfers between devices, scatter_panel(): return lax.all_to_all(parts, 'near', 0, 0, tiled=True)  12.4 us
    unnamed x30, local copies, waits for them, and re-layouts  10.9 us
    all_to_all x2, waiting for transfers between devices, gather_panels(): lax.all_to_all(payload, 'blk', 0, 0, tiled=True, axis_index_groups=z_groups)  9.75 us
  transfers between devices with their start and end apart: 14, of which 12 were waited for; matrix products, arithmetic and copies ran while one was open for 1% of the time, Pallas kernels for 15%

profile of v1, /device:TPU:0, one launch (start us, length us, event | category | flops | bytes accessed | tf_op | source)
XLA Modules:
  0.0 219.2 jit_solution(12898930876330419548)
XLA Ops:
  7.2 0.0 copy-start
  7.2 1.6 copy-done
  8.8 0.9 copy-done.4
  9.7 1.3 shard_map.94
  11.0 5.4 %all-to-all-start = ((bf16[4,528,256]{2,1,0:T(8,128)(2,1)}), bf16[4,528,256]{2,1,0:T(8,128)(2,1)S(1)}, u32[]{:S(2)}, u32[]{:S(2)}) async-start(bf16[4,528,256]{2,1,0:T(8,128)(2,1)} %shard_map.94), calls=%async_computation | async-start | bytes 2162688 | tf_op jit(solution)/shard_map/all_to_all | solution.py:220
  16.4 1.0 slice_bitcast_fusion
  17.3 3.1 %collective-permute-start = (bf16[528,256]{1,0:T(8,128)(2,1)S(1)}, bf16[528,256]{1,0:T(8,128)(2,1)S(1)}, u32[]{:S(2)}, u32[]{:S(2)}) collective-permute-start(bf16[528,256]{1,0:T(8,128)(2,1)S(1)} %slice_bitcast_fusion), channel_id=1, source_target_pairs={{0,64},{8,72},{16,80},{24,88},{32,96},{40,104},{48,112},{56,120},{... | collective-permute-start | bytes 811016 | tf_op jit(solution)/shard_map/ppermute | solution.py:219
  20.4 6.4 %collective-permute-done = bf16[528,256]{1,0:T(8,128)(2,1)S(1)} collective-permute-done((bf16[528,256]{1,0:T(8,128)(2,1)S(1)}, bf16[528,256]{1,0:T(8,128)(2,1)S(1)}, u32[]{:S(2)}, u32[]{:S(2)}) %collective-permute-start) | collective-permute-done | bytes 270368 | tf_op jit(solution)/shard_map/ppermute | solution.py:219
  26.9 4.9 %all-to-all-done.p00 = bf16[4,528,256]{2,1,0:T(8,128)(2,1)S(1)} async-done(((bf16[4,528,256]{2,1,0:T(8,128)(2,1)}), bf16[4,528,256]{2,1,0:T(8,128)(2,1)S(1)}, u32[]{:S(2)}, u32[]{:S(2)}) %all-to-all-start) | async-done | bytes 1081376 | tf_op jit(solution)/shard_map/all_to_all | solution.py:220
  31.8 1.1 broadcast_in_dim.13
  32.9 3.6 %all-to-all-start.1 = ((bf16[4,528,256]{2,1,0:T(8,128)(2,1)}), bf16[4,528,256]{2,1,0:T(8,128)(2,1)S(1)}, u32[]{:S(2)}, u32[]{:S(2)}) async-start(bf16[4,528,256]{2,1,0:T(8,128)(2,1)} %broadcast_in_dim.13), calls=%async_computation.1 | async-start | bytes 2162688 | tf_op jit(solution)/shard_map/all_to_all | solution.py:223
  36.5 0.0 all-gather.6.cloned.1.call-start
  36.6 0.7 all-gather.6.cloned.1.call-update
  37.3 0.1 collective-permute-start.1
  37.4 13.7 %all-to-all-done.1.p10 = bf16[4,528,256]{2,1,0:T(8,128)(2,1)S(1)} async-done(((bf16[4,528,256]{2,1,0:T(8,128)(2,1)}), bf16[4,528,256]{2,1,0:T(8,128)(2,1)S(1)}, u32[]{:S(2)}, u32[]{:S(2)}) %all-to-all-start.1) | async-done | bytes 1081376 | tf_op jit(solution)/shard_map/all_to_all | solution.py:223
  51.0 0.0 collective-permute-start.2
  51.0 0.0 copy-done.14
  51.1 0.0 copy-done.13
  51.1 0.1 and_reduce_fusion
  51.2 0.1 copy.18
  51.3 0.0 copy-done.12
  51.3 0.1 and_select_fusion
  51.4 0.1 copy.19
  51.4 0.1 pad_add_fusion.place_ref
  51.5 0.0 collective-permute-done.1.p01
  51.5 2.3 %collective-permute-done.2.p11 = bf16[4,528,256]{2,1,0:T(8,128)(2,1)} collective-permute-done((bf16[4,528,256]{2,1,0:T(8,128)(2,1)S(1)}, bf16[4,528,256]{2,1,0:T(8,128)(2,1)}, u32[]{:S(2)}, u32[]{:S(2)}) %collective-permute-start.2) | collective-permute-done | bytes 1081376 | tf_op jit(solution)/shard_map/ppermute | solution.py:224
  53.9 16.2 %shard_map.95 = bf16[8,528,256]{2,1,0:T(8,128)(2,1)S(1)} custom-call(s32[2]{0:T(128)S(1)} %pad_add_fusion.place_ref, s32[32,16]{1,0:T(8,128)S(1)} %bitcast.29, bf16[16,16,2,32,256]{4,3,2,1,0:T(8,128)(2,1)} %w_ref.3, bf16[16,16,2,32,256]{4,3,2,1,0:T(8,128)(2,1)} %u_ref.3, bf16[4,528,256]{2,1,0:T(8,128)(2,1)S(1)} %all-to-all-done.p00, ...), custom_call_target="tpu_custom_call" | custom-call | flops 4294967296 | bytes 25165824 | tf_op jit(solution)/shard_map/pallas_call | solution.py:240
  70.1 0.0 copy-start.2
  70.1 1.3 copy-done.2
  71.4 5.5 %all-to-all-start.2 = ((bf16[8,528,256]{2,1,0:T(8,128)(2,1)}), bf16[8,528,256]{2,1,0:T(8,128)(2,1)}, u32[]{:S(2)}, u32[]{:S(2)}) async-start(bf16[8,528,256]{2,1,0:T(8,128)(2,1)} %copy-done.2), calls=%async_computation.2 | async-start | bytes 4325376 | tf_op jit(solution)/shard_map/all_to_all | solution.py:271
  77.0 0.1 constant_dynamic-slice_fusion
  77.0 0.1 copy.17
  77.1 0.1 dynamic-slice_bitcast_fusion.count_ref
  77.2 15.3 %all-gather.6.cloned.1.call-done = bf16[1,16,256,256]{3,2,0,1:T(8,128)(2,1)} async-done(((bf16[1,2,256,256]{3,2,0,1:T(8,128)(2,1)}), bf16[1,16,256,256]{3,2,0,1:T(8,128)(2,1)}) %all-gather.6.cloned.1.call-update) | async-done | bytes 2097168 | tf_op jit(solution)/shard_map/all_gather | solution.py:286
  92.5 11.9 %all-to-all-done.2.far_ref = bf16[8,528,256]{2,1,0:T(8,128)(2,1)} async-done(((bf16[8,528,256]{2,1,0:T(8,128)(2,1)}), bf16[8,528,256]{2,1,0:T(8,128)(2,1)}, u32[]{:S(2)}, u32[]{:S(2)}) %all-to-all-start.2) | async-done | bytes 2162720 | tf_op jit(solution)/shard_map/all_to_all | solution.py:271
  104.5 0.0 copy-done.1
  104.5 0.0 copy-done.5
  104.5 1.6 copy-done.7
  106.1 4.4 %shard_map.96 = (f32[2,256,256]{2,1,0:T(8,128)S(1)}, bf16[2,256,256]{2,1,0:T(8,128)(2,1)S(1)}, bf16[4,528,256]{2,1,0:T(8,128)(2,1)S(1)}, f32[2,256]{1,0:T(2,128)S(1)}) custom-call(s32[2,8]{1,0:T(2,128)S(1)} %bitcast.31, s32[2]{0:T(128)S(1)} %dynamic-slice_bitcast_fusion.count_ref, bf16[8,528,256]{2,1,0:T(8,128)(2,1)} %all-to-all-done.2.far_ref, ...), custom_call_target="tpu_custom_call" | custom-call | tf_op jit(solution)/shard_map/pallas_call | solution.py:288
  110.5 0.0 copy-start.8
  110.5 1.0 copy-done.8
  111.4 0.8 copy-done.9
  112.2 0.7 copy-done.11
  112.9 3.5 %all-to-all-start.3 = ((bf16[4,528,256]{2,1,0:T(8,128)(2,1)}), bf16[4,528,256]{2,1,0:T(8,128)(2,1)S(1)}, u32[]{:S(2)}, u32[]{:S(2)}) async-start(bf16[4,528,256]{2,1,0:T(8,128)(2,1)} %copy-done.8), calls=%async_computation.3 | async-start | bytes 2162688 | tf_op jit(solution)/shard_map/all_to_all | solution.py:220
  116.5 1.0 slice_bitcast_fusion.1
  117.4 2.1 collective-permute-start.3
  119.5 6.6 %collective-permute-done.3 = bf16[528,256]{1,0:T(8,128)(2,1)} collective-permute-done((bf16[528,256]{1,0:T(8,128)(2,1)S(1)}, bf16[528,256]{1,0:T(8,128)(2,1)}, u32[]{:S(2)}, u32[]{:S(2)}) %collective-permute-start.3) | collective-permute-done | bytes 270368 | tf_op jit(solution)/shard_map/ppermute | solution.py:219
  126.1 4.8 %all-to-all-done.3.p00 = bf16[4,528,256]{2,1,0:T(8,128)(2,1)S(1)} async-done(((bf16[4,528,256]{2,1,0:T(8,128)(2,1)}), bf16[4,528,256]{2,1,0:T(8,128)(2,1)S(1)}, u32[]{:S(2)}, u32[]{:S(2)}) %all-to-all-start.3) | async-done | bytes 1081376 | tf_op jit(solution)/shard_map/all_to_all | solution.py:220
  130.9 2.0 broadcast_in_dim.14
  132.9 4.2 %all-to-all-start.4 = ((bf16[4,528,256]{2,1,0:T(8,128)(2,1)}), bf16[4,528,256]{2,1,0:T(8,128)(2,1)}, u32[]{:S(2)}, u32[]{:S(2)}) async-start(bf16[4,528,256]{2,1,0:T(8,128)(2,1)} %broadcast_in_dim.14), calls=%async_computation.4 | async-start | bytes 2162688 | tf_op jit(solution)/shard_map/all_to_all | solution.py:223
  137.2 0.0 all-gather.4.cloned.1.call-start
  137.2 0.7 all-gather.4.cloned.1.call-update
  137.9 0.1 collective-permute-start.4
  138.0 12.8 %all-to-all-done.4.p10 = bf16[4,528,256]{2,1,0:T(8,128)(2,1)} async-done(((bf16[4,528,256]{2,1,0:T(8,128)(2,1)}), bf16[4,528,256]{2,1,0:T(8,128)(2,1)}, u32[]{:S(2)}, u32[]{:S(2)}) %all-to-all-start.4) | async-done | bytes 1081376 | tf_op jit(solution)/shard_map/all_to_all | solution.py:223
  150.8 0.0 collective-permute-start.5
  150.8 0.0 collective-permute-done.4.p01
  150.8 2.9 %collective-permute-done.5.p11 = bf16[4,528,256]{2,1,0:T(8,128)(2,1)S(1)} collective-permute-done((bf16[4,528,256]{2,1,0:T(8,128)(2,1)}, bf16[4,528,256]{2,1,0:T(8,128)(2,1)S(1)}, u32[]{:S(2)}, u32[]{:S(2)}) %collective-permute-start.5) | collective-permute-done | bytes 1081376 | tf_op jit(solution)/shard_map/ppermute | solution.py:224
  153.7 16.4 %shard_map.97 = bf16[8,528,256]{2,1,0:T(8,128)(2,1)S(1)} custom-call(s32[2]{0:T(128)S(1)} %pad_add_fusion.place_ref, s32[32,16]{1,0:T(8,128)S(1)} %bitcast.30, bf16[16,16,2,32,256]{4,3,2,1,0:T(8,128)(2,1)} %w_ref.3, bf16[16,16,2,32,256]{4,3,2,1,0:T(8,128)(2,1)} %u_ref.3, bf16[4,528,256]{2,1,0:T(8,128)(2,1)S(1)} %all-to-all-done.3.p00, ...), custom_call_target="tpu_custom_call" | custom-call | flops 4294967296 | bytes 25165824 | tf_op jit(solution)/shard_map/pallas_call | solution.py:240
  170.1 1.3 copy-done.3
  171.5 6.9 %all-to-all-start.5 = ((bf16[8,528,256]{2,1,0:T(8,128)(2,1)}), bf16[8,528,256]{2,1,0:T(8,128)(2,1)}, u32[]{:S(2)}, u32[]{:S(2)}) async-start(bf16[8,528,256]{2,1,0:T(8,128)(2,1)} %copy-done.3), calls=%async_computation.5 | async-start | bytes 4325376 | tf_op jit(solution)/shard_map/all_to_all | solution.py:271
  178.4 3.9 %all-gather.4.cloned.1.call-done.panel_ref = bf16[16,256,256]{2,1,0:T(8,128)(2,1)} async-done(((bf16[2,256,256]{2,1,0:T(8,128)(2,1)}), bf16[16,256,256]{2,1,0:T(8,128)(2,1)}) %all-gather.4.cloned.1.call-update) | async-done | bytes 2097168 | tf_op jit(solution)/shard_map/all_gather | solution.py:301
  182.2 23.3 %all-to-all-done.5.far_ref = bf16[8,528,256]{2,1,0:T(8,128)(2,1)} async-done(((bf16[8,528,256]{2,1,0:T(8,128)(2,1)}), bf16[8,528,256]{2,1,0:T(8,128)(2,1)}, u32[]{:S(2)}, u32[]{:S(2)}) %all-to-all-start.5) | async-done | bytes 2162720 | tf_op jit(solution)/shard_map/all_to_all | solution.py:271
  205.5 1.6 copy-done.6
  207.1 5.2 %shard_map.98 = (bf16[2,256,256]{2,1,0:T(8,128)(2,1)}, f32[2,256,256]{2,1,0:T(8,128)}, f32[2,256]{1,0:T(2,128)}) custom-call(s32[2,8]{1,0:T(2,128)S(1)} %bitcast.32, s32[2]{0:T(128)S(1)} %dynamic-slice_bitcast_fusion.count_ref, bf16[8,528,256]{2,1,0:T(8,128)(2,1)} %all-to-all-done.5.far_ref, bf16[2,8,256,256]{3,2,1,0:T(8,128)(2,1)S(1)} %bitcast.23, ...), custom_call_target="tpu_custom_call" | custom-call | tf_op jit(solution)/shard_map/pallas_call | solution.py:303
  (16 shorter events, 0.0 us)
Async XLA Ops:
  7.2 1.6 copy-start
  8.8 0.9 copy-start.4
  11.0 20.8 %all-to-all-start = ((bf16[4,528,256]{2,1,0:T(8,128)(2,1)}), bf16[4,528,256]{2,1,0:T(8,128)(2,1)S(1)}, u32[]{:S(2)}, u32[]{:S(2)}) async-start(bf16[4,528,256]{2,1,0:T(8,128)(2,1)} %shard_map.94), calls=%async_computation | async-start | bytes 2162688 | tf_op jit(solution)/shard_map/all_to_all | solution.py:220
  17.3 9.5 %collective-permute-start = (bf16[528,256]{1,0:T(8,128)(2,1)S(1)}, bf16[528,256]{1,0:T(8,128)(2,1)S(1)}, u32[]{:S(2)}, u32[]{:S(2)}) collective-permute-start(bf16[528,256]{1,0:T(8,128)(2,1)S(1)} %slice_bitcast_fusion), channel_id=1, source_target_pairs={{0,64},{8,72},{16,80},{24,88},{32,96},{40,104},{48,112},{56,120},{... | collective-permute-start | bytes 811016 | tf_op jit(solution)/shard_map/ppermute | solution.py:219
  32.9 18.2 %copy-start.14 = (s32[1,16]{1,0:T(1,128)S(1)}, s32[1,16]{1,0:T(1,128)}, u32[]{:S(2)}) copy-start(s32[1,16]{1,0:T(1,128)} %param.13) | copy-start | bytes 196
  32.9 18.2 %copy-start.13 = (s32[1,16,8]{1,2,0:T(8,128)S(1)}, s32[1,16,8]{1,2,0:T(8,128)}, u32[]{:S(2)}) copy-start(s32[1,16,8]{1,2,0:T(8,128)} %param.12) | copy-start | bytes 1540
  32.9 18.4 %copy-start.12 = (s32[16,16,2]{1,2,0:T(2,128)S(1)}, s32[16,16,2]{1,2,0:T(2,128)}, u32[]{:S(2)}) copy-start(s32[16,16,2]{1,2,0:T(2,128)} %param.10) | copy-start | bytes 6148
  32.9 18.2 %all-to-all-start.1 = ((bf16[4,528,256]{2,1,0:T(8,128)(2,1)}), bf16[4,528,256]{2,1,0:T(8,128)(2,1)S(1)}, u32[]{:S(2)}, u32[]{:S(2)}) async-start(bf16[4,528,256]{2,1,0:T(8,128)(2,1)} %broadcast_in_dim.13), calls=%async_computation.1 | async-start | bytes 2162688 | tf_op jit(solution)/shard_map/all_to_all | solution.py:223
  36.5 56.0 %all-gather.6.cloned.1.call-start = ((), (), s32[]{:S(2)}) async-start(), calls=%async_computation.7 | async-start | bytes 2359296 | tf_op jit(solution)/shard_map/all_gather | solution.py:286
  37.3 14.2 %collective-permute-start.1 = (bf16[4,528,256]{2,1,0:T(8,128)(2,1)S(1)}, bf16[4,528,256]{2,1,0:T(8,128)(2,1)S(1)}, u32[]{:S(2)}, u32[]{:S(2)}) collective-permute-start(bf16[4,528,256]{2,1,0:T(8,128)(2,1)S(1)} %all-to-all-done.p00), channel_id=1, source_target_pairs={{0,8},{8,0},{16,24},{24,16},{32,40},{40,32},{48,56},{56,48},{64,72... | collective-permute-start | bytes 3244040 | tf_op jit(solution)/shard_map/ppermute | solution.py:221
  51.0 2.8 %collective-permute-start.2 = (bf16[4,528,256]{2,1,0:T(8,128)(2,1)S(1)}, bf16[4,528,256]{2,1,0:T(8,128)(2,1)}, u32[]{:S(2)}, u32[]{:S(2)}) collective-permute-start(bf16[4,528,256]{2,1,0:T(8,128)(2,1)S(1)} %all-to-all-done.1.p10), channel_id=1, source_target_pairs={{0,8},{8,0},{16,24},{24,16},{32,40},{40,32},{48,56},{56,48},{64,72... | collective-permute-start | bytes 3244040 | tf_op jit(solution)/shard_map/ppermute | solution.py:224
  70.1 1.3 copy-start.2
  71.4 33.0 %copy-start.1 = (bf16[1,2,8,256,256]{4,3,2,1,0:T(8,128)(2,1)S(1)}, bf16[1,2,8,256,256]{4,3,2,1,0:T(8,128)(2,1)}, u32[]{:S(2)}) copy-start(bf16[1,2,8,256,256]{4,3,2,1,0:T(8,128)(2,1)} %param.11) | copy-start | bytes 6291460
  71.4 33.0 %copy-start.5 = (bf16[1,2,256,256]{3,2,1,0:T(8,128)(2,1)S(1)}, bf16[1,2,256,256]{3,2,1,0:T(8,128)(2,1)}, u32[]{:S(2)}) copy-start(bf16[1,2,256,256]{3,2,1,0:T(8,128)(2,1)} %param.7) | copy-start | bytes 786436
  71.4 33.0 %all-to-all-start.2 = ((bf16[8,528,256]{2,1,0:T(8,128)(2,1)}), bf16[8,528,256]{2,1,0:T(8,128)(2,1)}, u32[]{:S(2)}, u32[]{:S(2)}) async-start(bf16[8,528,256]{2,1,0:T(8,128)(2,1)} %copy-done.2), calls=%async_computation.2 | async-start | bytes 4325376 | tf_op jit(solution)/shard_map/all_to_all | solution.py:271
  104.5 1.6 copy-start.7
  110.5 1.0 copy-start.8
  111.4 0.8 copy-start.9
  112.2 0.7 copy-start.11
  112.9 18.0 %all-to-all-start.3 = ((bf16[4,528,256]{2,1,0:T(8,128)(2,1)}), bf16[4,528,256]{2,1,0:T(8,128)(2,1)S(1)}, u32[]{:S(2)}, u32[]{:S(2)}) async-start(bf16[4,528,256]{2,1,0:T(8,128)(2,1)} %copy-done.8), calls=%async_computation.3 | async-start | bytes 2162688 | tf_op jit(solution)/shard_map/all_to_all | solution.py:220
  117.4 8.7 %collective-permute-start.3 = (bf16[528,256]{1,0:T(8,128)(2,1)S(1)}, bf16[528,256]{1,0:T(8,128)(2,1)}, u32[]{:S(2)}, u32[]{:S(2)}) collective-permute-start(bf16[528,256]{1,0:T(8,128)(2,1)S(1)} %slice_bitcast_fusion.1), channel_id=1, source_target_pairs={{0,64},{8,72},{16,80},{24,88},{32,96},{40,104},{48,112},{56,120},{... | collective-permute-start | bytes 811016 | tf_op jit(solution)/shard_map/ppermute | solution.py:219
  132.9 17.9 %all-to-all-start.4 = ((bf16[4,528,256]{2,1,0:T(8,128)(2,1)}), bf16[4,528,256]{2,1,0:T(8,128)(2,1)}, u32[]{:S(2)}, u32[]{:S(2)}) async-start(bf16[4,528,256]{2,1,0:T(8,128)(2,1)} %broadcast_in_dim.14), calls=%async_computation.4 | async-start | bytes 2162688 | tf_op jit(solution)/shard_map/all_to_all | solution.py:223
  137.2 45.0 %all-gather.4.cloned.1.call-start = ((), (), s32[]{:S(2)}) async-start(), calls=%async_computation.6 | async-start | bytes 2359296 | tf_op jit(solution)/shard_map/all_gather | solution.py:301
  137.9 12.9 %collective-permute-start.4 = (bf16[4,528,256]{2,1,0:T(8,128)(2,1)S(1)}, bf16[4,528,256]{2,1,0:T(8,128)(2,1)}, u32[]{:S(2)}, u32[]{:S(2)}) collective-permute-start(bf16[4,528,256]{2,1,0:T(8,128)(2,1)S(1)} %all-to-all-done.3.p00), channel_id=1, source_target_pairs={{0,8},{8,0},{16,24},{24,16},{32,40},{40,32},{48,56},{56,48},{64,72... | collective-permute-start | bytes 3244040 | tf_op jit(solution)/shard_map/ppermute | solution.py:221
  150.8 2.9 %collective-permute-start.5 = (bf16[4,528,256]{2,1,0:T(8,128)(2,1)}, bf16[4,528,256]{2,1,0:T(8,128)(2,1)S(1)}, u32[]{:S(2)}, u32[]{:S(2)}) collective-permute-start(bf16[4,528,256]{2,1,0:T(8,128)(2,1)} %all-to-all-done.4.p10), channel_id=1, source_target_pairs={{0,8},{8,0},{16,24},{24,16},{32,40},{40,32},{48,56},{56,48},{64,72... | collective-permute-start | bytes 3244040 | tf_op jit(solution)/shard_map/ppermute | solution.py:224
  170.1 1.3 copy-start.3
  171.5 34.0 %copy-start.10 = (f32[2,256,256]{2,1,0:T(8,128)S(1)}, f32[2,256,256]{2,1,0:T(8,128)}, u32[]{:S(2)}) copy-start(f32[2,256,256]{2,1,0:T(8,128)} %copy-done.9) | copy-start | bytes 1572868
  171.5 34.0 %all-to-all-start.5 = ((bf16[8,528,256]{2,1,0:T(8,128)(2,1)}), bf16[8,528,256]{2,1,0:T(8,128)(2,1)}, u32[]{:S(2)}, u32[]{:S(2)}) async-start(bf16[8,528,256]{2,1,0:T(8,128)(2,1)} %copy-done.3), calls=%async_computation.5 | async-start | bytes 4325376 | tf_op jit(solution)/shard_map/all_to_all | solution.py:271
  205.5 1.6 copy-start.6
Sparse Core Ops, SparseCore 0:
  39.0 53.4 all-gather.5
  140.2 41.9 all-gather.3

commit v2 on v0

v2 whole, which is shorter than its diff:
```python
import functools

import jax
import jax.numpy as jnp
from jax import lax
from jax.experimental import pallas as pl
from jax.experimental.pallas import tpu as pltpu
from jax.sharding import PartitionSpec as P

EPS = 1e-06
EXTRA = 16
MIB = 1 << 20


def put_sums(sums, width):
    rows = []
    for value in sums:
        high = value.astype(jnp.bfloat16)
        left = value - high.astype(jnp.float32)
        middle = left.astype(jnp.bfloat16)
        low = (left - middle.astype(jnp.float32)).astype(jnp.bfloat16)
        rows += [high, middle, low]
    rows.append(jnp.zeros((EXTRA - len(rows), width), jnp.bfloat16))
    return jnp.concatenate(rows, axis=0)


def get_sums(rows):
    return (
        rows[0:1] + rows[1:2] + rows[2:3],
        rows[3:4] + rows[4:5] + rows[5:6],
    )


def whole(shape):
    return pl.BlockSpec(shape, lambda *_: (0,) * len(shape))


def start_kernel(x_ref, own_ref, out_ref):
    per_dev, size, width = x_ref.shape
    square = jnp.zeros((1, width), jnp.float32)
    cross = jnp.zeros((1, width), jnp.float32)
    for p in range(per_dev):
        x = x_ref[p]
        x_f = x.astype(jnp.float32)
        image = jnp.dot(own_ref[p, 0], x, preferred_element_type=jnp.float32)
        square += jnp.sum(x_f * x_f, axis=0, keepdims=True)
        cross += jnp.sum(x_f * image, axis=0, keepdims=True)
        out_ref[p * size : (p + 1) * size, :] = x
    out_ref[per_dev * size :, :] = put_sums((square, cross), width)


def load_kernel(w_ref, u_ref, held_w, held_u, done_ref, w_sem, u_sem):
    copies = []
    for source, target, sems in ((w_ref, held_w, w_sem), (u_ref, held_u, u_sem)):
        copies += [
            pltpu.make_async_copy(source.at[k], target.at[k], sems.at[k])
            for k in range(source.shape[0])
        ]
    for copy in copies:
        copy.start()
    for copy in copies:
        copy.wait()
    done_ref[...] = jnp.zeros_like(done_ref)


def pack_kernel(*refs):
    count = len(refs) - 3
    _, out_ref, sems = refs[count:]
    copies = [
        pltpu.make_async_copy(refs[n], out_ref.at[n], sems.at[n]) for n in range(count)
    ]
    for copy in copies:
        copy.start()
    for copy in copies:
        copy.wait()


class Coder:
    def __init__(self, first, order_ref, rank_ref, w_ref, fields, field_buf, field_sem):
        self.first, self.order_ref, self.rank_ref = first, order_ref, rank_ref
        self.w_ref, self.field_buf = w_ref, field_buf
        parts = [field.at[n] for field in fields for n in range(field.shape[0])]
        self.copies = [
            pltpu.make_async_copy(part, field_buf.at[slot], field_sem.at[slot])
            for slot, part in enumerate(parts)
        ]

    def load(self):
        for copy in self.copies:
            copy.start()

    def run(self, coded_ref, sums_ref, by_panel):
        targets, _, per_dev, rank, size = self.w_ref.shape
        width = coded_ref.shape[3]
        row = lax.broadcasted_iota(jnp.int32, (rank, width), 0)
        for slot, copy in enumerate(self.copies):
            panel = self.order_ref[self.first + slot]
            place = panel if by_panel else slot
            copy.wait()
            sums_ref[...] += self.field_buf[slot, per_dev * size :, :].astype(jnp.float32)
            for p in range(per_dev):
                w = self.w_ref[:, panel, p].reshape(targets * rank, size)
                field = self.field_buf[slot, p * size : (p + 1) * size, :]
                value = jnp.dot(w, field, preferred_element_type=jnp.float32)
                for i in range(targets):
                    live = self.rank_ref[panel * per_dev + p, i]
                    part = value[i * rank : (i + 1) * rank]
                    part = jnp.where(row < live, part, 0.0).astype(jnp.bfloat16)
                    coded_ref[i, place, p * rank : (p + 1) * rank, :] = part


def code_kernel(order_ref, rank_ref, w_ref, *refs):
    fields, (coded_ref, sums_ref, field_buf, field_sem) = refs[:-4], refs[-4:]
    coder = Coder(0, order_ref, rank_ref, w_ref, fields, field_buf, field_sem)
    coder.load()
    sums_ref[...] = jnp.zeros_like(sums_ref)
    coder.run(coded_ref, sums_ref, False)


def far_kernel(order_ref, rank_ref, w_ref, u_ref, early_ref, early_sums_ref, *refs):
    fields, refs = refs[:-8], refs[-8:]
    out_ref, field_buf, coded_ref, out_buf, sums_ref, field_sem, early_sem, out_sem = refs
    receivers, rows, width = out_ref.shape
    _, _, per_dev, _, size = u_ref.shape
    blocks = per_dev * size
    early = early_ref.shape[1]

    def early_copy(slot):
        return pltpu.make_async_copy(
            early_ref.at[:, slot], coded_ref.at[:, order_ref[slot]], early_sem.at[slot]
        )

    def out_copy(j):
        return pltpu.make_async_copy(out_buf.at[j], out_ref.at[j], out_sem.at[j])

    coder = Coder(early, order_ref, rank_ref, w_ref, fields, field_buf, field_sem)
    coder.load()
    for slot in range(early):
        early_copy(slot).start()
    sums_ref[...] = early_sums_ref[...]
    coder.run(coded_ref, sums_ref, True)
    extra = put_sums(get_sums(sums_ref[...]), width)
    for slot in range(early):
        early_copy(slot).wait()

    def expand(j, carry):
        for p in range(per_dev):
            u = u_ref[per_dev * j + p].reshape(-1, size)
            value = coded_ref[per_dev * j + p].reshape(-1, width)
            total = lax.dot_general(
                u, value, (((0,), (0,)), ((), ())), preferred_element_type=jnp.float32
            )
            out_buf[j, p * size : (p + 1) * size, :] = total.astype(jnp.bfloat16)
        out_buf[j, blocks:, :] = extra
        out_copy(j).start()
        return carry

    lax.fori_loop(0, receivers, expand, 0)
    for j in range(receivers):
        out_copy(j).wait()


def near_kernel(cols_ref, count_ref, tiles_ref, panel_ref, out_ref, panel_buf, tile_buf, sems):
    per_dev = out_ref.shape[0]
    copies = [pltpu.make_async_copy(panel_ref, panel_buf, sems.at[per_dev])]
    copies += [
        pltpu.make_async_copy(tiles_ref.at[p], tile_buf.at[p], sems.at[p]) for p in range(per_dev)
    ]
    for copy in copies:
        copy.start()
    for copy in copies:
        copy.wait()
    for p in range(per_dev):
        out_ref[p] = jnp.zeros(out_ref.shape[1:], jnp.float32)
        for k in range(tile_buf.shape[1]):

            @pl.when(k < count_ref[p])
            def _():
                out_ref[p] += jnp.dot(
                    tile_buf[p, k], panel_buf[cols_ref[p, k]], preferred_element_type=jnp.float32
                )


class FarTotal:
    def __init__(self, far_ref, buf, sems):
        self.buf = buf
        self.copies = [
            pltpu.make_async_copy(far_ref.at[s], buf.at[s], sems.at[s])
            for s in range(buf.shape[0])
        ]
        for copy in self.copies:
            copy.start()

    def wait(self):
        for copy in self.copies:
            copy.wait()

    def rows(self, start, stop):
        total = self.buf[0, start:stop, :].astype(jnp.float32)
        for s in range(1, self.buf.shape[0]):
            total += self.buf[s, start:stop, :].astype(jnp.float32)
        return total

    def sums(self):
        rows = self.buf.shape[1]
        return get_sums(self.rows(rows - EXTRA, rows))


def middle_kernel(
    far_ref, near_ref, x_ref, image_ref, sums_ref, z_ref, out_ref, far_buf, far_sem, *, total_rows
):
    per_dev, size, width = x_ref.shape
    far = FarTotal(far_ref, far_buf, far_sem)
    far.wait()
    square_x, cross_x = far.sums()
    guess = cross_x / (square_x + EPS * total_rows)
    sums_ref[0:1, :] = square_x
    sums_ref[1:2, :] = guess
    cross = jnp.zeros((1, width), jnp.float32)
    square = jnp.zeros((1, width), jnp.float32)
    for p in range(per_dev):
        image = far.rows(p * size, (p + 1) * size) + near_ref[p]
        image_ref[p] = image
        x = x_ref[p].astype(jnp.float32)
        moved = image - guess * x
        cross += jnp.sum(x * moved, axis=0, keepdims=True)
        square += jnp.sum(moved * moved, axis=0, keepdims=True)
        z = moved.astype(jnp.bfloat16)
        z_ref[p] = z
        out_ref[p * size : (p + 1) * size, :] = z
    out_ref[per_dev * size :, :] = put_sums((cross, square), width)


def last_kernel(
    far_ref, near_ref, x_ref, image_ref, sums_ref, basis_ref, out_ref, coef_ref, far_buf, far_sem,
    *, total_rows,
):
    per_dev, size, _ = x_ref.shape
    far = FarTotal(far_ref, far_buf, far_sem)
    far.wait()
    cross, square = far.sums()
    cross, square = cross / total_rows, square / total_rows
    mean_x = sums_ref[0:1, :] / total_rows
    guess = sums_ref[1:2, :]
    scale = lax.rsqrt(mean_x + EPS)
    proj = scale * scale * (cross + guess * mean_x)
    off = proj - guess
    mean_rest = scale * scale * (square - 2.0 * off * cross + off * off * mean_x)
    mean_rest = jnp.maximum(mean_rest, 0.0) + EPS
    factor = scale * lax.rsqrt(mean_rest)
    coef_ref[0:1, :] = proj
    coef_ref[1:2, :] = jnp.sqrt(mean_rest)
    for p in range(per_dev):
        image = image_ref[p]
        x = x_ref[p].astype(jnp.float32)
        basis_ref[p] = ((image - guess * x - off * x) * factor).astype(jnp.bfloat16)
        second = far.rows(p * size, (p + 1) * size) + near_ref[p]
        out_ref[p] = (second - off * image) * factor


def body(rhs_block, far_u, far_w, far_ranks, near_tiles, near_cols, near_count):
    panel_count = lax.axis_size("blk")
    slice_count = lax.axis_size("near")
    my_panel = lax.axis_index("blk")
    my_slice = lax.axis_index("near")
    per_dev, size, width = rhs_block.shape[1:]
    total_rows = float(per_dev * size * panel_count * slice_count)
    slots = near_cols.shape[2]
    targets = far_u.shape[0]
    rank = far_u.shape[3]
    chips = panel_count // 2
    rows = per_dev * size + EXTRA
    bf16, f32, i32 = jnp.bfloat16, jnp.float32, jnp.int32

    x = rhs_block[0]
    tiles = near_tiles[0]
    slot_live = jnp.arange(slots, dtype=i32)[None, :] < near_count[0][:, None]
    mine = my_slice * per_dev + jnp.arange(per_dev, dtype=i32)
    is_near = jnp.any((near_cols[0][:, :, None] == mine) & slot_live[:, :, None], axis=1)
    same = jnp.arange(panel_count, dtype=i32) == my_panel
    near_pair = same[:, None, None] & is_near.T[None]
    ranks = jnp.where(near_pair, 0, far_ranks.transpose(1, 2, 0)).reshape(-1, targets)
    my_cols = lax.dynamic_slice_in_dim(near_cols[0], my_slice * per_dev, per_dev, 0)
    my_count = lax.dynamic_slice_in_dim(near_count[0], my_slice * per_dev, per_dev, 0)

    hbm = pl.BlockSpec(memory_space=pltpu.HBM)
    smem = pl.BlockSpec(memory_space=pltpu.SMEM)
    vmem = pl.BlockSpec(memory_space=pltpu.VMEM)
    sems = pltpu.SemaphoreType.DMA
    in_hbm = pltpu.HBM

    def params(mib):
        return pltpu.CompilerParams(vmem_limit_bytes=mib * MIB)

    def cost(flops, mib):
        return pl.CostEstimate(flops=flops, bytes_accessed=mib * MIB, transcendentals=0)

    zs = chips // 2
    z_turns = (0, 1, 3, 2)

    def along_z(turn):
        return [
            (i, i // chips * chips + ((i // 2 - turn) % zs) * 2 + i % 2) for i in range(panel_count)
        ]

    flip_core = [(i, i ^ 1) for i in range(panel_count)]
    flip_far = [(i, (i + chips) % panel_count) for i in range(panel_count)]
    core = my_panel % 2
    near_z = [
        my_panel // chips * chips + 2 * ((my_panel // 2 + turn) % zs) for turn in z_turns
    ]
    far_z = [(at + chips) % panel_count for at in near_z]
    first = near_z[:1] + far_z[:1] + near_z[1:] + far_z[1:]
    order = jnp.stack(
        [at + core for at in first] + [at + 1 - core for at in first]
    ).astype(i32)

    def pack(blocks, loaded):
        count = len(blocks)
        return pl.pallas_call(
            pack_kernel,
            out_shape=jax.ShapeDtypeStruct((count, rows, width), bf16),
            in_specs=[hbm] * count + [vmem],
            out_specs=hbm,
            scratch_shapes=[sems((count,))],
            compiler_params=params(1),
        )(*blocks, loaded)

    def gather_panels(payload, loaded):
        far = lax.ppermute(payload, "blk", flip_far)
        own = [lax.ppermute(payload, "blk", along_z(turn)) for turn in z_turns[1:]]
        late = [lax.ppermute(far, "blk", along_z(turn)) for turn in z_turns[1:]]
        own = pack([payload, far] + own + late, loaded)
        return [own], [lax.ppermute(own, "blk", flip_core)]

    flops = 2 * targets * panel_count * per_dev * rank * size * width

    def coder_scratch(n):
        return [pltpu.VMEM((n, rows, width), bf16)]

    far_w, order, ranks, my_cols, my_count = lax.optimization_barrier(
        (far_w, order, ranks, my_cols, my_count)
    )

    def load_factors(far_w, far_u):
        return pl.pallas_call(
            load_kernel,
            out_shape=(
                pltpu.VMEM(far_w.shape, bf16),
                pltpu.VMEM(far_u.shape, bf16),
                jax.ShapeDtypeStruct((8, 128), f32),
            ),
            in_specs=[hbm, hbm],
            out_specs=(vmem, vmem, vmem),
            scratch_shapes=[sems((targets,)), sems((targets,))],
            compiler_params=params(44),
            cost_estimate=cost(0, 32),
        )(far_w, far_u)

    def far_products(payload, far_w, far_u):
        held_w, held_u, loaded = load_factors(far_w, far_u)
        early, late = gather_panels(payload, loaded)
        n = sum(field.shape[0] for field in early)
        m = panel_count - n
        coded, sums = pl.pallas_call(
            code_kernel,
            out_shape=(
                pltpu.VMEM((targets, n, per_dev * rank, width), bf16),
                jax.ShapeDtypeStruct((EXTRA, width), f32),
            ),
            in_specs=[smem, smem, vmem] + [hbm] * len(early),
            out_specs=(vmem, vmem),
            scratch_shapes=coder_scratch(n) + [sems((n,))],
            compiler_params=params(8),
            cost_estimate=cost(flops * n // panel_count, 16),
        )(order, ranks, held_w, *early)
        return pl.pallas_call(
            far_kernel,
            out_shape=in_hbm((slice_count, rows, width), bf16),
            in_specs=[smem, smem, vmem, vmem, hbm, vmem] + [hbm] * len(late),
            out_specs=hbm,
            scratch_shapes=coder_scratch(m)
            + [
                pltpu.VMEM((targets, panel_count, per_dev * rank, width), bf16),
                pltpu.VMEM((slice_count, rows, width), bf16),
                pltpu.VMEM((EXTRA, width), f32),
            ]
            + [sems((m,)), sems((n,)), sems((slice_count,))],
            compiler_params=params(18),
            cost_estimate=cost(flops + flops * m // panel_count, 20),
        )(order, ranks, held_w, held_u, coded, sums, *late)

    def near_products(panel):
        return pl.pallas_call(
            near_kernel,
            out_shape=jax.ShapeDtypeStruct((per_dev, size, width), f32),
            in_specs=[smem, smem, hbm, hbm],
            out_specs=vmem,
            scratch_shapes=[
                pltpu.VMEM((slice_count * per_dev, size, width), bf16),
                pltpu.VMEM((per_dev, slots, size, size), bf16),
                sems((per_dev + 1,)),
            ],
            compiler_params=params(10),
            cost_estimate=cost(2 * per_dev * slots * size * size * width, 5),
        )(my_cols, my_count, tiles, panel)

    def gather_near(blocks):
        return lax.all_gather(blocks, "near", axis=0, tiled=True)

    def scatter_panel(parts, panel):
        parts, panel = lax.optimization_barrier((parts, panel))
        return lax.all_to_all(parts, "near", 0, 0, tiled=True), panel

    payload = pl.pallas_call(
        start_kernel,
        grid=(1,),
        out_shape=jax.ShapeDtypeStruct((rows, width), bf16),
        in_specs=[whole(x.shape), whole((per_dev, 1, size, size))],
        out_specs=whole((rows, width)),
        compiler_params=params(60),
    )(x, tiles)
    panel = gather_near(x)
    far_x, panel = scatter_panel(far_products(payload, far_w, far_u), panel)
    far_scratch = [pltpu.VMEM((slice_count, rows, width), bf16), sems((slice_count,))]
    image, sums, z, payload = pl.pallas_call(
        functools.partial(middle_kernel, total_rows=total_rows),
        out_shape=(
            jax.ShapeDtypeStruct((per_dev, size, width), f32),
            jax.ShapeDtypeStruct((2, width), f32),
            in_hbm((per_dev, size, width), bf16),
            jax.ShapeDtypeStruct((rows, width), bf16),
        ),
        in_specs=[hbm, vmem, vmem],
        out_specs=(vmem,) * 4,
        scratch_shapes=far_scratch,
        compiler_params=params(8),
    )(far_x, near_products(panel), x)
    panel = gather_near(z)
    payload, far_w, far_u = lax.optimization_barrier((payload, far_w, far_u))
    far_z, panel = scatter_panel(far_products(payload, far_w, far_u), panel)
    second_basis, second_image, coefficients = pl.pallas_call(
        functools.partial(last_kernel, total_rows=total_rows),
        out_shape=(
            jax.ShapeDtypeStruct((per_dev, size, width), bf16),
            jax.ShapeDtypeStruct((per_dev, size, width), f32),
            jax.ShapeDtypeStruct((2, width), f32),
        ),
        in_specs=[hbm, vmem, vmem, vmem, vmem],
        out_specs=(vmem, vmem, vmem),
        scratch_shapes=far_scratch,
        compiler_params=params(8),
    )(far_z, near_products(panel), x, image, sums)
    return second_basis[None], second_image[None], coefficients


def solution(mesh):
    placed = (
        P("blk", "near", None, None),
        P("blk", None, "near", None, None),
        P("blk", None, "near", None, None),
        P("blk", None, "near"),
        P("blk", "near", None, None, None),
        P("blk", None, None),
        P("blk", None),
    )
    return jax.shard_map(
        body,
        mesh=mesh,
        in_specs=placed,
        out_specs=(P("blk", "near", None, None), P("blk", "near", None, None), P()),
        check_vma=False,
    )
```

time: 495 us -> 179 us (0.36)
  blocking collectives: 195 us -> 0 us
  waiting for transfers between devices: 219 us -> 74.6 us
  Pallas kernels: 0 us -> 53.6 us
  matrix products: 40.4 us -> 0 us
  starting transfers between devices: 0.43 us -> 29.1 us
  local copies, waits for them, and re-layouts: 21.9 us -> 5.79 us
    psum x3 -> x0, blocking collectives: 195 us -> none  [the longest x1 68.2 us: body(): lax.psum(jnp.sum(start * start, axis=(0, 1, 2)), ('blk', 'near'))]
    all_gather x4 -> x2, waiting for transfers between devices: 145 us -> 0.04 us  [gather_near(): return lax.all_gather(blocks, 'near', axis=0, tiled=True)]
    reduce_scatter x2 -> x0, waiting for transfers between devices: 73.9 us -> none  [apply_matrix(): lax.psum_scatter(far_total.astype(jnp.bfloat16), 'near', scatter_dimensio...]
    pallas_call x0 -> x13, Pallas kernels: none -> 53.6 us  [the longest x2 17.1 us: far_products(): pl.pallas_call(far_kernel, out_shape=in_hbm((slice_count, rows, width), b...]
    all_to_all x0 -> x2, waiting for transfers between devices: none -> 44.5 us  [scatter_panel(): return (lax.all_to_all(parts, 'near', 0, 0, tiled=True), panel)]
    dot_general x6 -> x0, matrix products: 40.4 us -> none  [the longest x2 19.3 us: apply_matrix(): jnp.einsum('imprs,imprc->isc', far_u, coded, preferred_element_type=jnp.f...]
    ppermute x0 -> x16, waiting for transfers between devices: none -> 29.4 us  [the longest x6 13.5 us: gather_panels(): late = [lax.ppermute(far, 'blk', along_z(turn)) for turn in z_turns[1:]]]
    ppermute x0 -> x16, starting transfers between devices: none -> 20.1 us  [the longest x6 8.53 us: gather_panels(): own = [lax.ppermute(payload, 'blk', along_z(turn)) for turn in z_turns[1:]]]
  transfers between devices with their start and end apart: 6 -> 20, of which waited for: 6 -> 11; matrix products, arithmetic and copies ran while one was open for 11% -> 0% of each run, Pallas kernels for 0% -> 27%
where the time goes in v2:
time: 179 us; the launch traced here: 178 us
  waiting for transfers between devices  74.6 us (42%)
  Pallas kernels  53.6 us (30%)
  starting transfers between devices  29.1 us (16%)
  between operations  14.5 us (8%)
  local copies, waits for them, and re-layouts  5.79 us (3%)
    all_to_all x2, waiting for transfers between devices, scatter_panel(): return (lax.all_to_all(parts, 'near', 0, 0, tiled=True), panel)  44.5 us
    pallas_call x2, Pallas kernels, far_products(): pl.pallas_call(far_kernel, out_shape=in_hbm((slice_count, rows, width), b...  17.1 us
    pallas_call x2, Pallas kernels, load_factors(): pl.pallas_call(load_kernel, out_shape=(pltpu.VMEM(far_w.shape, bf16), plt...  13.5 us
    ppermute x6, waiting for transfers between devices, gather_panels(): late = [lax.ppermute(far, 'blk', along_z(turn)) for turn in z_turns[1:]]  13.5 us
    all_to_all x2, starting transfers between devices, scatter_panel(): return (lax.all_to_all(parts, 'near', 0, 0, tiled=True), panel)  8.98 us
    ppermute x6, starting transfers between devices, gather_panels(): own = [lax.ppermute(payload, 'blk', along_z(turn)) for turn in z_turns[1:]]  8.53 us
    ppermute x2, waiting for transfers between devices, gather_panels(): far = lax.ppermute(payload, 'blk', flip_far)  8.35 us
    pallas_call x2, Pallas kernels, far_products(): pl.pallas_call(code_kernel, out_shape=(pltpu.VMEM((targets, n, per_dev *...  7.02 us
  transfers between devices with their start and end apart: 20, of which 11 were waited for; matrix products, arithmetic and copies ran while one was open for 0% of the time, Pallas kernels for 27%

profile of v2, /device:TPU:0, one launch (start us, length us, event | category | flops | bytes accessed | tf_op | source)
XLA Modules:
  0.0 177.9 jit_solution(13958706302648667466)
XLA Ops:
  7.2 0.0 all-gather.6.cloned.1.call-start
  7.2 0.7 all-gather.6.cloned.1.call-update
  7.9 2.0 %shard_map.95.refs_0_ = bf16[528,256]{1,0:T(8,128)(2,1)} custom-call(bf16[2,256,256]{2,1,0:T(8,128)(2,1)} %bitcast.35, bf16[2,8,256,256]{3,2,1,0:T(8,128)(2,1)} %bitcast.31), custom_call_target="tpu_custom_call" | custom-call | tf_op jit(solution)/shard_map/pallas_call | solution.py:415
  9.9 3.1 %collective-permute-start = (bf16[528,256]{1,0:T(8,128)(2,1)}, bf16[528,256]{1,0:T(8,128)(2,1)S(1)}, u32[]{:S(2)}, u32[]{:S(2)}) collective-permute-start(bf16[528,256]{1,0:T(8,128)(2,1)} %shard_map.95.refs_0_), channel_id=1, source_target_pairs={{0,64},{8,72},{16,80},{24,88},{32,96},{40,104},{48,112},{56,120},{... | collective-permute-start | bytes 811016 | tf_op jit(solution)/shard_map/ppermute | solution.py:330
  13.0 4.0 %collective-permute-start.1 = (bf16[528,256]{1,0:T(8,128)(2,1)}, bf16[528,256]{1,0:T(8,128)(2,1)S(1)}, u32[]{:S(2)}, u32[]{:S(2)}) collective-permute-start(bf16[528,256]{1,0:T(8,128)(2,1)} %shard_map.95.refs_0_), channel_id=1, source_target_pairs={{0,48},{8,56},{16,0},{24,8},{32,16},{40,24},{48,32},{56,40},{64,11... | collective-permute-start | bytes 811016 | tf_op jit(solution)/shard_map/ppermute | solution.py:331
  17.1 0.0 collective-permute-start.2
  17.1 1.9 %collective-permute-start.3 = (bf16[528,256]{1,0:T(8,128)(2,1)}, bf16[528,256]{1,0:T(8,128)(2,1)S(1)}, u32[]{:S(2)}, u32[]{:S(2)}) collective-permute-start(bf16[528,256]{1,0:T(8,128)(2,1)} %shard_map.95.refs_0_), channel_id=1, source_target_pairs={{0,32},{8,40},{16,48},{24,56},{32,0},{40,8},{48,16},{56,24},{64,96... | collective-permute-start | bytes 811016 | tf_op jit(solution)/shard_map/ppermute | solution.py:331
  19.0 0.1 and_reduce_fusion
  19.0 0.1 copy.17
  19.1 0.6 collective-permute-done.refs_1_
  19.7 4.3 %collective-permute-start.4 = (bf16[528,256]{1,0:T(8,128)(2,1)S(1)}, bf16[528,256]{1,0:T(8,128)(2,1)S(1)}, u32[]{:S(2)}, u32[]{:S(2)}) collective-permute-start(bf16[528,256]{1,0:T(8,128)(2,1)S(1)} %collective-permute-done.refs_1_), channel_id=1, source_target_pairs={{0,48},{8,56},{16,0},{24,8},{32,16},{40,24},{48,32},{56,40},{64,11... | collective-permute-start | bytes 811016 | tf_op jit(solution)/shard_map/ppermute | solution.py:332
  24.0 6.1 %collective-permute-done.1.refs_2_ = bf16[528,256]{1,0:T(8,128)(2,1)S(1)} collective-permute-done((bf16[528,256]{1,0:T(8,128)(2,1)}, bf16[528,256]{1,0:T(8,128)(2,1)S(1)}, u32[]{:S(2)}, u32[]{:S(2)}) %collective-permute-start.1) | collective-permute-done | bytes 270368 | tf_op jit(solution)/shard_map/ppermute | solution.py:331
  30.1 0.0 collective-permute-start.6
  30.1 0.1 and_select_fusion
  30.4 0.1 copy.18
  30.5 0.1 constant_dynamic-slice_fusion
  30.5 0.1 copy.19
  30.6 0.1 stack.67.order_ref
  30.7 0.1 dynamic-slice_bitcast_fusion.count_ref
  30.8 6.8 %shard_map.94 = (bf16[16,16,2,32,256]{4,3,2,1,0:T(8,128)(2,1)S(1)}, bf16[16,16,2,32,256]{4,3,2,1,0:T(8,128)(2,1)S(1)}, f32[8,128]{1,0:T(8,128)}) custom-call(bf16[16,16,2,32,256]{4,3,2,1,0:T(8,128)(2,1)} %w_ref.1, bf16[16,16,2,32,256]{4,3,2,1,0:T(8,128)(2,1)} %u_ref.2), custom_call_target="tpu_custom_call" | custom-call | bytes 33554432 | tf_op jit(solution)/shard_map/pallas_call | solution.py:346
  37.6 0.0 collective-permute-done.3.refs_4_
  37.6 2.5 %collective-permute-done.4.refs_5_ = bf16[528,256]{1,0:T(8,128)(2,1)S(1)} collective-permute-done((bf16[528,256]{1,0:T(8,128)(2,1)S(1)}, bf16[528,256]{1,0:T(8,128)(2,1)S(1)}, u32[]{:S(2)}, u32[]{:S(2)}) %collective-permute-start.4) | collective-permute-done | bytes 270368 | tf_op jit(solution)/shard_map/ppermute | solution.py:332
  40.1 3.4 %collective-permute-done.5.refs_6_ = bf16[528,256]{1,0:T(8,128)(2,1)S(1)} collective-permute-done((bf16[528,256]{1,0:T(8,128)(2,1)S(1)}, bf16[528,256]{1,0:T(8,128)(2,1)S(1)}, u32[]{:S(2)}, u32[]{:S(2)}) %collective-permute-start.5) | collective-permute-done | bytes 270368 | tf_op jit(solution)/shard_map/ppermute | solution.py:332
  43.5 0.0 collective-permute-done.6.refs_7_
  43.5 0.7 copy-done.7
  44.2 0.3 shard_map.96.refs_0_
  44.5 0.1 collective-permute-start.7
  44.6 3.5 %shard_map.97 = (bf16[16,8,64,256]{3,2,1,0:T(8,128)(2,1)S(1)}, f32[16,256]{1,0:T(8,128)S(1)}) custom-call(s32[16]{0:T(128)S(1)} %stack.67.order_ref, s32[32,16]{1,0:T(8,128)S(1)} %bitcast.39, bf16[16,16,2,32,256]{4,3,2,1,0:T(8,128)(2,1)S(1)} %get-tuple-element.35.w_ref, bf16[8,528,256]{2,1,0:T(8,128)(2,1)S(1)} %shard_map.96.refs_0_), custom_call_target="tpu_custom_call" | custom-call | flops 1073741824 | bytes 16777216 | tf_op jit(solution)/shard_map/pallas_call | solution.py:365
  48.1 0.7 collective-permute-done.7.refs_0_
  48.9 8.5 %shard_map.98 = bf16[8,528,256]{2,1,0:T(8,128)(2,1)} custom-call(s32[16]{0:T(128)S(1)} %stack.67.order_ref, s32[32,16]{1,0:T(8,128)S(1)} %bitcast.40, bf16[16,16,2,32,256]{4,3,2,1,0:T(8,128)(2,1)S(1)} %get-tuple-element.35.w_ref, bf16[16,16,2,32,256]{4,3,2,1,0:T(8,128)(2,1)S(1)} %get-tuple-element.36.u_ref, ...), custom_call_target="tpu_custom_call" | custom-call | flops 3221225472 | bytes 20971520 | tf_op jit(solution)/shard_map/pallas_call | solution.py:377
  57.4 0.0 all-gather.6.cloned.1.call-done
  57.4 0.0 copy-start
  57.5 4.6 %all-to-all-start = ((bf16[8,528,256]{2,1,0:T(8,128)(2,1)}), bf16[8,528,256]{2,1,0:T(8,128)(2,1)}, u32[]{:S(2)}, u32[]{:S(2)}) async-start(bf16[8,528,256]{2,1,0:T(8,128)(2,1)} %shard_map.98), calls=%async_computation | async-start | bytes 4325376 | tf_op jit(solution)/shard_map/all_to_all | solution.py:413
  62.1 0.0 all-gather.4.cloned.1.call-start
  62.1 1.6 copy-done.2
  63.8 3.4 %shard_map.99.near_ref = f32[2,256,256]{2,1,0:T(8,128)S(1)} custom-call(s32[2,8]{1,0:T(2,128)S(1)} %bitcast.43, s32[2]{0:T(128)S(1)} %dynamic-slice_bitcast_fusion.count_ref, bf16[2,8,256,256]{3,2,1,0:T(8,128)(2,1)S(1)} %bitcast.32, bf16[16,256,256]{2,1,0:T(8,128)(2,1)S(1)} %bitcast.38), custom_call_target="tpu_custom_call" | custom-call | flops 536870912 | bytes 5242880 | tf_op jit(solution)/shard_map/pallas_call | solution.py:394
  67.2 22.2 %all-to-all-done.far_ref = bf16[8,528,256]{2,1,0:T(8,128)(2,1)} async-done(((bf16[8,528,256]{2,1,0:T(8,128)(2,1)}), bf16[8,528,256]{2,1,0:T(8,128)(2,1)}, u32[]{:S(2)}, u32[]{:S(2)}) %all-to-all-start) | async-done | bytes 2162720 | tf_op jit(solution)/shard_map/all_to_all | solution.py:413
  89.4 2.7 %shard_map.100 = (f32[2,256,256]{2,1,0:T(8,128)S(1)}, f32[2,256]{1,0:T(2,128)S(1)}, bf16[2,256,256]{2,1,0:T(8,128)(2,1)}, bf16[528,256]{1,0:T(8,128)(2,1)S(1)}) custom-call(bf16[8,528,256]{2,1,0:T(8,128)(2,1)} %all-to-all-done.far_ref, f32[2,256,256]{2,1,0:T(8,128)S(1)} %shard_map.99.near_ref, bf16[2,256,256]{2,1,0:T(8,128)(2,1)S(1)} %bitcast.36), custom_call_target="tpu_custom_call" | custom-call | tf_op jit(solution)/shard_map/pallas_call | solution.py:426
  92.1 0.0 copy-start.5
  92.1 0.7 copy-done.5
  92.8 0.0 all-gather.4.cloned.1.call-update
  92.8 2.0 %collective-permute-start.8 = (bf16[528,256]{1,0:T(8,128)(2,1)}, bf16[528,256]{1,0:T(8,128)(2,1)S(1)}, u32[]{:S(2)}, u32[]{:S(2)}) collective-permute-start(bf16[528,256]{1,0:T(8,128)(2,1)} %copy-done.5), channel_id=1, source_target_pairs={{0,64},{8,72},{16,80},{24,88},{32,96},{40,104},{48,112},{56,120},{... | collective-permute-start | bytes 811016 | tf_op jit(solution)/shard_map/ppermute | solution.py:330
  94.8 0.3 collective-permute-start.9
  95.1 1.8 collective-permute-start.10
  96.8 0.6 collective-permute-start.11
  97.4 7.8 %collective-permute-done.8.refs_1_ = bf16[528,256]{1,0:T(8,128)(2,1)S(1)} collective-permute-done((bf16[528,256]{1,0:T(8,128)(2,1)}, bf16[528,256]{1,0:T(8,128)(2,1)S(1)}, u32[]{:S(2)}, u32[]{:S(2)}) %collective-permute-start.8) | collective-permute-done | bytes 270368 | tf_op jit(solution)/shard_map/ppermute | solution.py:330
  105.2 0.0 collective-permute-start.12
  105.2 2.0 %collective-permute-start.13 = (bf16[528,256]{1,0:T(8,128)(2,1)S(1)}, bf16[528,256]{1,0:T(8,128)(2,1)}, u32[]{:S(2)}, u32[]{:S(2)}) collective-permute-start(bf16[528,256]{1,0:T(8,128)(2,1)S(1)} %collective-permute-done.8.refs_1_), channel_id=1, source_target_pairs={{0,16},{8,24},{16,32},{24,40},{32,48},{40,56},{48,0},{56,8},{64,80... | collective-permute-start | bytes 811016 | tf_op jit(solution)/shard_map/ppermute | solution.py:332
  107.3 6.7 %shard_map.101 = (bf16[16,16,2,32,256]{4,3,2,1,0:T(8,128)(2,1)S(1)}, bf16[16,16,2,32,256]{4,3,2,1,0:T(8,128)(2,1)S(1)}, f32[8,128]{1,0:T(8,128)}) custom-call(bf16[16,16,2,32,256]{4,3,2,1,0:T(8,128)(2,1)} %w_ref.1, bf16[16,16,2,32,256]{4,3,2,1,0:T(8,128)(2,1)} %u_ref.2), custom_call_target="tpu_custom_call" | custom-call | bytes 33554432 | tf_op jit(solution)/shard_map/pallas_call | solution.py:346
  114.0 0.0 collective-permute-done.10.refs_3_
  114.0 2.2 %collective-permute-done.12.refs_5_ = bf16[528,256]{1,0:T(8,128)(2,1)} collective-permute-done((bf16[528,256]{1,0:T(8,128)(2,1)S(1)}, bf16[528,256]{1,0:T(8,128)(2,1)}, u32[]{:S(2)}, u32[]{:S(2)}) %collective-permute-start.12) | collective-permute-done | bytes 270368 | tf_op jit(solution)/shard_map/ppermute | solution.py:332
  116.2 5.3 %collective-permute-done.13.refs_6_ = bf16[528,256]{1,0:T(8,128)(2,1)} collective-permute-done((bf16[528,256]{1,0:T(8,128)(2,1)S(1)}, bf16[528,256]{1,0:T(8,128)(2,1)}, u32[]{:S(2)}, u32[]{:S(2)}) %collective-permute-start.13) | collective-permute-done | bytes 270368 | tf_op jit(solution)/shard_map/ppermute | solution.py:332
  121.5 0.7 copy-done.8
  122.2 1.4 shard_map.102.refs_0_
  123.6 0.1 collective-permute-start.15
  123.7 3.5 %shard_map.103 = (bf16[16,8,64,256]{3,2,1,0:T(8,128)(2,1)S(1)}, f32[16,256]{1,0:T(8,128)S(1)}) custom-call(s32[16]{0:T(128)S(1)} %stack.67.order_ref, s32[32,16]{1,0:T(8,128)S(1)} %bitcast.41, bf16[16,16,2,32,256]{4,3,2,1,0:T(8,128)(2,1)S(1)} %get-tuple-element.47.w_ref, bf16[8,528,256]{2,1,0:T(8,128)(2,1)S(1)} %shard_map.102.refs_0_), custom_call_target="tpu_custom_call" | custom-call | flops 1073741824 | bytes 16777216 | tf_op jit(solution)/shard_map/pallas_call | solution.py:365
  127.2 0.7 collective-permute-done.15.refs_0_
  128.0 8.5 %shard_map.104 = bf16[8,528,256]{2,1,0:T(8,128)(2,1)} custom-call(s32[16]{0:T(128)S(1)} %stack.67.order_ref, s32[32,16]{1,0:T(8,128)S(1)} %bitcast.42, bf16[16,16,2,32,256]{4,3,2,1,0:T(8,128)(2,1)S(1)} %get-tuple-element.47.w_ref, bf16[16,16,2,32,256]{4,3,2,1,0:T(8,128)(2,1)S(1)} %get-tuple-element.48.u_ref, ...), custom_call_target="tpu_custom_call" | custom-call | flops 3221225472 | bytes 20971520 | tf_op jit(solution)/shard_map/pallas_call | solution.py:377
  136.5 0.0 all-gather.4.cloned.1.call-done.panel_ref
  136.5 4.4 %all-to-all-start.1 = ((bf16[8,528,256]{2,1,0:T(8,128)(2,1)}), bf16[8,528,256]{2,1,0:T(8,128)(2,1)}, u32[]{:S(2)}, u32[]{:S(2)}) async-start(bf16[8,528,256]{2,1,0:T(8,128)(2,1)} %shard_map.104), calls=%async_computation.1 | async-start | bytes 4325376 | tf_op jit(solution)/shard_map/all_to_all | solution.py:413
  140.9 1.6 copy-done.3
  142.5 3.4 %shard_map.105.near_ref = f32[2,256,256]{2,1,0:T(8,128)S(1)} custom-call(s32[2,8]{1,0:T(2,128)S(1)} %bitcast.44, s32[2]{0:T(128)S(1)} %dynamic-slice_bitcast_fusion.count_ref, bf16[2,8,256,256]{3,2,1,0:T(8,128)(2,1)S(1)} %bitcast.33, bf16[16,256,256]{2,1,0:T(8,128)(2,1)S(1)} %copy-done.3), custom_call_target="tpu_custom_call" | custom-call | flops 536870912 | bytes 5242880 | tf_op jit(solution)/shard_map/pallas_call | solution.py:394
  145.9 22.3 %all-to-all-done.1.far_ref = bf16[8,528,256]{2,1,0:T(8,128)(2,1)} async-done(((bf16[8,528,256]{2,1,0:T(8,128)(2,1)}), bf16[8,528,256]{2,1,0:T(8,128)(2,1)}, u32[]{:S(2)}, u32[]{:S(2)}) %all-to-all-start.1) | async-done | bytes 2162720 | tf_op jit(solution)/shard_map/all_to_all | solution.py:413
  168.2 2.8 %shard_map.106 = (bf16[2,256,256]{2,1,0:T(8,128)(2,1)}, f32[2,256,256]{2,1,0:T(8,128)}, f32[2,256]{1,0:T(2,128)}) custom-call(bf16[8,528,256]{2,1,0:T(8,128)(2,1)} %all-to-all-done.1.far_ref, f32[2,256,256]{2,1,0:T(8,128)S(1)} %shard_map.105.near_ref, bf16[2,256,256]{2,1,0:T(8,128)(2,1)S(1)} %bitcast.37, f32[2,256,256]{2,1,0:T(8,128)S(1)} %get-tuple-element.56.image_ref, ...), custom_call_target="tpu_custom_call" | custom-call | tf_op jit(solution)/shard_map/pallas_call | solution.py:442
  (26 shorter events, 0.1 us)
Async XLA Ops:
  7.2 11.8 %copy-start.11 = (s32[1,16]{1,0:T(1,128)S(1)}, s32[1,16]{1,0:T(1,128)}, u32[]{:S(2)}) copy-start(s32[1,16]{1,0:T(1,128)} %param.13) | copy-start | bytes 196
  7.2 11.8 %copy-start.10 = (s32[1,16,8]{1,2,0:T(8,128)S(1)}, s32[1,16,8]{1,2,0:T(8,128)}, u32[]{:S(2)}) copy-start(s32[1,16,8]{1,2,0:T(8,128)} %param.12) | copy-start | bytes 1540
  7.2 22.9 %copy-start.9 = (s32[16,16,2]{1,2,0:T(2,128)S(1)}, s32[16,16,2]{1,2,0:T(2,128)}, u32[]{:S(2)}) copy-start(s32[16,16,2]{1,2,0:T(2,128)} %param.10) | copy-start | bytes 6148
  7.2 50.2 %all-gather.6.cloned.1.call-start = ((), (), s32[]{:S(2)}) async-start(), calls=%async_computation.3 | async-start | bytes 2359296 | tf_op jit(solution)/shard_map/all_gather | solution.py:409
  9.9 9.8 %collective-permute-start = (bf16[528,256]{1,0:T(8,128)(2,1)}, bf16[528,256]{1,0:T(8,128)(2,1)S(1)}, u32[]{:S(2)}, u32[]{:S(2)}) collective-permute-start(bf16[528,256]{1,0:T(8,128)(2,1)} %shard_map.95.refs_0_), channel_id=1, source_target_pairs={{0,64},{8,72},{16,80},{24,88},{32,96},{40,104},{48,112},{56,120},{... | collective-permute-start | bytes 811016 | tf_op jit(solution)/shard_map/ppermute | solution.py:330
  13.0 17.1 %collective-permute-start.1 = (bf16[528,256]{1,0:T(8,128)(2,1)}, bf16[528,256]{1,0:T(8,128)(2,1)S(1)}, u32[]{:S(2)}, u32[]{:S(2)}) collective-permute-start(bf16[528,256]{1,0:T(8,128)(2,1)} %shard_map.95.refs_0_), channel_id=1, source_target_pairs={{0,48},{8,56},{16,0},{24,8},{32,16},{40,24},{48,32},{56,40},{64,11... | collective-permute-start | bytes 811016 | tf_op jit(solution)/shard_map/ppermute | solution.py:331
  17.1 20.5 %collective-permute-start.2 = (bf16[528,256]{1,0:T(8,128)(2,1)}, bf16[528,256]{1,0:T(8,128)(2,1)S(1)}, u32[]{:S(2)}, u32[]{:S(2)}) collective-permute-start(bf16[528,256]{1,0:T(8,128)(2,1)} %shard_map.95.refs_0_), channel_id=1, source_target_pairs={{0,16},{8,24},{16,32},{24,40},{32,48},{40,56},{48,0},{56,8},{64,80... | collective-permute-start | bytes 811016 | tf_op jit(solution)/shard_map/ppermute | solution.py:331
  17.1 20.5 %collective-permute-start.3 = (bf16[528,256]{1,0:T(8,128)(2,1)}, bf16[528,256]{1,0:T(8,128)(2,1)S(1)}, u32[]{:S(2)}, u32[]{:S(2)}) collective-permute-start(bf16[528,256]{1,0:T(8,128)(2,1)} %shard_map.95.refs_0_), channel_id=1, source_target_pairs={{0,32},{8,40},{16,48},{24,56},{32,0},{40,8},{48,16},{56,24},{64,96... | collective-permute-start | bytes 811016 | tf_op jit(solution)/shard_map/ppermute | solution.py:331
  19.7 20.4 %collective-permute-start.4 = (bf16[528,256]{1,0:T(8,128)(2,1)S(1)}, bf16[528,256]{1,0:T(8,128)(2,1)S(1)}, u32[]{:S(2)}, u32[]{:S(2)}) collective-permute-start(bf16[528,256]{1,0:T(8,128)(2,1)S(1)} %collective-permute-done.refs_1_), channel_id=1, source_target_pairs={{0,48},{8,56},{16,0},{24,8},{32,16},{40,24},{48,32},{56,40},{64,11... | collective-permute-start | bytes 811016 | tf_op jit(solution)/shard_map/ppermute | solution.py:332
  24.0 19.6 %collective-permute-start.5 = (bf16[528,256]{1,0:T(8,128)(2,1)S(1)}, bf16[528,256]{1,0:T(8,128)(2,1)S(1)}, u32[]{:S(2)}, u32[]{:S(2)}) collective-permute-start(bf16[528,256]{1,0:T(8,128)(2,1)S(1)} %collective-permute-done.refs_1_), channel_id=1, source_target_pairs={{0,16},{8,24},{16,32},{24,40},{32,48},{40,56},{48,0},{56,8},{64,80... | collective-permute-start | bytes 811016 | tf_op jit(solution)/shard_map/ppermute | solution.py:332
  30.1 13.4 %collective-permute-start.6 = (bf16[528,256]{1,0:T(8,128)(2,1)S(1)}, bf16[528,256]{1,0:T(8,128)(2,1)S(1)}, u32[]{:S(2)}, u32[]{:S(2)}) collective-permute-start(bf16[528,256]{1,0:T(8,128)(2,1)S(1)} %collective-permute-done.refs_1_), channel_id=1, source_target_pairs={{0,32},{8,40},{16,48},{24,56},{32,0},{40,8},{48,16},{56,24},{64,96... | collective-permute-start | bytes 811016 | tf_op jit(solution)/shard_map/ppermute | solution.py:332
  30.8 12.7 %copy-start.4 = (bf16[528,256]{1,0:T(8,128)(2,1)S(1)}, bf16[528,256]{1,0:T(8,128)(2,1)}, u32[]{:S(2)}) copy-start(bf16[528,256]{1,0:T(8,128)(2,1)} %shard_map.95.refs_0_) | copy-start | bytes 811012
  43.5 0.7 copy-start.7
  44.5 4.3 %collective-permute-start.7 = (bf16[8,528,256]{2,1,0:T(8,128)(2,1)S(1)}, bf16[8,528,256]{2,1,0:T(8,128)(2,1)S(1)}, u32[]{:S(2)}, u32[]{:S(2)}) collective-permute-start(bf16[8,528,256]{2,1,0:T(8,128)(2,1)S(1)} %shard_map.96.refs_0_), channel_id=1, source_target_pairs={{0,8},{8,0},{16,24},{24,16},{32,40},{40,32},{48,56},{56,48},{64,72... | collective-permute-start | bytes 6488072 | tf_op jit(solution)/shard_map/ppermute | solution.py:334
  57.4 4.7 %copy-start = (bf16[1,2,8,256,256]{4,3,2,1,0:T(8,128)(2,1)S(1)}, bf16[1,2,8,256,256]{4,3,2,1,0:T(8,128)(2,1)}, u32[]{:S(2)}) copy-start(bf16[1,2,8,256,256]{4,3,2,1,0:T(8,128)(2,1)} %param.11) | copy-start | bytes 6291460
  57.5 31.9 %all-to-all-start = ((bf16[8,528,256]{2,1,0:T(8,128)(2,1)}), bf16[8,528,256]{2,1,0:T(8,128)(2,1)}, u32[]{:S(2)}, u32[]{:S(2)}) async-start(bf16[8,528,256]{2,1,0:T(8,128)(2,1)} %shard_map.98), calls=%async_computation | async-start | bytes 4325376 | tf_op jit(solution)/shard_map/all_to_all | solution.py:413
  62.1 27.3 %copy-start.1 = (bf16[1,2,256,256]{3,2,1,0:T(8,128)(2,1)S(1)}, bf16[1,2,256,256]{3,2,1,0:T(8,128)(2,1)}, u32[]{:S(2)}) copy-start(bf16[1,2,256,256]{3,2,1,0:T(8,128)(2,1)} %param.7) | copy-start | bytes 786436
  62.1 74.5 %all-gather.4.cloned.1.call-start = ((), (), s32[]{:S(2)}) async-start(), calls=%async_computation.2 | async-start | bytes 2359296 | tf_op jit(solution)/shard_map/all_gather | solution.py:409
  62.1 1.6 copy-start.2
  92.1 0.7 copy-start.5
  92.8 28.7 %copy-start.6 = (bf16[528,256]{1,0:T(8,128)(2,1)S(1)}, bf16[528,256]{1,0:T(8,128)(2,1)}, u32[]{:S(2)}) copy-start(bf16[528,256]{1,0:T(8,128)(2,1)} %copy-done.5) | copy-start | bytes 811012
  92.8 12.4 %collective-permute-start.8 = (bf16[528,256]{1,0:T(8,128)(2,1)}, bf16[528,256]{1,0:T(8,128)(2,1)S(1)}, u32[]{:S(2)}, u32[]{:S(2)}) collective-permute-start(bf16[528,256]{1,0:T(8,128)(2,1)} %copy-done.5), channel_id=1, source_target_pairs={{0,64},{8,72},{16,80},{24,88},{32,96},{40,104},{48,112},{56,120},{... | collective-permute-start | bytes 811016 | tf_op jit(solution)/shard_map/ppermute | solution.py:330
  94.8 12.5 %collective-permute-start.9 = (bf16[528,256]{1,0:T(8,128)(2,1)}, bf16[528,256]{1,0:T(8,128)(2,1)S(1)}, u32[]{:S(2)}, u32[]{:S(2)}) collective-permute-start(bf16[528,256]{1,0:T(8,128)(2,1)} %copy-done.5), channel_id=1, source_target_pairs={{0,48},{8,56},{16,0},{24,8},{32,16},{40,24},{48,32},{56,40},{64,11... | collective-permute-start | bytes 811016 | tf_op jit(solution)/shard_map/ppermute | solution.py:331
  95.1 18.9 %collective-permute-start.10 = (bf16[528,256]{1,0:T(8,128)(2,1)}, bf16[528,256]{1,0:T(8,128)(2,1)}, u32[]{:S(2)}, u32[]{:S(2)}) collective-permute-start(bf16[528,256]{1,0:T(8,128)(2,1)} %copy-done.5), channel_id=1, source_target_pairs={{0,16},{8,24},{16,32},{24,40},{32,48},{40,56},{48,0},{56,8},{64,80... | collective-permute-start | bytes 811016 | tf_op jit(solution)/shard_map/ppermute | solution.py:331
  96.8 17.2 %collective-permute-start.11 = (bf16[528,256]{1,0:T(8,128)(2,1)}, bf16[528,256]{1,0:T(8,128)(2,1)}, u32[]{:S(2)}, u32[]{:S(2)}) collective-permute-start(bf16[528,256]{1,0:T(8,128)(2,1)} %copy-done.5), channel_id=1, source_target_pairs={{0,32},{8,40},{16,48},{24,56},{32,0},{40,8},{48,16},{56,24},{64,96... | collective-permute-start | bytes 811016 | tf_op jit(solution)/shard_map/ppermute | solution.py:331
  105.2 10.9 %collective-permute-start.12 = (bf16[528,256]{1,0:T(8,128)(2,1)S(1)}, bf16[528,256]{1,0:T(8,128)(2,1)}, u32[]{:S(2)}, u32[]{:S(2)}) collective-permute-start(bf16[528,256]{1,0:T(8,128)(2,1)S(1)} %collective-permute-done.8.refs_1_), channel_id=1, source_target_pairs={{0,48},{8,56},{16,0},{24,8},{32,16},{40,24},{48,32},{56,40},{64,11... | collective-permute-start | bytes 811016 | tf_op jit(solution)/shard_map/ppermute | solution.py:332
  105.2 16.3 %collective-permute-start.13 = (bf16[528,256]{1,0:T(8,128)(2,1)S(1)}, bf16[528,256]{1,0:T(8,128)(2,1)}, u32[]{:S(2)}, u32[]{:S(2)}) collective-permute-start(bf16[528,256]{1,0:T(8,128)(2,1)S(1)} %collective-permute-done.8.refs_1_), channel_id=1, source_target_pairs={{0,16},{8,24},{16,32},{24,40},{32,48},{40,56},{48,0},{56,8},{64,80... | collective-permute-start | bytes 811016 | tf_op jit(solution)/shard_map/ppermute | solution.py:332
  107.3 14.3 %collective-permute-start.14 = (bf16[528,256]{1,0:T(8,128)(2,1)S(1)}, bf16[528,256]{1,0:T(8,128)(2,1)}, u32[]{:S(2)}, u32[]{:S(2)}) collective-permute-start(bf16[528,256]{1,0:T(8,128)(2,1)S(1)} %collective-permute-done.8.refs_1_), channel_id=1, source_target_pairs={{0,32},{8,40},{16,48},{24,56},{32,0},{40,8},{48,16},{56,24},{64,96... | collective-permute-start | bytes 811016 | tf_op jit(solution)/shard_map/ppermute | solution.py:332
  121.5 0.7 copy-start.8
  123.6 4.3 %collective-permute-start.15 = (bf16[8,528,256]{2,1,0:T(8,128)(2,1)S(1)}, bf16[8,528,256]{2,1,0:T(8,128)(2,1)S(1)}, u32[]{:S(2)}, u32[]{:S(2)}) collective-permute-start(bf16[8,528,256]{2,1,0:T(8,128)(2,1)S(1)} %shard_map.102.refs_0_), channel_id=1, source_target_pairs={{0,8},{8,0},{16,24},{24,16},{32,40},{40,32},{48,56},{56,48},{64,72... | collective-permute-start | bytes 6488072 | tf_op jit(solution)/shard_map/ppermute | solution.py:334
  136.5 31.7 %all-to-all-start.1 = ((bf16[8,528,256]{2,1,0:T(8,128)(2,1)}), bf16[8,528,256]{2,1,0:T(8,128)(2,1)}, u32[]{:S(2)}, u32[]{:S(2)}) async-start(bf16[8,528,256]{2,1,0:T(8,128)(2,1)} %shard_map.104), calls=%async_computation.1 | async-start | bytes 4325376 | tf_op jit(solution)/shard_map/all_to_all | solution.py:413
  140.9 1.6 copy-start.3
Sparse Core Ops, SparseCore 0:
  9.7 43.7 all-gather.5
  92.9 37.5 all-gather.3

commit v3 on v2

--- a/solution.py
+++ b/solution.py
@@ -49,7 +49,7 @@
     out_ref[per_dev * size :, :] = put_sums((square, cross), width)
 
 
-def load_kernel(w_ref, u_ref, held_w, held_u, done_ref, w_sem, u_sem):
+def load_kernel(w_ref, u_ref, held_w, held_u, w_sem, u_sem):
     copies = []
     for source, target, sems in ((w_ref, held_w, w_sem), (u_ref, held_u, u_sem)):
         copies += [
@@ -60,7 +60,6 @@
         copy.start()
     for copy in copies:
         copy.wait()
-    done_ref[...] = jnp.zeros_like(done_ref)
 
 
 def pack_kernel(*refs):
@@ -117,21 +116,19 @@
     coder.run(coded_ref, sums_ref, False)
 
 
-def far_kernel(order_ref, rank_ref, w_ref, u_ref, early_ref, early_sums_ref, *refs):
-    fields, refs = refs[:-8], refs[-8:]
-    out_ref, field_buf, coded_ref, out_buf, sums_ref, field_sem, early_sem, out_sem = refs
-    receivers, rows, width = out_ref.shape
+def far_kernel(order_ref, rank_ref, target_ref, w_ref, u_ref, early_ref, early_sums_ref, *refs):
+    fields, refs = refs[:-11], refs[-11:]
+    cross_ref, stay_ref, around_refs, near_ref = refs[0], refs[1], refs[2:5], refs[5]
+    field_buf, coded_ref, sums_ref, field_sem, early_sem = refs[6:]
+    turns = cross_ref.shape[0]
+    width = cross_ref.shape[2]
     _, _, per_dev, _, size = u_ref.shape
-    blocks = per_dev * size
     early = early_ref.shape[1]
 
     def early_copy(slot):
         return pltpu.make_async_copy(
             early_ref.at[:, slot], coded_ref.at[:, order_ref[slot]], early_sem.at[slot]
         )
-
-    def out_copy(j):
-        return pltpu.make_async_copy(out_buf.at[j], out_ref.at[j], out_sem.at[j])
 
     coder = Coder(early, order_ref, rank_ref, w_ref, fields, field_buf, field_sem)
     coder.load()
@@ -143,21 +140,43 @@
     for slot in range(early):
         early_copy(slot).wait()
 
-    def expand(j, carry):
-        for p in range(per_dev):
-            u = u_ref[per_dev * j + p].reshape(-1, size)
-            value = coded_ref[per_dev * j + p].reshape(-1, width)
-            total = lax.dot_general(
-                u, value, (((0,), (0,)), ((), ())), preferred_element_type=jnp.float32
-            )
-            out_buf[j, p * size : (p + 1) * size, :] = total.astype(jnp.bfloat16)
-        out_buf[j, blocks:, :] = extra
-        out_copy(j).start()
-        return carry
-
-    lax.fori_loop(0, receivers, expand, 0)
-    for j in range(receivers):
-        out_copy(j).wait()
+    def expand(target):
+        u = u_ref[target].reshape(-1, size)
+        value = coded_ref[target].reshape(-1, width)
+        total = lax.dot_general(
+            u, value, (((0,), (0,)), ((), ())), preferred_element_type=jnp.float32
+        )
+        return total.astype(jnp.bfloat16)
+
+    for turn in range(turns):
+        around_ref = near_ref if turn == 0 else around_refs[turn - 1]
+        for side, first_ref in ((1, cross_ref), (0, stay_ref)):
+            target = target_ref[side * turns + turn] * per_dev
+            first_ref[turn] = expand(target)
+            around_ref[side * size : (side + 1) * size, :] = expand(target + 1)
+        around_ref[2 * size :, :] = extra
+
+
+def add_kernel(
+    stay_ref, cross_ref, near_ref, a1_ref, a2_ref, a3_ref,
+    first_ref, s1_ref, s2_ref, s3_ref, second_ref, send_ref, sums_ref,
+):
+    size = stay_ref.shape[1]
+    for turn, out_ref in enumerate((first_ref, s1_ref, s2_ref, s3_ref)):
+        total = stay_ref[turn].astype(jnp.float32) + cross_ref[turn].astype(jnp.float32)
+        out_ref[...] = total.astype(out_ref.dtype)
+
+    def rows(start, stop):
+        total = near_ref[start:stop, :].astype(jnp.float32)
+        for ref in (a1_ref, a2_ref, a3_ref):
+            total += ref[start:stop, :].astype(jnp.float32)
+        return total
+
+    second_ref[...] = rows(0, size)
+    send_ref[:size, :] = rows(size, 2 * size).astype(jnp.bfloat16)
+    sums = get_sums(rows(2 * size, 2 * size + EXTRA))
+    send_ref[size:, :] = put_sums(sums, send_ref.shape[1])
+    sums_ref[0:1, :], sums_ref[1:2, :] = sums
 
 
 def near_kernel(cols_ref, count_ref, tiles_ref, panel_ref, out_ref, panel_buf, tile_buf, sems):
@@ -182,36 +201,29 @@
 
 
 class FarTotal:
-    def __init__(self, far_ref, buf, sems):
-        self.buf = buf
-        self.copies = [
-            pltpu.make_async_copy(far_ref.at[s], buf.at[s], sems.at[s])
-            for s in range(buf.shape[0])
-        ]
-        for copy in self.copies:
-            copy.start()
-
-    def wait(self):
-        for copy in self.copies:
-            copy.wait()
-
-    def rows(self, start, stop):
-        total = self.buf[0, start:stop, :].astype(jnp.float32)
-        for s in range(1, self.buf.shape[0]):
-            total += self.buf[s, start:stop, :].astype(jnp.float32)
+    def __init__(self, first_ref, r1_ref, r2_ref, r3_ref, second_ref, cross_ref, sums_ref):
+        self.blocks = ((first_ref, r1_ref, r2_ref, r3_ref), (second_ref, cross_ref))
+        self.sums_ref = sums_ref
+
+    def block(self, p):
+        total, *others = self.blocks[p]
+        size = total.shape[0]
+        total = total[...]
+        for ref in others:
+            total += ref[:size, :].astype(jnp.float32)
         return total
 
     def sums(self):
-        rows = self.buf.shape[1]
-        return get_sums(self.rows(rows - EXTRA, rows))
-
-
-def middle_kernel(
-    far_ref, near_ref, x_ref, image_ref, sums_ref, z_ref, out_ref, far_buf, far_sem, *, total_rows
-):
+        cross_ref = self.blocks[1][1]
+        size = cross_ref.shape[0] - EXTRA
+        came = get_sums(cross_ref[size:, :].astype(jnp.float32))
+        return self.sums_ref[0:1, :] + came[0], self.sums_ref[1:2, :] + came[1]
+
+
+def middle_kernel(*refs, total_rows):
+    near_ref, x_ref, image_ref, sums_ref, z_ref, out_ref = refs[7:]
     per_dev, size, width = x_ref.shape
-    far = FarTotal(far_ref, far_buf, far_sem)
-    far.wait()
+    far = FarTotal(*refs[:7])
     square_x, cross_x = far.sums()
     guess = cross_x / (square_x + EPS * total_rows)
     sums_ref[0:1, :] = square_x
@@ -219,7 +231,7 @@
     cross = jnp.zeros((1, width), jnp.float32)
     square = jnp.zeros((1, width), jnp.float32)
     for p in range(per_dev):
-        image = far.rows(p * size, (p + 1) * size) + near_ref[p]
+        image = far.block(p) + near_ref[p]
         image_ref[p] = image
         x = x_ref[p].astype(jnp.float32)
         moved = image - guess * x
@@ -231,17 +243,14 @@
     out_ref[per_dev * size :, :] = put_sums((cross, square), width)
 
 
-def last_kernel(
-    far_ref, near_ref, x_ref, image_ref, sums_ref, basis_ref, out_ref, coef_ref, far_buf, far_sem,
-    *, total_rows,
-):
-    per_dev, size, _ = x_ref.shape
-    far = FarTotal(far_ref, far_buf, far_sem)
-    far.wait()
+def last_kernel(*refs, total_rows):
+    near_ref, x_ref, image_ref, scale_ref, basis_ref, out_ref, coef_ref = refs[7:]
+    per_dev = x_ref.shape[0]
+    far = FarTotal(*refs[:7])
     cross, square = far.sums()
     cross, square = cross / total_rows, square / total_rows
-    mean_x = sums_ref[0:1, :] / total_rows
-    guess = sums_ref[1:2, :]
+    mean_x = scale_ref[0:1, :] / total_rows
+    guess = scale_ref[1:2, :]
     scale = lax.rsqrt(mean_x + EPS)
     proj = scale * scale * (cross + guess * mean_x)
     off = proj - guess
@@ -254,7 +263,7 @@
         image = image_ref[p]
         x = x_ref[p].astype(jnp.float32)
         basis_ref[p] = ((image - guess * x - off * x) * factor).astype(jnp.bfloat16)
-        second = far.rows(p * size, (p + 1) * size) + near_ref[p]
+        second = far.block(p) + near_ref[p]
         out_ref[p] = (second - off * image) * factor
 
 
@@ -296,6 +305,16 @@
         return pl.CostEstimate(flops=flops, bytes_accessed=mib * MIB, transcendentals=0)
 
     zs = chips // 2
+    ys = slice_count // 2
+    my_x, my_y = my_slice // ys, my_slice % ys
+    receivers = jnp.stack(
+        [(my_x + side) % 2 * ys + (my_y + turn) % ys for side in range(2) for turn in range(ys)]
+    ).astype(i32)
+    flip_x = [(i, (i + ys) % slice_count) for i in range(slice_count)]
+
+    def up_y(turn):
+        return [(i, i // ys * ys + (i + turn) % ys) for i in range(slice_count)]
+
     z_turns = (0, 1, 3, 2)
 
     def along_z(turn):
@@ -329,7 +348,8 @@
     def gather_panels(payload, loaded):
         far = lax.ppermute(payload, "blk", flip_far)
         own = [lax.ppermute(payload, "blk", along_z(turn)) for turn in z_turns[1:]]
-        late = [lax.ppermute(far, "blk", along_z(turn)) for turn in z_turns[1:]]
+        late = [lax.ppermute(far, "blk", along_z(turn)) for turn in z_turns[1:3]]
+        late.append(lax.ppermute(own[2], "blk", flip_far))
         own = pack([payload, far] + own + late, loaded)
         return [own], [lax.ppermute(own, "blk", flip_core)]
 
@@ -338,28 +358,24 @@
     def coder_scratch(n):
         return [pltpu.VMEM((n, rows, width), bf16)]
 
-    far_w, order, ranks, my_cols, my_count = lax.optimization_barrier(
-        (far_w, order, ranks, my_cols, my_count)
+    far_w, order, ranks, receivers, my_cols, my_count = lax.optimization_barrier(
+        (far_w, order, ranks, receivers, my_cols, my_count)
     )
 
     def load_factors(far_w, far_u):
         return pl.pallas_call(
             load_kernel,
-            out_shape=(
-                pltpu.VMEM(far_w.shape, bf16),
-                pltpu.VMEM(far_u.shape, bf16),
-                jax.ShapeDtypeStruct((8, 128), f32),
-            ),
+            out_shape=(pltpu.VMEM(far_w.shape, bf16), pltpu.VMEM(far_u.shape, bf16)),
             in_specs=[hbm, hbm],
-            out_specs=(vmem, vmem, vmem),
+            out_specs=(vmem, vmem),
             scratch_shapes=[sems((targets,)), sems((targets,))],
-            compiler_params=params(44),
+            compiler_params=params(34),
             cost_estimate=cost(0, 32),
         )(far_w, far_u)
 
     def far_products(payload, far_w, far_u):
-        held_w, held_u, loaded = load_factors(far_w, far_u)
-        early, late = gather_panels(payload, loaded)
+        held_w, held_u = load_factors(far_w, far_u)
+        early, late = gather_panels(payload, held_w)
         n = sum(field.shape[0] for field in early)
         m = panel_count - n
         coded, sums = pl.pallas_call(
@@ -374,21 +390,21 @@
             compiler_params=params(8),
             cost_estimate=cost(flops * n // panel_count, 16),
         )(order, ranks, held_w, *early)
+        around = jax.ShapeDtypeStruct((2 * size + EXTRA, width), bf16)
         return pl.pallas_call(
             far_kernel,
-            out_shape=in_hbm((slice_count, rows, width), bf16),
-            in_specs=[smem, smem, vmem, vmem, hbm, vmem] + [hbm] * len(late),
-            out_specs=hbm,
+            out_shape=(jax.ShapeDtypeStruct((ys, size, width), bf16),) * 2 + (around,) * ys,
+            in_specs=[smem, smem, smem, vmem, vmem, hbm, vmem] + [hbm] * len(late),
+            out_specs=(vmem,) * (2 + ys),
             scratch_shapes=coder_scratch(m)
             + [
                 pltpu.VMEM((targets, panel_count, per_dev * rank, width), bf16),
-                pltpu.VMEM((slice_count, rows, width), bf16),
                 pltpu.VMEM((EXTRA, width), f32),
             ]
-            + [sems((m,)), sems((n,)), sems((slice_count,))],
+            + [sems((m,)), sems((n,))],
             compiler_params=params(18),
             cost_estimate=cost(flops + flops * m // panel_count, 20),
-        )(order, ranks, held_w, held_u, coded, sums, *late)
+        )(order, ranks, receivers, held_w, held_u, coded, sums, *late)
 
     def near_products(panel):
         return pl.pallas_call(
@@ -409,8 +425,28 @@
         return lax.all_gather(blocks, "near", axis=0, tiled=True)
 
     def scatter_panel(parts, panel):
-        parts, panel = lax.optimization_barrier((parts, panel))
-        return lax.all_to_all(parts, "near", 0, 0, tiled=True), panel
+        cross, stay, *around = parts
+        around, own = around[:-1], around[-1]
+        cross = lax.ppermute(cross, "near", flip_x)
+        around = [lax.ppermute(part, "near", up_y(turn + 1)) for turn, part in enumerate(around)]
+        block = (size, width)
+        first, *sends, second, send, sums = pl.pallas_call(
+            add_kernel,
+            out_shape=(jax.ShapeDtypeStruct(block, f32),)
+            + (in_hbm(block, bf16),) * (ys - 1)
+            + (
+                jax.ShapeDtypeStruct(block, f32),
+                in_hbm((size + EXTRA, width), bf16),
+                jax.ShapeDtypeStruct((2, width), f32),
+            ),
+            in_specs=[vmem] * (3 + len(around)),
+            out_specs=(vmem,) * (ys + 3),
+            compiler_params=params(8),
+            cost_estimate=cost(0, 3),
+        )(stay, cross, own, *around)
+        send, panel = lax.optimization_barrier((send, panel))
+        sends = [lax.ppermute(part, "near", up_y(turn + 1)) for turn, part in enumerate(sends)]
+        return (first, *sends, second, lax.ppermute(send, "near", flip_x), sums), panel
 
     payload = pl.pallas_call(
         start_kernel,
@@ -422,20 +458,18 @@
     )(x, tiles)
     panel = gather_near(x)
     far_x, panel = scatter_panel(far_products(payload, far_w, far_u), panel)
-    far_scratch = [pltpu.VMEM((slice_count, rows, width), bf16), sems((slice_count,))]
     image, sums, z, payload = pl.pallas_call(
         functools.partial(middle_kernel, total_rows=total_rows),
         out_shape=(
-            jax.ShapeDtypeStruct((per_dev, size, width), f32),
+            in_hbm((per_dev, size, width), f32),
             jax.ShapeDtypeStruct((2, width), f32),
             in_hbm((per_dev, size, width), bf16),
             jax.ShapeDtypeStruct((rows, width), bf16),
         ),
-        in_specs=[hbm, vmem, vmem],
+        in_specs=[vmem] * 9,
         out_specs=(vmem,) * 4,
-        scratch_shapes=far_scratch,
         compiler_params=params(8),
-    )(far_x, near_products(panel), x)
+    )(*far_x, near_products(panel), x)
     panel = gather_near(z)
     payload, far_w, far_u = lax.optimization_barrier((payload, far_w, far_u))
     far_z, panel = scatter_panel(far_products(payload, far_w, far_u), panel)
@@ -446,11 +480,10 @@
             jax.ShapeDtypeStruct((per_dev, size, width), f32),
             jax.ShapeDtypeStruct((2, width), f32),
         ),
-        in_specs=[hbm, vmem, vmem, vmem, vmem],
+        in_specs=[vmem] * 11,
         out_specs=(vmem, vmem, vmem),
-        scratch_shapes=far_scratch,
         compiler_params=params(8),
-    )(far_z, near_products(panel), x, image, sums)
+    )(*far_z, near_products(panel), x, image, sums)
     return second_basis[None], second_image[None], coefficients
 
 

time: 179 us -> 162 us (0.905)
  waiting for transfers between devices: 74.6 us -> 48.4 us
  starting transfers between devices: 29.1 us -> 46 us
  Pallas kernels: 53.6 us -> 45.3 us
  other arithmetic: 0.19 us -> 2.24 us
    all_to_all x2 -> x0, waiting for transfers between devices: 44.5 us -> none  [scatter_panel(): return (lax.all_to_all(parts, 'near', 0, 0, tiled=True), panel)]
    ppermute x6 -> x22, starting transfers between devices: 6.3 us -> 31.1 us  [the longest x12 18.5 us: scatter_panel(): lax.ppermute(part, 'near', up_y(turn + 1))]
    ppermute x6 -> x22, waiting for transfers between devices: 13.5 us -> 33.9 us  [the longest x12 26.2 us: scatter_panel(): lax.ppermute(part, 'near', up_y(turn + 1))]
    all_to_all x2 -> x0, starting transfers between devices: 8.98 us -> none  [scatter_panel(): return (lax.all_to_all(parts, 'near', 0, 0, tiled=True), panel)]
    ppermute x2, waiting for transfers between devices: 8.35 us -> 3.13 us  [gather_panels(): far = lax.ppermute(payload, 'blk', flip_far)]
    ppermute x6, waiting for transfers between devices: 6.13 us -> 9.94 us  [gather_panels(): own = [lax.ppermute(payload, 'blk', along_z(turn)) for turn in z_turns[1:]]]
    pallas_call x2 -> x4, Pallas kernels: 17.1 us -> 14.4 us  [the longest x2 12.5 us: far_products(): pl.pallas_call(far_kernel, out_shape=(jax.ShapeDtypeStruct((ys, size, wid...]
    unnamed x24 -> x20, local copies, waits for them, and re-layouts: 5.29 us -> 3.22 us
  transfers between devices with their start and end apart: 20 -> 34, of which waited for: 11 -> 16; matrix products, arithmetic and copies ran while one was open for 0% -> 3% of each run, Pallas kernels for 27% -> 25%
where the time goes in v3:
time: 162 us
  waiting for transfers between devices  48.4 us (30%)
  starting transfers between devices  46 us (28%)
  Pallas kernels  45.3 us (28%)
  between operations  14.6 us (9%)
  local copies, waits for them, and re-layouts  5.16 us (3%)
  other arithmetic  2.24 us (1%)
    ppermute x12, waiting for transfers between devices, scatter_panel(): lax.ppermute(part, 'near', up_y(turn + 1))  26.2 us
    ppermute x12, starting transfers between devices, scatter_panel(): lax.ppermute(part, 'near', up_y(turn + 1))  18.5 us
    pallas_call x2, Pallas kernels, far_products(): pl.pallas_call(far_kernel, out_shape=(jax.ShapeDtypeStruct((ys, size, wid...  12.5 us
    pallas_call x2, Pallas kernels, load_factors(): pl.pallas_call(load_kernel, out_shape=(pltpu.VMEM(far_w.shape, bf16), plt...  12.3 us
    ppermute x6, starting transfers between devices, gather_panels(): own = [lax.ppermute(payload, 'blk', along_z(turn)) for turn in z_turns[1:]]  10.1 us
    ppermute x6, waiting for transfers between devices, gather_panels(): own = [lax.ppermute(payload, 'blk', along_z(turn)) for turn in z_turns[1:]]  9.94 us
    pallas_call x2, Pallas kernels, far_products(): pl.pallas_call(code_kernel, out_shape=(pltpu.VMEM((targets, n, per_dev *...  7.01 us
    ppermute x2, waiting for transfers between devices, gather_panels(): late.append(lax.ppermute(own[2], 'blk', flip_far))  7 us
  transfers between devices with their start and end apart: 34, of which 16 were waited for; matrix products, arithmetic and copies ran while one was open for 3% of the time, Pallas kernels for 25%

profile of v3, /device:TPU:0, one launch (start us, length us, event | category | flops | bytes accessed | tf_op | source)
XLA Modules:
  0.0 161.7 jit_solution(14667361739033802019)
XLA Ops:
  7.2 2.0 %shard_map.95.refs_0_ = bf16[528,256]{1,0:T(8,128)(2,1)} custom-call(bf16[2,256,256]{2,1,0:T(8,128)(2,1)} %bitcast.42, bf16[2,8,256,256]{3,2,1,0:T(8,128)(2,1)} %bitcast.39), custom_call_target="tpu_custom_call" | custom-call | tf_op jit(solution)/shard_map/pallas_call | solution.py:451
  9.2 3.1 %collective-permute-start = (bf16[528,256]{1,0:T(8,128)(2,1)}, bf16[528,256]{1,0:T(8,128)(2,1)S(1)}, u32[]{:S(2)}, u32[]{:S(2)}) collective-permute-start(bf16[528,256]{1,0:T(8,128)(2,1)} %shard_map.95.refs_0_), channel_id=1, source_target_pairs={{0,64},{8,72},{16,80},{24,88},{32,96},{40,104},{48,112},{56,120},{... | collective-permute-start | bytes 811016 | tf_op jit(solution)/shard_map/ppermute | solution.py:349
  12.3 4.0 %collective-permute-start.1 = (bf16[528,256]{1,0:T(8,128)(2,1)}, bf16[528,256]{1,0:T(8,128)(2,1)S(1)}, u32[]{:S(2)}, u32[]{:S(2)}) collective-permute-start(bf16[528,256]{1,0:T(8,128)(2,1)} %shard_map.95.refs_0_), channel_id=1, source_target_pairs={{0,48},{8,56},{16,0},{24,8},{32,16},{40,24},{48,32},{56,40},{64,11... | collective-permute-start | bytes 811016 | tf_op jit(solution)/shard_map/ppermute | solution.py:350
  16.3 1.9 %collective-permute-start.3 = (bf16[528,256]{1,0:T(8,128)(2,1)}, bf16[528,256]{1,0:T(8,128)(2,1)S(1)}, u32[]{:S(2)}, u32[]{:S(2)}) collective-permute-start(bf16[528,256]{1,0:T(8,128)(2,1)} %shard_map.95.refs_0_), channel_id=1, source_target_pairs={{0,32},{8,40},{16,48},{24,56},{32,0},{40,8},{48,16},{56,24},{64,96... | collective-permute-start | bytes 811016 | tf_op jit(solution)/shard_map/ppermute | solution.py:350
  18.3 0.7 iota_compare_fusion
  19.0 0.8 and_reduce_fusion
  19.7 0.1 copy.17
  19.8 3.4 %collective-permute-start.4 = (bf16[528,256]{1,0:T(8,128)(2,1)S(1)}, bf16[528,256]{1,0:T(8,128)(2,1)S(1)}, u32[]{:S(2)}, u32[]{:S(2)}) collective-permute-start(bf16[528,256]{1,0:T(8,128)(2,1)S(1)} %collective-permute-done.refs_1_), channel_id=1, source_target_pairs={{0,48},{8,56},{16,0},{24,8},{32,16},{40,24},{48,32},{56,40},{64,11... | collective-permute-start | bytes 811016 | tf_op jit(solution)/shard_map/ppermute | solution.py:351
  23.3 8.4 %collective-permute-done.3.refs_4_ = bf16[528,256]{1,0:T(8,128)(2,1)S(1)} collective-permute-done((bf16[528,256]{1,0:T(8,128)(2,1)}, bf16[528,256]{1,0:T(8,128)(2,1)S(1)}, u32[]{:S(2)}, u32[]{:S(2)}) %collective-permute-start.3) | collective-permute-done | bytes 270368 | tf_op jit(solution)/shard_map/ppermute | solution.py:350
  31.6 0.5 collective-permute-start.6
  32.2 0.8 and_select_fusion
  33.4 0.8 constant_dynamic-slice_fusion
  34.1 0.1 copy.19
  34.2 0.1 stack.103.target_ref
  34.3 0.1 stack.94.order_ref
  34.4 0.7 dynamic-slice_bitcast_fusion.count_ref
  35.1 6.2 %shard_map.94 = (bf16[16,16,2,32,256]{4,3,2,1,0:T(8,128)(2,1)S(1)}, bf16[16,16,2,32,256]{4,3,2,1,0:T(8,128)(2,1)S(1)}) custom-call(bf16[16,16,2,32,256]{4,3,2,1,0:T(8,128)(2,1)} %w_ref.1, bf16[16,16,2,32,256]{4,3,2,1,0:T(8,128)(2,1)} %u_ref.2), custom_call_target="tpu_custom_call" | custom-call | bytes 33554432 | tf_op jit(solution)/shard_map/pallas_call | solution.py:366
  41.3 3.8 %collective-permute-done.6.refs_7_ = bf16[528,256]{1,0:T(8,128)(2,1)S(1)} collective-permute-done((bf16[528,256]{1,0:T(8,128)(2,1)S(1)}, bf16[528,256]{1,0:T(8,128)(2,1)S(1)}, u32[]{:S(2)}, u32[]{:S(2)}) %collective-permute-start.6) | collective-permute-done | bytes 270368 | tf_op jit(solution)/shard_map/ppermute | solution.py:352
  45.1 0.3 shard_map.96.refs_0_
  45.5 0.1 collective-permute-start.7
  45.6 3.5 %shard_map.97 = (bf16[16,8,64,256]{3,2,1,0:T(8,128)(2,1)S(1)}, f32[16,256]{1,0:T(8,128)S(1)}) custom-call(s32[16]{0:T(128)S(1)} %stack.94.order_ref, s32[32,16]{1,0:T(8,128)S(1)} %bitcast.47, bf16[16,16,2,32,256]{4,3,2,1,0:T(8,128)(2,1)S(1)} %get-tuple-element.61.refs_8_.w_ref, bf16[8,528,256]{2,1,0:T(8,128)(2,1)S(1)} %shard_map.96.refs_0_), custom_call_target="tpu_custom_call" | custom-call | flops 1073741824 | bytes 16777216 | tf_op jit(solution)/shard_map/pallas_call | solution.py:381
  49.1 0.7 collective-permute-done.7.refs_0_
  49.8 6.3 %shard_map.98 = (bf16[4,256,256]{2,1,0:T(8,128)(2,1)S(1)}, bf16[4,256,256]{2,1,0:T(8,128)(2,1)S(1)}, bf16[528,256]{1,0:T(8,128)(2,1)S(1)}, bf16[528,256]{1,0:T(8...) custom-call(s32[16]{0:T(128)S(1)} %stack.94.order_ref, s32[32,16]{1,0:T(8,128)S(1)} %bitcast.48, ...), custom_call_target="tpu_custom_call" | custom-call | flops 3221225472 | bytes 20971520 | tf_op jit(solution)/shard_map/pallas_call | solution.py:394
  56.1 1.0 collective-permute-start.8
  57.0 1.3 collective-permute-start.9
  58.3 4.1 %collective-permute-start.10 = (bf16[528,256]{1,0:T(8,128)(2,1)S(1)}, bf16[528,256]{1,0:T(8,128)(2,1)S(1)}, u32[]{:S(2)}, u32[]{:S(2)}) collective-permute-start(bf16[528,256]{1,0:T(8,128)(2,1)S(1)} %get-tuple-element.69), channel_id=1, source_target_pairs={{0,2},{1,3},{2,0},{3,1},{4,6},{5,7},{6,4},{7,5},{8,10},{9,11},{10,... | collective-permute-start | bytes 811016 | tf_op jit(solution)/shard_map/ppermute | solution.py:431
  62.4 0.1 collective-permute-start.11
  62.6 4.9 %collective-permute-done.9.a1_ref = bf16[528,256]{1,0:T(8,128)(2,1)S(1)} collective-permute-done((bf16[528,256]{1,0:T(8,128)(2,1)S(1)}, bf16[528,256]{1,0:T(8,128)(2,1)S(1)}, u32[]{:S(2)}, u32[]{:S(2)}) %collective-permute-start.9) | collective-permute-done | bytes 270368 | tf_op jit(solution)/shard_map/ppermute | solution.py:431
  67.5 7.0 %collective-permute-done.10.a2_ref = bf16[528,256]{1,0:T(8,128)(2,1)S(1)} collective-permute-done((bf16[528,256]{1,0:T(8,128)(2,1)S(1)}, bf16[528,256]{1,0:T(8,128)(2,1)S(1)}, u32[]{:S(2)}, u32[]{:S(2)}) %collective-permute-start.10) | collective-permute-done | bytes 270368 | tf_op jit(solution)/shard_map/ppermute | solution.py:431
  74.4 0.9 shard_map.99
  75.3 1.3 collective-permute-start.15
  76.6 3.5 %collective-permute-start.13 = (bf16[256,256]{1,0:T(8,128)(2,1)}, bf16[256,256]{1,0:T(8,128)(2,1)S(1)}, u32[]{:S(2)}, u32[]{:S(2)}) collective-permute-start(bf16[256,256]{1,0:T(8,128)(2,1)} %get-tuple-element.73), channel_id=1, source_target_pairs={{0,2},{1,3},{2,0},{3,1},{4,6},{5,7},{6,4},{7,5},{8,10},{9,11},{10,... | collective-permute-start | bytes 393224 | tf_op jit(solution)/shard_map/ppermute | solution.py:448
  80.1 1.6 copy-done.6
  81.7 3.4 %shard_map.100.refs_7_ = f32[2,256,256]{2,1,0:T(8,128)S(1)} custom-call(s32[2,8]{1,0:T(2,128)S(1)} %bitcast.51, s32[2]{0:T(128)S(1)} %dynamic-slice_bitcast_fusion.count_ref, bf16[2,8,256,256]{3,2,1,0:T(8,128)(2,1)S(1)} %bitcast.40, bf16[16,256,256]{2,1,0:T(8,128)(2,1)S(1)} %bitcast.46), custom_call_target="tpu_custom_call" | custom-call | flops 536870912 | bytes 5242880 | tf_op jit(solution)/shard_map/pallas_call | solution.py:410
  85.2 1.1 collective-permute-done.13.refs_2_
  86.3 1.1 shard_map.101
  87.5 1.4 collective-permute-start.16
  88.9 2.2 %collective-permute-start.19 = (bf16[528,256]{1,0:T(8,128)(2,1)S(1)}, bf16[528,256]{1,0:T(8,128)(2,1)S(1)}, u32[]{:S(2)}, u32[]{:S(2)}) collective-permute-start(bf16[528,256]{1,0:T(8,128)(2,1)S(1)} %get-tuple-element.87.refs_0_), channel_id=1, source_target_pairs={{0,32},{8,40},{16,48},{24,56},{32,0},{40,8},{48,16},{56,24},{64,96... | collective-permute-start | bytes 811016 | tf_op jit(solution)/shard_map/ppermute | solution.py:350
  91.1 0.4 collective-permute-start.17
  91.5 1.6 collective-permute-start.18
  93.1 3.1 %collective-permute-done.16.refs_1_ = bf16[528,256]{1,0:T(8,128)(2,1)S(1)} collective-permute-done((bf16[528,256]{1,0:T(8,128)(2,1)S(1)}, bf16[528,256]{1,0:T(8,128)(2,1)S(1)}, u32[]{:S(2)}, u32[]{:S(2)}) %collective-permute-start.16) | collective-permute-done | bytes 270368 | tf_op jit(solution)/shard_map/ppermute | solution.py:349
  96.2 0.3 collective-permute-start.20
  96.5 1.8 %collective-permute-start.21 = (bf16[528,256]{1,0:T(8,128)(2,1)S(1)}, bf16[528,256]{1,0:T(8,128)(2,1)S(1)}, u32[]{:S(2)}, u32[]{:S(2)}) collective-permute-start(bf16[528,256]{1,0:T(8,128)(2,1)S(1)} %collective-permute-done.16.refs_1_), channel_id=1, source_target_pairs={{0,16},{8,24},{16,32},{24,40},{32,48},{40,56},{48,0},{56,8},{64,80... | collective-permute-start | bytes 811016 | tf_op jit(solution)/shard_map/ppermute | solution.py:351
  98.3 1.5 collective-permute-done.19.refs_4_
  99.8 2.2 %collective-permute-start.22 = (bf16[528,256]{1,0:T(8,128)(2,1)S(1)}, bf16[528,256]{1,0:T(8,128)(2,1)S(1)}, u32[]{:S(2)}, u32[]{:S(2)}) collective-permute-start(bf16[528,256]{1,0:T(8,128)(2,1)S(1)} %collective-permute-done.19.refs_4_), channel_id=1, source_target_pairs={{0,64},{8,72},{16,80},{24,88},{32,96},{40,104},{48,112},{56,120},{... | collective-permute-start | bytes 811016 | tf_op jit(solution)/shard_map/ppermute | solution.py:352
  102.0 6.2 %shard_map.102 = (bf16[16,16,2,32,256]{4,3,2,1,0:T(8,128)(2,1)S(1)}, bf16[16,16,2,32,256]{4,3,2,1,0:T(8,128)(2,1)S(1)}) custom-call(bf16[16,16,2,32,256]{4,3,2,1,0:T(8,128)(2,1)} %w_ref.1, bf16[16,16,2,32,256]{4,3,2,1,0:T(8,128)(2,1)} %u_ref.2), custom_call_target="tpu_custom_call" | custom-call | bytes 33554432 | tf_op jit(solution)/shard_map/pallas_call | solution.py:366
  108.2 0.7 collective-permute-done.21.refs_6_
  108.9 3.2 %collective-permute-done.22.refs_7_ = bf16[528,256]{1,0:T(8,128)(2,1)S(1)} collective-permute-done((bf16[528,256]{1,0:T(8,128)(2,1)S(1)}, bf16[528,256]{1,0:T(8,128)(2,1)S(1)}, u32[]{:S(2)}, u32[]{:S(2)}) %collective-permute-start.22) | collective-permute-done | bytes 270368 | tf_op jit(solution)/shard_map/ppermute | solution.py:352
  112.1 0.3 shard_map.103.refs_0_
  112.4 0.1 collective-permute-start.23
  112.5 3.5 %shard_map.104 = (bf16[16,8,64,256]{3,2,1,0:T(8,128)(2,1)S(1)}, f32[16,256]{1,0:T(8,128)S(1)}) custom-call(s32[16]{0:T(128)S(1)} %stack.94.order_ref, s32[32,16]{1,0:T(8,128)S(1)} %bitcast.49, bf16[16,16,2,32,256]{4,3,2,1,0:T(8,128)(2,1)S(1)} %get-tuple-element.85.refs_8_.w_ref, bf16[8,528,256]{2,1,0:T(8,128)(2,1)S(1)} %shard_map.103.refs_0_), custom_call_target="tpu_custom_call" | custom-call | flops 1073741824 | bytes 16777216 | tf_op jit(solution)/shard_map/pallas_call | solution.py:381
  116.0 0.7 collective-permute-done.23.refs_0_
  116.7 6.3 %shard_map.105 = (bf16[4,256,256]{2,1,0:T(8,128)(2,1)S(1)}, bf16[4,256,256]{2,1,0:T(8,128)(2,1)S(1)}, bf16[528,256]{1,0:T(8,128)(2,1)S(1)}, bf16[528,256]{1,0:T(...) custom-call(s32[16]{0:T(128)S(1)} %stack.94.order_ref, s32[32,16]{1,0:T(8,128)S(1)} %bitcast.50, ...), custom_call_target="tpu_custom_call" | custom-call | flops 3221225472 | bytes 20971520 | tf_op jit(solution)/shard_map/pallas_call | solution.py:394
  123.0 1.0 collective-permute-start.24
  124.0 5.9 %collective-permute-start.26 = (bf16[528,256]{1,0:T(8,128)(2,1)S(1)}, bf16[528,256]{1,0:T(8,128)(2,1)S(1)}, u32[]{:S(2)}, u32[]{:S(2)}) collective-permute-start(bf16[528,256]{1,0:T(8,128)(2,1)S(1)} %get-tuple-element.94), channel_id=1, source_target_pairs={{0,2},{1,3},{2,0},{3,1},{4,6},{5,7},{6,4},{7,5},{8,10},{9,11},{10,... | collective-permute-start | bytes 811016 | tf_op jit(solution)/shard_map/ppermute | solution.py:431
  129.9 5.0 %collective-permute-done.25.a1_ref = bf16[528,256]{1,0:T(8,128)(2,1)S(1)} collective-permute-done((bf16[528,256]{1,0:T(8,128)(2,1)S(1)}, bf16[528,256]{1,0:T(8,128)(2,1)S(1)}, u32[]{:S(2)}, u32[]{:S(2)}) %collective-permute-start.25) | collective-permute-done | bytes 270368 | tf_op jit(solution)/shard_map/ppermute | solution.py:431
  135.0 7.0 %collective-permute-done.26.a2_ref = bf16[528,256]{1,0:T(8,128)(2,1)S(1)} collective-permute-done((bf16[528,256]{1,0:T(8,128)(2,1)S(1)}, bf16[528,256]{1,0:T(8,128)(2,1)S(1)}, u32[]{:S(2)}, u32[]{:S(2)}) %collective-permute-start.26) | collective-permute-done | bytes 270368 | tf_op jit(solution)/shard_map/ppermute | solution.py:431
  141.9 0.9 shard_map.106
  142.9 1.2 collective-permute-start.31
  144.1 3.5 %collective-permute-start.29 = (bf16[256,256]{1,0:T(8,128)(2,1)}, bf16[256,256]{1,0:T(8,128)(2,1)S(1)}, u32[]{:S(2)}, u32[]{:S(2)}) collective-permute-start(bf16[256,256]{1,0:T(8,128)(2,1)} %get-tuple-element.98), channel_id=1, source_target_pairs={{0,2},{1,3},{2,0},{3,1},{4,6},{5,7},{6,4},{7,5},{8,10},{9,11},{10,... | collective-permute-start | bytes 393224 | tf_op jit(solution)/shard_map/ppermute | solution.py:448
  147.7 1.6 copy-done.7
  149.2 3.4 %shard_map.107.refs_7_ = f32[2,256,256]{2,1,0:T(8,128)S(1)} custom-call(s32[2,8]{1,0:T(2,128)S(1)} %bitcast.52, s32[2]{0:T(128)S(1)} %dynamic-slice_bitcast_fusion.count_ref, bf16[2,8,256,256]{3,2,1,0:T(8,128)(2,1)S(1)} %bitcast.41, bf16[16,256,256]{2,1,0:T(8,128)(2,1)S(1)} %copy-done.7), custom_call_target="tpu_custom_call" | custom-call | flops 536870912 | bytes 5242880 | tf_op jit(solution)/shard_map/pallas_call | solution.py:410
  152.7 1.1 collective-permute-done.29.refs_2_
  153.8 1.0 shard_map.108
  (53 shorter events, 0.4 us)
Async XLA Ops:
  7.2 68.2 %all-gather.6.cloned.1.call-start = ((), (), s32[]{:S(2)}) async-start(), calls=%async_computation.1 | async-start | bytes 2359296 | tf_op jit(solution)/shard_map/all_gather | solution.py:425
  9.2 10.6 %collective-permute-start = (bf16[528,256]{1,0:T(8,128)(2,1)}, bf16[528,256]{1,0:T(8,128)(2,1)S(1)}, u32[]{:S(2)}, u32[]{:S(2)}) collective-permute-start(bf16[528,256]{1,0:T(8,128)(2,1)} %shard_map.95.refs_0_), channel_id=1, source_target_pairs={{0,64},{8,72},{16,80},{24,88},{32,96},{40,104},{48,112},{56,120},{... | collective-permute-start | bytes 811016 | tf_op jit(solution)/shard_map/ppermute | solution.py:349
  12.3 29.0 %collective-permute-start.1 = (bf16[528,256]{1,0:T(8,128)(2,1)}, bf16[528,256]{1,0:T(8,128)(2,1)S(1)}, u32[]{:S(2)}, u32[]{:S(2)}) collective-permute-start(bf16[528,256]{1,0:T(8,128)(2,1)} %shard_map.95.refs_0_), channel_id=1, source_target_pairs={{0,48},{8,56},{16,0},{24,8},{32,16},{40,24},{48,32},{56,40},{64,11... | collective-permute-start | bytes 811016 | tf_op jit(solution)/shard_map/ppermute | solution.py:350
  16.3 25.0 %collective-permute-start.2 = (bf16[528,256]{1,0:T(8,128)(2,1)}, bf16[528,256]{1,0:T(8,128)(2,1)S(1)}, u32[]{:S(2)}, u32[]{:S(2)}) collective-permute-start(bf16[528,256]{1,0:T(8,128)(2,1)} %shard_map.95.refs_0_), channel_id=1, source_target_pairs={{0,16},{8,24},{16,32},{24,40},{32,48},{40,56},{48,0},{56,8},{64,80... | collective-permute-start | bytes 811016 | tf_op jit(solution)/shard_map/ppermute | solution.py:350
  16.3 15.3 %collective-permute-start.3 = (bf16[528,256]{1,0:T(8,128)(2,1)}, bf16[528,256]{1,0:T(8,128)(2,1)S(1)}, u32[]{:S(2)}, u32[]{:S(2)}) collective-permute-start(bf16[528,256]{1,0:T(8,128)(2,1)} %shard_map.95.refs_0_), channel_id=1, source_target_pairs={{0,32},{8,40},{16,48},{24,56},{32,0},{40,8},{48,16},{56,24},{64,96... | collective-permute-start | bytes 811016 | tf_op jit(solution)/shard_map/ppermute | solution.py:350
  18.2 124.6 %all-gather.4.cloned.1.call-start = ((), (), s32[]{:S(2)}) async-start(), calls=%async_computation | async-start | bytes 2359296 | tf_op jit(solution)/shard_map/all_gather | solution.py:425
  19.8 21.5 %collective-permute-start.4 = (bf16[528,256]{1,0:T(8,128)(2,1)S(1)}, bf16[528,256]{1,0:T(8,128)(2,1)S(1)}, u32[]{:S(2)}, u32[]{:S(2)}) collective-permute-start(bf16[528,256]{1,0:T(8,128)(2,1)S(1)} %collective-permute-done.refs_1_), channel_id=1, source_target_pairs={{0,48},{8,56},{16,0},{24,8},{32,16},{40,24},{48,32},{56,40},{64,11... | collective-permute-start | bytes 811016 | tf_op jit(solution)/shard_map/ppermute | solution.py:351
  23.3 18.1 %collective-permute-start.5 = (bf16[528,256]{1,0:T(8,128)(2,1)S(1)}, bf16[528,256]{1,0:T(8,128)(2,1)S(1)}, u32[]{:S(2)}, u32[]{:S(2)}) collective-permute-start(bf16[528,256]{1,0:T(8,128)(2,1)S(1)} %collective-permute-done.refs_1_), channel_id=1, source_target_pairs={{0,16},{8,24},{16,32},{24,40},{32,48},{40,56},{48,0},{56,8},{64,80... | collective-permute-start | bytes 811016 | tf_op jit(solution)/shard_map/ppermute | solution.py:351
  31.6 13.5 %collective-permute-start.6 = (bf16[528,256]{1,0:T(8,128)(2,1)S(1)}, bf16[528,256]{1,0:T(8,128)(2,1)S(1)}, u32[]{:S(2)}, u32[]{:S(2)}) collective-permute-start(bf16[528,256]{1,0:T(8,128)(2,1)S(1)} %collective-permute-done.3.refs_4_), channel_id=1, source_target_pairs={{0,64},{8,72},{16,80},{24,88},{32,96},{40,104},{48,112},{56,120},{... | collective-permute-start | bytes 811016 | tf_op jit(solution)/shard_map/ppermute | solution.py:352
  35.1 10.0 %copy-start.8 = (bf16[528,256]{1,0:T(8,128)(2,1)S(1)}, bf16[528,256]{1,0:T(8,128)(2,1)}, u32[]{:S(2)}) copy-start(bf16[528,256]{1,0:T(8,128)(2,1)} %shard_map.95.refs_0_) | copy-start | bytes 811012
  41.3 4.2 %copy-start.3 = (bf16[16,16,2,32,256]{4,3,2,1,0:T(8,128)(2,1)}, bf16[16,16,2,32,256]{4,3,2,1,0:T(8,128)(2,1)S(1)}, u32[]{:S(2)}) copy-start(bf16[16,16,2,32,256]{4,3,2,1,0:T(8,128)(2,1)S(1)} %get-tuple-element.62.u_ref) | copy-start | bytes 25165828
  45.5 4.3 %collective-permute-start.7 = (bf16[8,528,256]{2,1,0:T(8,128)(2,1)S(1)}, bf16[8,528,256]{2,1,0:T(8,128)(2,1)S(1)}, u32[]{:S(2)}, u32[]{:S(2)}) collective-permute-start(bf16[8,528,256]{2,1,0:T(8,128)(2,1)S(1)} %shard_map.96.refs_0_), channel_id=1, source_target_pairs={{0,8},{8,0},{16,24},{24,16},{32,40},{40,32},{48,56},{56,48},{64,72... | collective-permute-start | bytes 6488072 | tf_op jit(solution)/shard_map/ppermute | solution.py:354
  45.5 4.2 %copy-start.4 = (bf16[16,16,2,32,256]{4,3,2,1,0:T(8,128)(2,1)S(1)}, bf16[16,16,2,32,256]{4,3,2,1,0:T(8,128)(2,1)}, u32[]{:S(2)}) copy-start(bf16[16,16,2,32,256]{4,3,2,1,0:T(8,128)(2,1)} %copy-done.3) | copy-start | bytes 25165828
  49.8 30.4 %copy-start = (bf16[1,2,8,256,256]{4,3,2,1,0:T(8,128)(2,1)S(1)}, bf16[1,2,8,256,256]{4,3,2,1,0:T(8,128)(2,1)}, u32[]{:S(2)}) copy-start(bf16[1,2,8,256,256]{4,3,2,1,0:T(8,128)(2,1)} %param.11) | copy-start | bytes 6291460
  56.1 30.3 %copy-start.5 = (bf16[1,2,256,256]{3,2,1,0:T(8,128)(2,1)S(1)}, bf16[1,2,256,256]{3,2,1,0:T(8,128)(2,1)}, u32[]{:S(2)}) copy-start(bf16[1,2,256,256]{3,2,1,0:T(8,128)(2,1)} %param.7) | copy-start | bytes 786436
  56.1 18.4 %collective-permute-start.8 = (bf16[4,256,256]{2,1,0:T(8,128)(2,1)S(1)}, bf16[4,256,256]{2,1,0:T(8,128)(2,1)S(1)}, u32[]{:S(2)}, u32[]{:S(2)}) collective-permute-start(bf16[4,256,256]{2,1,0:T(8,128)(2,1)S(1)} %get-tuple-element.66), channel_id=1, source_target_pairs={{0,4},{1,5},{2,6},{3,7},{4,0},{5,1},{6,2},{7,3},{8,12},{9,13},{10,... | collective-permute-start | bytes 1572872 | tf_op jit(solution)/shard_map/ppermute | solution.py:430
  57.0 10.4 %collective-permute-start.9 = (bf16[528,256]{1,0:T(8,128)(2,1)S(1)}, bf16[528,256]{1,0:T(8,128)(2,1)S(1)}, u32[]{:S(2)}, u32[]{:S(2)}) collective-permute-start(bf16[528,256]{1,0:T(8,128)(2,1)S(1)} %get-tuple-element.68), channel_id=1, source_target_pairs={{0,1},{1,2},{2,3},{3,0},{4,5},{5,6},{6,7},{7,4},{8,9},{9,10},{10,1... | collective-permute-start | bytes 811016 | tf_op jit(solution)/shard_map/ppermute | solution.py:431
  58.3 16.1 %collective-permute-start.10 = (bf16[528,256]{1,0:T(8,128)(2,1)S(1)}, bf16[528,256]{1,0:T(8,128)(2,1)S(1)}, u32[]{:S(2)}, u32[]{:S(2)}) collective-permute-start(bf16[528,256]{1,0:T(8,128)(2,1)S(1)} %get-tuple-element.69), channel_id=1, source_target_pairs={{0,2},{1,3},{2,0},{3,1},{4,6},{5,7},{6,4},{7,5},{8,10},{9,11},{10,... | collective-permute-start | bytes 811016 | tf_op jit(solution)/shard_map/ppermute | solution.py:431
  62.4 12.0 %collective-permute-start.11 = (bf16[528,256]{1,0:T(8,128)(2,1)S(1)}, bf16[528,256]{1,0:T(8,128)(2,1)S(1)}, u32[]{:S(2)}, u32[]{:S(2)}) collective-permute-start(bf16[528,256]{1,0:T(8,128)(2,1)S(1)} %get-tuple-element.70), channel_id=1, source_target_pairs={{0,3},{1,0},{2,1},{3,2},{4,7},{5,4},{6,5},{7,6},{8,11},{9,8},{10,9... | collective-permute-start | bytes 811016 | tf_op jit(solution)/shard_map/ppermute | solution.py:431
  75.3 11.0 %collective-permute-start.15 = (bf16[272,256]{1,0:T(8,128)(2,1)}, bf16[272,256]{1,0:T(8,128)(2,1)S(1)}, u32[]{:S(2)}, u32[]{:S(2)}) collective-permute-start(bf16[272,256]{1,0:T(8,128)(2,1)} %get-tuple-element.77), channel_id=1, source_target_pairs={{0,4},{1,5},{2,6},{3,7},{4,0},{5,1},{6,2},{7,3},{8,12},{9,13},{10,... | collective-permute-start | bytes 417800 | tf_op jit(solution)/shard_map/ppermute | solution.py:449
  76.6 8.6 %collective-permute-start.12 = (bf16[256,256]{1,0:T(8,128)(2,1)}, bf16[256,256]{1,0:T(8,128)(2,1)S(1)}, u32[]{:S(2)}, u32[]{:S(2)}) collective-permute-start(bf16[256,256]{1,0:T(8,128)(2,1)} %get-tuple-element.72), channel_id=1, source_target_pairs={{0,1},{1,2},{2,3},{3,0},{4,5},{5,6},{6,7},{7,4},{8,9},{9,10},{10,1... | collective-permute-start | bytes 393224 | tf_op jit(solution)/shard_map/ppermute | solution.py:448
  76.6 9.7 %collective-permute-start.13 = (bf16[256,256]{1,0:T(8,128)(2,1)}, bf16[256,256]{1,0:T(8,128)(2,1)S(1)}, u32[]{:S(2)}, u32[]{:S(2)}) collective-permute-start(bf16[256,256]{1,0:T(8,128)(2,1)} %get-tuple-element.73), channel_id=1, source_target_pairs={{0,2},{1,3},{2,0},{3,1},{4,6},{5,7},{6,4},{7,5},{8,10},{9,11},{10,... | collective-permute-start | bytes 393224 | tf_op jit(solution)/shard_map/ppermute | solution.py:448
  80.1 6.2 %collective-permute-start.14 = (bf16[256,256]{1,0:T(8,128)(2,1)}, bf16[256,256]{1,0:T(8,128)(2,1)S(1)}, u32[]{:S(2)}, u32[]{:S(2)}) collective-permute-start(bf16[256,256]{1,0:T(8,128)(2,1)} %get-tuple-element.74), channel_id=1, source_target_pairs={{0,3},{1,0},{2,1},{3,2},{4,7},{5,4},{6,5},{7,6},{8,11},{9,8},{10,9... | collective-permute-start | bytes 393224 | tf_op jit(solution)/shard_map/ppermute | solution.py:448
  80.1 1.6 copy-start.6
  87.5 8.8 %collective-permute-start.16 = (bf16[528,256]{1,0:T(8,128)(2,1)S(1)}, bf16[528,256]{1,0:T(8,128)(2,1)S(1)}, u32[]{:S(2)}, u32[]{:S(2)}) collective-permute-start(bf16[528,256]{1,0:T(8,128)(2,1)S(1)} %get-tuple-element.87.refs_0_), channel_id=1, source_target_pairs={{0,64},{8,72},{16,80},{24,88},{32,96},{40,104},{48,112},{56,120},{... | collective-permute-start | bytes 811016 | tf_op jit(solution)/shard_map/ppermute | solution.py:349
  88.9 10.9 %collective-permute-start.19 = (bf16[528,256]{1,0:T(8,128)(2,1)S(1)}, bf16[528,256]{1,0:T(8,128)(2,1)S(1)}, u32[]{:S(2)}, u32[]{:S(2)}) collective-permute-start(bf16[528,256]{1,0:T(8,128)(2,1)S(1)} %get-tuple-element.87.refs_0_), channel_id=1, source_target_pairs={{0,32},{8,40},{16,48},{24,56},{32,0},{40,8},{48,16},{56,24},{64,96... | collective-permute-start | bytes 811016 | tf_op jit(solution)/shard_map/ppermute | solution.py:350
  91.1 17.1 %collective-permute-start.17 = (bf16[528,256]{1,0:T(8,128)(2,1)S(1)}, bf16[528,256]{1,0:T(8,128)(2,1)S(1)}, u32[]{:S(2)}, u32[]{:S(2)}) collective-permute-start(bf16[528,256]{1,0:T(8,128)(2,1)S(1)} %get-tuple-element.87.refs_0_), channel_id=1, source_target_pairs={{0,48},{8,56},{16,0},{24,8},{32,16},{40,24},{48,32},{56,40},{64,11... | collective-permute-start | bytes 811016 | tf_op jit(solution)/shard_map/ppermute | solution.py:350
  91.5 16.7 %collective-permute-start.18 = (bf16[528,256]{1,0:T(8,128)(2,1)S(1)}, bf16[528,256]{1,0:T(8,128)(2,1)S(1)}, u32[]{:S(2)}, u32[]{:S(2)}) collective-permute-start(bf16[528,256]{1,0:T(8,128)(2,1)S(1)} %get-tuple-element.87.refs_0_), channel_id=1, source_target_pairs={{0,16},{8,24},{16,32},{24,40},{32,48},{40,56},{48,0},{56,8},{64,80... | collective-permute-start | bytes 811016 | tf_op jit(solution)/shard_map/ppermute | solution.py:350
  96.2 12.0 %collective-permute-start.20 = (bf16[528,256]{1,0:T(8,128)(2,1)S(1)}, bf16[528,256]{1,0:T(8,128)(2,1)S(1)}, u32[]{:S(2)}, u32[]{:S(2)}) collective-permute-start(bf16[528,256]{1,0:T(8,128)(2,1)S(1)} %collective-permute-done.16.refs_1_), channel_id=1, source_target_pairs={{0,48},{8,56},{16,0},{24,8},{32,16},{40,24},{48,32},{56,40},{64,11... | collective-permute-start | bytes 811016 | tf_op jit(solution)/shard_map/ppermute | solution.py:351
  96.5 12.4 %collective-permute-start.21 = (bf16[528,256]{1,0:T(8,128)(2,1)S(1)}, bf16[528,256]{1,0:T(8,128)(2,1)S(1)}, u32[]{:S(2)}, u32[]{:S(2)}) collective-permute-start(bf16[528,256]{1,0:T(8,128)(2,1)S(1)} %collective-permute-done.16.refs_1_), channel_id=1, source_target_pairs={{0,16},{8,24},{16,32},{24,40},{32,48},{40,56},{48,0},{56,8},{64,80... | collective-permute-start | bytes 811016 | tf_op jit(solution)/shard_map/ppermute | solution.py:351
  99.8 12.3 %collective-permute-start.22 = (bf16[528,256]{1,0:T(8,128)(2,1)S(1)}, bf16[528,256]{1,0:T(8,128)(2,1)S(1)}, u32[]{:S(2)}, u32[]{:S(2)}) collective-permute-start(bf16[528,256]{1,0:T(8,128)(2,1)S(1)} %collective-permute-done.19.refs_4_), channel_id=1, source_target_pairs={{0,64},{8,72},{16,80},{24,88},{32,96},{40,104},{48,112},{56,120},{... | collective-permute-start | bytes 811016 | tf_op jit(solution)/shard_map/ppermute | solution.py:352
  108.2 4.2 %copy-start.1 = (bf16[16,16,2,32,256]{4,3,2,1,0:T(8,128)(2,1)}, bf16[16,16,2,32,256]{4,3,2,1,0:T(8,128)(2,1)S(1)}, u32[]{:S(2)}) copy-start(bf16[16,16,2,32,256]{4,3,2,1,0:T(8,128)(2,1)S(1)} %get-tuple-element.86.u_ref) | copy-start | bytes 25165828
  112.4 4.3 %collective-permute-start.23 = (bf16[8,528,256]{2,1,0:T(8,128)(2,1)S(1)}, bf16[8,528,256]{2,1,0:T(8,128)(2,1)S(1)}, u32[]{:S(2)}, u32[]{:S(2)}) collective-permute-start(bf16[8,528,256]{2,1,0:T(8,128)(2,1)S(1)} %shard_map.103.refs_0_), channel_id=1, source_target_pairs={{0,8},{8,0},{16,24},{24,16},{32,40},{40,32},{48,56},{56,48},{64,72... | collective-permute-start | bytes 6488072 | tf_op jit(solution)/shard_map/ppermute | solution.py:354
  112.5 4.2 %copy-start.2 = (bf16[16,16,2,32,256]{4,3,2,1,0:T(8,128)(2,1)S(1)}, bf16[16,16,2,32,256]{4,3,2,1,0:T(8,128)(2,1)}, u32[]{:S(2)}) copy-start(bf16[16,16,2,32,256]{4,3,2,1,0:T(8,128)(2,1)} %copy-done.1) | copy-start | bytes 25165828
  123.0 30.8 %copy-start.9 = (f32[2,256,256]{2,1,0:T(8,128)S(1)}, f32[2,256,256]{2,1,0:T(8,128)}, u32[]{:S(2)}) copy-start(f32[2,256,256]{2,1,0:T(8,128)} %get-tuple-element.106.refs_9_) | copy-start | bytes 1572868
  123.0 18.9 %collective-permute-start.24 = (bf16[4,256,256]{2,1,0:T(8,128)(2,1)S(1)}, bf16[4,256,256]{2,1,0:T(8,128)(2,1)S(1)}, u32[]{:S(2)}, u32[]{:S(2)}) collective-permute-start(bf16[4,256,256]{2,1,0:T(8,128)(2,1)S(1)} %get-tuple-element.91), channel_id=1, source_target_pairs={{0,4},{1,5},{2,6},{3,7},{4,0},{5,1},{6,2},{7,3},{8,12},{9,13},{10,... | collective-permute-start | bytes 1572872 | tf_op jit(solution)/shard_map/ppermute | solution.py:430
  124.0 11.0 %collective-permute-start.25 = (bf16[528,256]{1,0:T(8,128)(2,1)S(1)}, bf16[528,256]{1,0:T(8,128)(2,1)S(1)}, u32[]{:S(2)}, u32[]{:S(2)}) collective-permute-start(bf16[528,256]{1,0:T(8,128)(2,1)S(1)} %get-tuple-element.93), channel_id=1, source_target_pairs={{0,1},{1,2},{2,3},{3,0},{4,5},{5,6},{6,7},{7,4},{8,9},{9,10},{10,1... | collective-permute-start | bytes 811016 | tf_op jit(solution)/shard_map/ppermute | solution.py:431
  124.0 17.9 %collective-permute-start.26 = (bf16[528,256]{1,0:T(8,128)(2,1)S(1)}, bf16[528,256]{1,0:T(8,128)(2,1)S(1)}, u32[]{:S(2)}, u32[]{:S(2)}) collective-permute-start(bf16[528,256]{1,0:T(8,128)(2,1)S(1)} %get-tuple-element.94), channel_id=1, source_target_pairs={{0,2},{1,3},{2,0},{3,1},{4,6},{5,7},{6,4},{7,5},{8,10},{9,11},{10,... | collective-permute-start | bytes 811016 | tf_op jit(solution)/shard_map/ppermute | solution.py:431
  129.9 12.0 %collective-permute-start.27 = (bf16[528,256]{1,0:T(8,128)(2,1)S(1)}, bf16[528,256]{1,0:T(8,128)(2,1)S(1)}, u32[]{:S(2)}, u32[]{:S(2)}) collective-permute-start(bf16[528,256]{1,0:T(8,128)(2,1)S(1)} %get-tuple-element.95), channel_id=1, source_target_pairs={{0,3},{1,0},{2,1},{3,2},{4,7},{5,4},{6,5},{7,6},{8,11},{9,8},{10,9... | collective-permute-start | bytes 811016 | tf_op jit(solution)/shard_map/ppermute | solution.py:431
  142.9 11.0 %collective-permute-start.31 = (bf16[272,256]{1,0:T(8,128)(2,1)}, bf16[272,256]{1,0:T(8,128)(2,1)S(1)}, u32[]{:S(2)}, u32[]{:S(2)}) collective-permute-start(bf16[272,256]{1,0:T(8,128)(2,1)} %get-tuple-element.103), channel_id=1, source_target_pairs={{0,4},{1,5},{2,6},{3,7},{4,0},{5,1},{6,2},{7,3},{8,12},{9,13},{10,... | collective-permute-start | bytes 417800 | tf_op jit(solution)/shard_map/ppermute | solution.py:449
  144.1 8.5 %collective-permute-start.28 = (bf16[256,256]{1,0:T(8,128)(2,1)}, bf16[256,256]{1,0:T(8,128)(2,1)S(1)}, u32[]{:S(2)}, u32[]{:S(2)}) collective-permute-start(bf16[256,256]{1,0:T(8,128)(2,1)} %get-tuple-element.97), channel_id=1, source_target_pairs={{0,1},{1,2},{2,3},{3,0},{4,5},{5,6},{6,7},{7,4},{8,9},{9,10},{10,1... | collective-permute-start | bytes 393224 | tf_op jit(solution)/shard_map/ppermute | solution.py:448
  144.1 9.7 %collective-permute-start.29 = (bf16[256,256]{1,0:T(8,128)(2,1)}, bf16[256,256]{1,0:T(8,128)(2,1)S(1)}, u32[]{:S(2)}, u32[]{:S(2)}) collective-permute-start(bf16[256,256]{1,0:T(8,128)(2,1)} %get-tuple-element.98), channel_id=1, source_target_pairs={{0,2},{1,3},{2,0},{3,1},{4,6},{5,7},{6,4},{7,5},{8,10},{9,11},{10,... | collective-permute-start | bytes 393224 | tf_op jit(solution)/shard_map/ppermute | solution.py:448
  147.6 6.2 %collective-permute-start.30 = (bf16[256,256]{1,0:T(8,128)(2,1)}, bf16[256,256]{1,0:T(8,128)(2,1)S(1)}, u32[]{:S(2)}, u32[]{:S(2)}) collective-permute-start(bf16[256,256]{1,0:T(8,128)(2,1)} %get-tuple-element.99), channel_id=1, source_target_pairs={{0,3},{1,0},{2,1},{3,2},{4,7},{5,4},{6,5},{7,6},{8,11},{9,8},{10,9... | collective-permute-start | bytes 393224 | tf_op jit(solution)/shard_map/ppermute | solution.py:448
  147.7 1.6 copy-start.7
Sparse Core Ops, SparseCore 0:
  18.4 40.4 all-gather.5
  87.6 39.4 all-gather.3

commit v4 on v3

--- a/solution.py
+++ b/solution.py
@@ -75,9 +75,9 @@
 
 
 class Coder:
-    def __init__(self, first, order_ref, rank_ref, w_ref, fields, field_buf, field_sem):
+    def __init__(self, first, order_ref, rank_ref, w_ref, fields, field_buf, field_sem, near=None):
         self.first, self.order_ref, self.rank_ref = first, order_ref, rank_ref
-        self.w_ref, self.field_buf = w_ref, field_buf
+        self.w_ref, self.field_buf, self.near = w_ref, field_buf, near
         parts = [field.at[n] for field in fields for n in range(field.shape[0])]
         self.copies = [
             pltpu.make_async_copy(part, field_buf.at[slot], field_sem.at[slot])
@@ -102,27 +102,39 @@
                 field = self.field_buf[slot, p * size : (p + 1) * size, :]
                 value = jnp.dot(w, field, preferred_element_type=jnp.float32)
                 for i in range(targets):
-                    live = self.rank_ref[panel * per_dev + p, i]
+                    live = self.rank_ref[i, p, panel]
+                    if slot == 0 and self.near is not None:
+                        live = jnp.where(self.near(p, i), 0, live)
                     part = value[i * rank : (i + 1) * rank]
                     part = jnp.where(row < live, part, 0.0).astype(jnp.bfloat16)
                     coded_ref[i, place, p * rank : (p + 1) * rank, :] = part
 
 
-def code_kernel(order_ref, rank_ref, w_ref, *refs):
+def code_kernel(order_ref, rank_ref, cols_ref, count_ref, w_ref, *refs):
     fields, (coded_ref, sums_ref, field_buf, field_sem) = refs[:-4], refs[-4:]
-    coder = Coder(0, order_ref, rank_ref, w_ref, fields, field_buf, field_sem)
+    slots = cols_ref.shape[0]
+    per_dev = w_ref.shape[2]
+
+    def near(p, i):
+        mine = order_ref[order_ref.shape[0] - 1] * per_dev + p
+        hit = cols_ref[0, i] == mine
+        for k in range(1, slots):
+            hit = hit | ((cols_ref[k, i] == mine) & (k < count_ref[i]))
+        return hit
+
+    coder = Coder(0, order_ref, rank_ref, w_ref, fields, field_buf, field_sem, near)
     coder.load()
     sums_ref[...] = jnp.zeros_like(sums_ref)
     coder.run(coded_ref, sums_ref, False)
 
 
-def far_kernel(order_ref, rank_ref, target_ref, w_ref, u_ref, early_ref, early_sums_ref, *refs):
+def far_kernel(order_ref, rank_ref, w_ref, u_ref, early_ref, early_sums_ref, *refs):
     fields, refs = refs[:-11], refs[-11:]
     cross_ref, stay_ref, around_refs, near_ref = refs[0], refs[1], refs[2:5], refs[5]
     field_buf, coded_ref, sums_ref, field_sem, early_sem = refs[6:]
     turns = cross_ref.shape[0]
     width = cross_ref.shape[2]
-    _, _, per_dev, _, size = u_ref.shape
+    _, panels, per_dev, _, size = u_ref.shape
     early = early_ref.shape[1]
 
     def early_copy(slot):
@@ -151,7 +163,7 @@
     for turn in range(turns):
         around_ref = near_ref if turn == 0 else around_refs[turn - 1]
         for side, first_ref in ((1, cross_ref), (0, stay_ref)):
-            target = target_ref[side * turns + turn] * per_dev
+            target = order_ref[panels + side * turns + turn] * per_dev
             first_ref[turn] = expand(target)
             around_ref[side * size : (side + 1) * size, :] = expand(target + 1)
         around_ref[2 * size :, :] = extra
@@ -179,7 +191,9 @@
     sums_ref[0:1, :], sums_ref[1:2, :] = sums
 
 
-def near_kernel(cols_ref, count_ref, tiles_ref, panel_ref, out_ref, panel_buf, tile_buf, sems):
+def near_kernel(
+    order_ref, cols_ref, count_ref, tiles_ref, panel_ref, out_ref, panel_buf, tile_buf, sems
+):
     per_dev = out_ref.shape[0]
     copies = [pltpu.make_async_copy(panel_ref, panel_buf, sems.at[per_dev])]
     copies += [
@@ -190,13 +204,14 @@
     for copy in copies:
         copy.wait()
     for p in range(per_dev):
+        block = order_ref[order_ref.shape[0] - 1] * per_dev + p
         out_ref[p] = jnp.zeros(out_ref.shape[1:], jnp.float32)
         for k in range(tile_buf.shape[1]):
 
-            @pl.when(k < count_ref[p])
+            @pl.when(k < count_ref[block])
             def _():
                 out_ref[p] += jnp.dot(
-                    tile_buf[p, k], panel_buf[cols_ref[p, k]], preferred_element_type=jnp.float32
+                    tile_buf[p, k], panel_buf[cols_ref[k, block]], preferred_element_type=jnp.float32
                 )
 
 
@@ -283,14 +298,8 @@
 
     x = rhs_block[0]
     tiles = near_tiles[0]
-    slot_live = jnp.arange(slots, dtype=i32)[None, :] < near_count[0][:, None]
-    mine = my_slice * per_dev + jnp.arange(per_dev, dtype=i32)
-    is_near = jnp.any((near_cols[0][:, :, None] == mine) & slot_live[:, :, None], axis=1)
-    same = jnp.arange(panel_count, dtype=i32) == my_panel
-    near_pair = same[:, None, None] & is_near.T[None]
-    ranks = jnp.where(near_pair, 0, far_ranks.transpose(1, 2, 0)).reshape(-1, targets)
-    my_cols = lax.dynamic_slice_in_dim(near_cols[0], my_slice * per_dev, per_dev, 0)
-    my_count = lax.dynamic_slice_in_dim(near_count[0], my_slice * per_dev, per_dev, 0)
+    ranks = far_ranks.transpose(0, 2, 1)
+    cols, count = near_cols[0].T, near_count[0]
 
     hbm = pl.BlockSpec(memory_space=pltpu.HBM)
     smem = pl.BlockSpec(memory_space=pltpu.SMEM)
@@ -307,9 +316,9 @@
     zs = chips // 2
     ys = slice_count // 2
     my_x, my_y = my_slice // ys, my_slice % ys
-    receivers = jnp.stack(
-        [(my_x + side) % 2 * ys + (my_y + turn) % ys for side in range(2) for turn in range(ys)]
-    ).astype(i32)
+    receivers = [
+        (my_x + side) % 2 * ys + (my_y + turn) % ys for side in range(2) for turn in range(ys)
+    ]
     flip_x = [(i, (i + ys) % slice_count) for i in range(slice_count)]
 
     def up_y(turn):
@@ -331,7 +340,7 @@
     far_z = [(at + chips) % panel_count for at in near_z]
     first = near_z[:1] + far_z[:1] + near_z[1:] + far_z[1:]
     order = jnp.stack(
-        [at + core for at in first] + [at + 1 - core for at in first]
+        [at + core for at in first] + [at + 1 - core for at in first] + receivers + [my_slice]
     ).astype(i32)
 
     def pack(blocks, loaded):
@@ -358,8 +367,8 @@
     def coder_scratch(n):
         return [pltpu.VMEM((n, rows, width), bf16)]
 
-    far_w, order, ranks, receivers, my_cols, my_count = lax.optimization_barrier(
-        (far_w, order, ranks, receivers, my_cols, my_count)
+    far_w, order, ranks, cols, count = lax.optimization_barrier(
+        (far_w, order, ranks, cols, count)
     )
 
     def load_factors(far_w, far_u):
@@ -384,17 +393,17 @@
                 pltpu.VMEM((targets, n, per_dev * rank, width), bf16),
                 jax.ShapeDtypeStruct((EXTRA, width), f32),
             ),
-            in_specs=[smem, smem, vmem] + [hbm] * len(early),
+            in_specs=[smem, smem, smem, smem, vmem] + [hbm] * len(early),
             out_specs=(vmem, vmem),
             scratch_shapes=coder_scratch(n) + [sems((n,))],
             compiler_params=params(8),
             cost_estimate=cost(flops * n // panel_count, 16),
-        )(order, ranks, held_w, *early)
+        )(order, ranks, cols, count, held_w, *early)
         around = jax.ShapeDtypeStruct((2 * size + EXTRA, width), bf16)
         return pl.pallas_call(
             far_kernel,
             out_shape=(jax.ShapeDtypeStruct((ys, size, width), bf16),) * 2 + (around,) * ys,
-            in_specs=[smem, smem, smem, vmem, vmem, hbm, vmem] + [hbm] * len(late),
+            in_specs=[smem, smem, vmem, vmem, hbm, vmem] + [hbm] * len(late),
             out_specs=(vmem,) * (2 + ys),
             scratch_shapes=coder_scratch(m)
             + [
@@ -404,13 +413,13 @@
             + [sems((m,)), sems((n,))],
             compiler_params=params(18),
             cost_estimate=cost(flops + flops * m // panel_count, 20),
-        )(order, ranks, receivers, held_w, held_u, coded, sums, *late)
+        )(order, ranks, held_w, held_u, coded, sums, *late)
 
     def near_products(panel):
         return pl.pallas_call(
             near_kernel,
             out_shape=jax.ShapeDtypeStruct((per_dev, size, width), f32),
-            in_specs=[smem, smem, hbm, hbm],
+            in_specs=[smem, smem, smem, hbm, hbm],
             out_specs=vmem,
             scratch_shapes=[
                 pltpu.VMEM((slice_count * per_dev, size, width), bf16),
@@ -419,7 +428,7 @@
             ],
             compiler_params=params(10),
             cost_estimate=cost(2 * per_dev * slots * size * size * width, 5),
-        )(my_cols, my_count, tiles, panel)
+        )(order, cols, count, tiles, panel)
 
     def gather_near(blocks):
         return lax.all_gather(blocks, "near", axis=0, tiled=True)

time: 162 us -> 156 us (0.963)
  waiting for transfers between devices: 48.4 us -> 41.6 us
  starting transfers between devices: 46 us -> 51.1 us
  other arithmetic: 2.24 us -> 0 us
    ppermute x6, waiting for transfers between devices: 9.94 us -> 0.99 us  [gather_panels(): own = [lax.ppermute(payload, 'blk', along_z(turn)) for turn in z_turns[1:]]]
    ppermute x4, waiting for transfers between devices: 0.67 us -> 3.34 us  [gather_panels(): late = [lax.ppermute(far, 'blk', along_z(turn)) for turn in z_turns[1:3]]]
    ppermute x4, starting transfers between devices: 5.44 us -> 7.77 us  [gather_panels(): late = [lax.ppermute(far, 'blk', along_z(turn)) for turn in z_turns[1:3]]]
    unnamed x20 -> x26, local copies, waits for them, and re-layouts: 3.22 us -> 3.51 us
  transfers between devices with their start and end apart: 34 -> 34, of which waited for: 16 -> 18; matrix products, arithmetic and copies ran while one was open for 3% -> 0% of each run, Pallas kernels for 25% -> 28%
where the time goes in v4:
time: 156 us
  starting transfers between devices  51.1 us (33%)
  Pallas kernels  45.5 us (29%)
  waiting for transfers between devices  41.6 us (27%)
  between operations  14.3 us (9%)
  local copies, waits for them, and re-layouts  3.61 us (2%)
    ppermute x12, waiting for transfers between devices, scatter_panel(): lax.ppermute(part, 'near', up_y(turn + 1))  26.5 us
    ppermute x12, starting transfers between devices, scatter_panel(): lax.ppermute(part, 'near', up_y(turn + 1))  18.5 us
    pallas_call x2, Pallas kernels, far_products(): pl.pallas_call(far_kernel, out_shape=(jax.ShapeDtypeStruct((ys, size, wid...  12.6 us
    pallas_call x2, Pallas kernels, load_factors(): pl.pallas_call(load_kernel, out_shape=(pltpu.VMEM(far_w.shape, bf16), plt...  12.3 us
    ppermute x6, starting transfers between devices, gather_panels(): own = [lax.ppermute(payload, 'blk', along_z(turn)) for turn in z_turns[1:]]  10.7 us
    ppermute x4, starting transfers between devices, gather_panels(): late = [lax.ppermute(far, 'blk', along_z(turn)) for turn in z_turns[1:3]]  7.77 us
    pallas_call x2, Pallas kernels, far_products(): pl.pallas_call(code_kernel, out_shape=(pltpu.VMEM((targets, n, per_dev *...  7.42 us
    pallas_call x2, Pallas kernels, near_products(): pl.pallas_call(near_kernel, out_shape=jax.ShapeDtypeStruct((per_dev, size...  6.6 us
  transfers between devices with their start and end apart: 34, of which 18 were waited for; matrix products, arithmetic and copies ran while one was open for 0% of the time, Pallas kernels for 28%

profile of v4, /device:TPU:0, one launch (start us, length us, event | category | flops | bytes accessed | tf_op | source)
XLA Modules:
  0.0 156.1 jit_solution(16484884589541812250)
XLA Ops:
  7.2 0.0 all-gather.6.cloned.1.call-start
  7.2 0.7 all-gather.6.cloned.1.call-update
  7.9 0.0 all-gather.4.cloned.1.call-start
  7.9 2.0 %shard_map.95.refs_0_ = bf16[528,256]{1,0:T(8,128)(2,1)} custom-call(bf16[2,256,256]{2,1,0:T(8,128)(2,1)} %bitcast.40, bf16[2,8,256,256]{3,2,1,0:T(8,128)(2,1)} %bitcast.36), custom_call_target="tpu_custom_call" | custom-call | tf_op jit(solution)/shard_map/pallas_call | solution.py:460
  9.9 3.1 %collective-permute-start = (bf16[528,256]{1,0:T(8,128)(2,1)}, bf16[528,256]{1,0:T(8,128)(2,1)S(1)}, u32[]{:S(2)}, u32[]{:S(2)}) collective-permute-start(bf16[528,256]{1,0:T(8,128)(2,1)} %shard_map.95.refs_0_), channel_id=1, source_target_pairs={{0,64},{8,72},{16,80},{24,88},{32,96},{40,104},{48,112},{56,120},{... | collective-permute-start | bytes 811016 | tf_op jit(solution)/shard_map/ppermute | solution.py:358
  13.0 3.9 %collective-permute-start.3 = (bf16[528,256]{1,0:T(8,128)(2,1)}, bf16[528,256]{1,0:T(8,128)(2,1)S(1)}, u32[]{:S(2)}, u32[]{:S(2)}) collective-permute-start(bf16[528,256]{1,0:T(8,128)(2,1)} %shard_map.95.refs_0_), channel_id=1, source_target_pairs={{0,32},{8,40},{16,48},{24,56},{32,0},{40,8},{48,16},{56,24},{64,96... | collective-permute-start | bytes 811016 | tf_op jit(solution)/shard_map/ppermute | solution.py:359
  16.9 0.7 collective-permute-start.1
  17.6 1.3 collective-permute-start.2
  18.9 0.8 collective-permute-done.refs_1_
  19.7 4.3 %collective-permute-start.4 = (bf16[528,256]{1,0:T(8,128)(2,1)S(1)}, bf16[528,256]{1,0:T(8,128)(2,1)S(1)}, u32[]{:S(2)}, u32[]{:S(2)}) collective-permute-start(bf16[528,256]{1,0:T(8,128)(2,1)S(1)} %collective-permute-done.refs_1_), channel_id=1, source_target_pairs={{0,48},{8,56},{16,0},{24,8},{32,16},{40,24},{48,32},{56,40},{64,11... | collective-permute-start | bytes 811016 | tf_op jit(solution)/shard_map/ppermute | solution.py:360
  24.0 0.5 collective-permute-done.3.refs_4_
  24.5 2.5 %collective-permute-start.6 = (bf16[528,256]{1,0:T(8,128)(2,1)S(1)}, bf16[528,256]{1,0:T(8,128)(2,1)S(1)}, u32[]{:S(2)}, u32[]{:S(2)}) collective-permute-start(bf16[528,256]{1,0:T(8,128)(2,1)S(1)} %collective-permute-done.3.refs_4_), channel_id=1, source_target_pairs={{0,64},{8,72},{16,80},{24,88},{32,96},{40,104},{48,112},{56,120},{... | collective-permute-start | bytes 811016 | tf_op jit(solution)/shard_map/ppermute | solution.py:361
  27.0 0.1 stack.103.order_ref
  27.1 0.0 copy-start.8
  27.1 6.2 %shard_map.94 = (bf16[16,16,2,32,256]{4,3,2,1,0:T(8,128)(2,1)S(1)}, bf16[16,16,2,32,256]{4,3,2,1,0:T(8,128)(2,1)S(1)}) custom-call(bf16[16,16,2,32,256]{4,3,2,1,0:T(8,128)(2,1)} %w_ref.1, bf16[16,16,2,32,256]{4,3,2,1,0:T(8,128)(2,1)} %u_ref.2), custom_call_target="tpu_custom_call" | custom-call | bytes 33554432 | tf_op jit(solution)/shard_map/pallas_call | solution.py:375
  33.4 2.3 %collective-permute-done.4.refs_5_ = bf16[528,256]{1,0:T(8,128)(2,1)S(1)} collective-permute-done((bf16[528,256]{1,0:T(8,128)(2,1)S(1)}, bf16[528,256]{1,0:T(8,128)(2,1)S(1)}, u32[]{:S(2)}, u32[]{:S(2)}) %collective-permute-start.4) | collective-permute-done | bytes 270368 | tf_op jit(solution)/shard_map/ppermute | solution.py:360
  35.7 2.6 %collective-permute-done.6.refs_7_ = bf16[528,256]{1,0:T(8,128)(2,1)S(1)} collective-permute-done((bf16[528,256]{1,0:T(8,128)(2,1)S(1)}, bf16[528,256]{1,0:T(8,128)(2,1)S(1)}, u32[]{:S(2)}, u32[]{:S(2)}) %collective-permute-start.6) | collective-permute-done | bytes 270368 | tf_op jit(solution)/shard_map/ppermute | solution.py:361
  38.3 0.3 shard_map.96.refs_0_
  38.6 0.1 collective-permute-start.7
  38.7 0.3 copy-done.10
  39.0 3.7 %shard_map.97 = (bf16[16,8,64,256]{3,2,1,0:T(8,128)(2,1)S(1)}, f32[16,256]{1,0:T(8,128)S(1)}) custom-call(s32[25]{0:T(128)S(1)} %stack.103.order_ref, s32[16,2,16]{2,1,0:T(2,128)S(1)} %bitcast.44, s32[8,16]{1,0:T(8,128)S(1)} %bitcast.48, s32[16]{0:T(128)S(1)} %bitcast.52, bf16[16,16,2,32,256]{4,3,2,1,0:T(8,128)(2,1)S(1)} %get-tuple-element.59.refs_8_.w_ref, ...), custom_call_target="tpu_custom_call" | custom-call | flops 1073741824 | bytes 16777216 | tf_op jit(solution)/shard_map/pallas_call | solution.py:390
  42.7 0.2 collective-permute-done.7.refs_0_
  43.0 6.3 %shard_map.98 = (bf16[4,256,256]{2,1,0:T(8,128)(2,1)S(1)}, bf16[4,256,256]{2,1,0:T(8,128)(2,1)S(1)}, bf16[528,256]{1,0:T(8,128)(2,1)S(1)}, bf16[528,256]{1,0:T(8...) custom-call(s32[25]{0:T(128)S(1)} %stack.103.order_ref, s32[16,2,16]{2,1,0:T(2,128)S(1)} %bitcast.45, ...), custom_call_target="tpu_custom_call" | custom-call | flops 3221225472 | bytes 20971520 | tf_op jit(solution)/shard_map/pallas_call | solution.py:403
  49.3 2.0 %collective-permute-start.8 = (bf16[4,256,256]{2,1,0:T(8,128)(2,1)S(1)}, bf16[4,256,256]{2,1,0:T(8,128)(2,1)S(1)}, u32[]{:S(2)}, u32[]{:S(2)}) collective-permute-start(bf16[4,256,256]{2,1,0:T(8,128)(2,1)S(1)} %get-tuple-element.66), channel_id=1, source_target_pairs={{0,4},{1,5},{2,6},{3,7},{4,0},{5,1},{6,2},{7,3},{8,12},{9,13},{10,... | collective-permute-start | bytes 1572872 | tf_op jit(solution)/shard_map/ppermute | solution.py:439
  51.3 5.2 %collective-permute-start.10 = (bf16[528,256]{1,0:T(8,128)(2,1)S(1)}, bf16[528,256]{1,0:T(8,128)(2,1)S(1)}, u32[]{:S(2)}, u32[]{:S(2)}) collective-permute-start(bf16[528,256]{1,0:T(8,128)(2,1)S(1)} %get-tuple-element.69), channel_id=1, source_target_pairs={{0,2},{1,3},{2,0},{3,1},{4,6},{5,7},{6,4},{7,5},{8,10},{9,11},{10,... | collective-permute-start | bytes 811016 | tf_op jit(solution)/shard_map/ppermute | solution.py:440
  56.5 5.0 %collective-permute-done.9.a1_ref = bf16[528,256]{1,0:T(8,128)(2,1)S(1)} collective-permute-done((bf16[528,256]{1,0:T(8,128)(2,1)S(1)}, bf16[528,256]{1,0:T(8,128)(2,1)S(1)}, u32[]{:S(2)}, u32[]{:S(2)}) %collective-permute-start.9) | collective-permute-done | bytes 270368 | tf_op jit(solution)/shard_map/ppermute | solution.py:440
  61.6 7.0 %collective-permute-done.10.a2_ref = bf16[528,256]{1,0:T(8,128)(2,1)S(1)} collective-permute-done((bf16[528,256]{1,0:T(8,128)(2,1)S(1)}, bf16[528,256]{1,0:T(8,128)(2,1)S(1)}, u32[]{:S(2)}, u32[]{:S(2)}) %collective-permute-start.10) | collective-permute-done | bytes 270368 | tf_op jit(solution)/shard_map/ppermute | solution.py:440
  68.5 0.9 shard_map.99
  69.4 1.0 collective-permute-start.15
  70.4 3.5 %collective-permute-start.13 = (bf16[256,256]{1,0:T(8,128)(2,1)}, bf16[256,256]{1,0:T(8,128)(2,1)S(1)}, u32[]{:S(2)}, u32[]{:S(2)}) collective-permute-start(bf16[256,256]{1,0:T(8,128)(2,1)} %get-tuple-element.73), channel_id=1, source_target_pairs={{0,2},{1,3},{2,0},{3,1},{4,6},{5,7},{6,4},{7,5},{8,10},{9,11},{10,... | collective-permute-start | bytes 393224 | tf_op jit(solution)/shard_map/ppermute | solution.py:457
  73.9 1.6 %copy-done.6 = bf16[1,16,256,256]{3,2,0,1:T(8,128)(2,1)S(1)} copy-done((bf16[1,16,256,256]{3,2,0,1:T(8,128)(2,1)S(1)}, bf16[1,16,256,256]{3,2,0,1:T(8,128)(2,1)}, u32[]{:S(2)}) %copy-start.6) | copy-done | bytes 2097176
  75.5 3.3 %shard_map.100.refs_7_ = f32[2,256,256]{2,1,0:T(8,128)S(1)} custom-call(s32[25]{0:T(128)S(1)} %stack.103.order_ref, s32[8,16]{1,0:T(8,128)S(1)} %bitcast.49, s32[16]{0:T(128)S(1)} %bitcast.53, bf16[2,8,256,256]{3,2,1,0:T(8,128)(2,1)S(1)} %bitcast.37, bf16[16,256,256]{2,1,0:T(8,128)(2,1)S(1)} %bitcast.43), custom_call_target="tpu_custom_call" | custom-call | flops 536870912 | bytes 5242880 | tf_op jit(solution)/shard_map/pallas_call | solution.py:419
  78.8 1.2 collective-permute-done.13.refs_2_
  80.1 0.1 collective-permute-done.14.refs_3_
  80.1 1.1 shard_map.101
  81.2 0.0 all-gather.4.cloned.1.call-update
  81.3 1.8 %collective-permute-start.16 = (bf16[528,256]{1,0:T(8,128)(2,1)S(1)}, bf16[528,256]{1,0:T(8,128)(2,1)S(1)}, u32[]{:S(2)}, u32[]{:S(2)}) collective-permute-start(bf16[528,256]{1,0:T(8,128)(2,1)S(1)} %get-tuple-element.85.refs_0_), channel_id=1, source_target_pairs={{0,64},{8,72},{16,80},{24,88},{32,96},{40,104},{48,112},{56,120},{... | collective-permute-start | bytes 811016 | tf_op jit(solution)/shard_map/ppermute | solution.py:358
  83.1 2.7 %collective-permute-start.19 = (bf16[528,256]{1,0:T(8,128)(2,1)S(1)}, bf16[528,256]{1,0:T(8,128)(2,1)S(1)}, u32[]{:S(2)}, u32[]{:S(2)}) collective-permute-start(bf16[528,256]{1,0:T(8,128)(2,1)S(1)} %get-tuple-element.85.refs_0_), channel_id=1, source_target_pairs={{0,32},{8,40},{16,48},{24,56},{32,0},{40,8},{48,16},{56,24},{64,96... | collective-permute-start | bytes 811016 | tf_op jit(solution)/shard_map/ppermute | solution.py:359
  85.8 0.9 collective-permute-start.17
  86.7 1.1 collective-permute-start.18
  87.8 2.2 %collective-permute-done.16.refs_1_ = bf16[528,256]{1,0:T(8,128)(2,1)S(1)} collective-permute-done((bf16[528,256]{1,0:T(8,128)(2,1)S(1)}, bf16[528,256]{1,0:T(8,128)(2,1)S(1)}, u32[]{:S(2)}, u32[]{:S(2)}) %collective-permute-start.16) | collective-permute-done | bytes 270368 | tf_op jit(solution)/shard_map/ppermute | solution.py:358
  90.0 3.5 %collective-permute-start.20 = (bf16[528,256]{1,0:T(8,128)(2,1)S(1)}, bf16[528,256]{1,0:T(8,128)(2,1)S(1)}, u32[]{:S(2)}, u32[]{:S(2)}) collective-permute-start(bf16[528,256]{1,0:T(8,128)(2,1)S(1)} %collective-permute-done.16.refs_1_), channel_id=1, source_target_pairs={{0,48},{8,56},{16,0},{24,8},{32,16},{40,24},{48,32},{56,40},{64,11... | collective-permute-start | bytes 811016 | tf_op jit(solution)/shard_map/ppermute | solution.py:360
  93.5 0.5 collective-permute-done.19.refs_4_
  94.0 1.8 %collective-permute-start.22 = (bf16[528,256]{1,0:T(8,128)(2,1)S(1)}, bf16[528,256]{1,0:T(8,128)(2,1)S(1)}, u32[]{:S(2)}, u32[]{:S(2)}) collective-permute-start(bf16[528,256]{1,0:T(8,128)(2,1)S(1)} %collective-permute-done.19.refs_4_), channel_id=1, source_target_pairs={{0,64},{8,72},{16,80},{24,88},{32,96},{40,104},{48,112},{56,120},{... | collective-permute-start | bytes 811016 | tf_op jit(solution)/shard_map/ppermute | solution.py:361
  95.8 6.2 %shard_map.102 = (bf16[16,16,2,32,256]{4,3,2,1,0:T(8,128)(2,1)S(1)}, bf16[16,16,2,32,256]{4,3,2,1,0:T(8,128)(2,1)S(1)}) custom-call(bf16[16,16,2,32,256]{4,3,2,1,0:T(8,128)(2,1)} %w_ref.1, bf16[16,16,2,32,256]{4,3,2,1,0:T(8,128)(2,1)} %u_ref.2), custom_call_target="tpu_custom_call" | custom-call | bytes 33554432 | tf_op jit(solution)/shard_map/pallas_call | solution.py:375
  102.0 1.0 collective-permute-done.20.refs_5_
  103.0 3.7 %collective-permute-done.22.refs_7_ = bf16[528,256]{1,0:T(8,128)(2,1)S(1)} collective-permute-done((bf16[528,256]{1,0:T(8,128)(2,1)S(1)}, bf16[528,256]{1,0:T(8,128)(2,1)S(1)}, u32[]{:S(2)}, u32[]{:S(2)}) %collective-permute-start.22) | collective-permute-done | bytes 270368 | tf_op jit(solution)/shard_map/ppermute | solution.py:361
  106.7 0.3 shard_map.103.refs_0_
  107.0 0.1 collective-permute-start.23
  107.1 3.7 %shard_map.104 = (bf16[16,8,64,256]{3,2,1,0:T(8,128)(2,1)S(1)}, f32[16,256]{1,0:T(8,128)S(1)}) custom-call(s32[25]{0:T(128)S(1)} %stack.103.order_ref, s32[16,2,16]{2,1,0:T(2,128)S(1)} %bitcast.46, s32[8,16]{1,0:T(8,128)S(1)} %bitcast.50, s32[16]{0:T(128)S(1)} %bitcast.54, bf16[16,16,2,32,256]{4,3,2,1,0:T(8,128)(2,1)S(1)} %get-tuple-element.83.refs_8_.w_ref, ...), custom_call_target="tpu_custom_call" | custom-call | flops 1073741824 | bytes 16777216 | tf_op jit(solution)/shard_map/pallas_call | solution.py:390
  110.8 0.5 collective-permute-done.23.refs_0_
  111.3 6.3 %shard_map.105 = (bf16[4,256,256]{2,1,0:T(8,128)(2,1)S(1)}, bf16[4,256,256]{2,1,0:T(8,128)(2,1)S(1)}, bf16[528,256]{1,0:T(8,128)(2,1)S(1)}, bf16[528,256]{1,0:T(...) custom-call(s32[25]{0:T(128)S(1)} %stack.103.order_ref, s32[16,2,16]{2,1,0:T(2,128)S(1)} %bitcast.47, ...), custom_call_target="tpu_custom_call" | custom-call | flops 3221225472 | bytes 20971520 | tf_op jit(solution)/shard_map/pallas_call | solution.py:403
  117.7 0.8 collective-permute-start.24
  118.5 6.2 %collective-permute-start.26 = (bf16[528,256]{1,0:T(8,128)(2,1)S(1)}, bf16[528,256]{1,0:T(8,128)(2,1)S(1)}, u32[]{:S(2)}, u32[]{:S(2)}) collective-permute-start(bf16[528,256]{1,0:T(8,128)(2,1)S(1)} %get-tuple-element.92), channel_id=1, source_target_pairs={{0,2},{1,3},{2,0},{3,1},{4,6},{5,7},{6,4},{7,5},{8,10},{9,11},{10,... | collective-permute-start | bytes 811016 | tf_op jit(solution)/shard_map/ppermute | solution.py:440
  124.7 5.0 %collective-permute-done.25.a1_ref = bf16[528,256]{1,0:T(8,128)(2,1)S(1)} collective-permute-done((bf16[528,256]{1,0:T(8,128)(2,1)S(1)}, bf16[528,256]{1,0:T(8,128)(2,1)S(1)}, u32[]{:S(2)}, u32[]{:S(2)}) %collective-permute-start.25) | collective-permute-done | bytes 270368 | tf_op jit(solution)/shard_map/ppermute | solution.py:440
  129.7 7.0 %collective-permute-done.26.a2_ref = bf16[528,256]{1,0:T(8,128)(2,1)S(1)} collective-permute-done((bf16[528,256]{1,0:T(8,128)(2,1)S(1)}, bf16[528,256]{1,0:T(8,128)(2,1)S(1)}, u32[]{:S(2)}, u32[]{:S(2)}) %collective-permute-start.26) | collective-permute-done | bytes 270368 | tf_op jit(solution)/shard_map/ppermute | solution.py:440
  136.7 0.9 shard_map.106
  137.6 0.9 collective-permute-start.31
  138.5 3.5 %collective-permute-start.29 = (bf16[256,256]{1,0:T(8,128)(2,1)}, bf16[256,256]{1,0:T(8,128)(2,1)S(1)}, u32[]{:S(2)}, u32[]{:S(2)}) collective-permute-start(bf16[256,256]{1,0:T(8,128)(2,1)} %get-tuple-element.96), channel_id=1, source_target_pairs={{0,2},{1,3},{2,0},{3,1},{4,6},{5,7},{6,4},{7,5},{8,10},{9,11},{10,... | collective-permute-start | bytes 393224 | tf_op jit(solution)/shard_map/ppermute | solution.py:457
  142.0 1.6 %copy-done.7 = bf16[16,256,256]{2,1,0:T(8,128)(2,1)S(1)} copy-done((bf16[16,256,256]{2,1,0:T(8,128)(2,1)S(1)}, bf16[16,256,256]{2,1,0:T(8,128)(2,1)}, u32[]{:S(2)}) %copy-start.7) | copy-done | bytes 2097176
  143.6 3.3 %shard_map.107.refs_7_ = f32[2,256,256]{2,1,0:T(8,128)S(1)} custom-call(s32[25]{0:T(128)S(1)} %stack.103.order_ref, s32[8,16]{1,0:T(8,128)S(1)} %bitcast.51, s32[16]{0:T(128)S(1)} %bitcast.55, bf16[2,8,256,256]{3,2,1,0:T(8,128)(2,1)S(1)} %bitcast.38, bf16[16,256,256]{2,1,0:T(8,128)(2,1)S(1)} %copy-done.7), custom_call_target="tpu_custom_call" | custom-call | flops 536870912 | bytes 5242880 | tf_op jit(solution)/shard_map/pallas_call | solution.py:419
  147.0 1.2 collective-permute-done.29.refs_2_
  148.2 0.1 collective-permute-done.30.refs_3_
  148.2 1.1 shard_map.108
  (48 shorter events, 0.1 us)
Async XLA Ops:
  7.2 62.3 %all-gather.6.cloned.1.call-start = ((), (), s32[]{:S(2)}) async-start(), calls=%async_computation.1 | async-start | bytes 2359296 | tf_op jit(solution)/shard_map/all_gather | solution.py:434
  7.9 129.7 %all-gather.4.cloned.1.call-start = ((), (), s32[]{:S(2)}) async-start(), calls=%async_computation | async-start | bytes 2359296 | tf_op jit(solution)/shard_map/all_gather | solution.py:434
  9.9 9.8 %collective-permute-start = (bf16[528,256]{1,0:T(8,128)(2,1)}, bf16[528,256]{1,0:T(8,128)(2,1)S(1)}, u32[]{:S(2)}, u32[]{:S(2)}) collective-permute-start(bf16[528,256]{1,0:T(8,128)(2,1)} %shard_map.95.refs_0_), channel_id=1, source_target_pairs={{0,64},{8,72},{16,80},{24,88},{32,96},{40,104},{48,112},{56,120},{... | collective-permute-start | bytes 811016 | tf_op jit(solution)/shard_map/ppermute | solution.py:358
  13.0 11.5 %collective-permute-start.3 = (bf16[528,256]{1,0:T(8,128)(2,1)}, bf16[528,256]{1,0:T(8,128)(2,1)S(1)}, u32[]{:S(2)}, u32[]{:S(2)}) collective-permute-start(bf16[528,256]{1,0:T(8,128)(2,1)} %shard_map.95.refs_0_), channel_id=1, source_target_pairs={{0,32},{8,40},{16,48},{24,56},{32,0},{40,8},{48,16},{56,24},{64,96... | collective-permute-start | bytes 811016 | tf_op jit(solution)/shard_map/ppermute | solution.py:359
  16.9 16.4 %collective-permute-start.1 = (bf16[528,256]{1,0:T(8,128)(2,1)}, bf16[528,256]{1,0:T(8,128)(2,1)S(1)}, u32[]{:S(2)}, u32[]{:S(2)}) collective-permute-start(bf16[528,256]{1,0:T(8,128)(2,1)} %shard_map.95.refs_0_), channel_id=1, source_target_pairs={{0,48},{8,56},{16,0},{24,8},{32,16},{40,24},{48,32},{56,40},{64,11... | collective-permute-start | bytes 811016 | tf_op jit(solution)/shard_map/ppermute | solution.py:359
  17.6 15.7 %collective-permute-start.2 = (bf16[528,256]{1,0:T(8,128)(2,1)}, bf16[528,256]{1,0:T(8,128)(2,1)S(1)}, u32[]{:S(2)}, u32[]{:S(2)}) collective-permute-start(bf16[528,256]{1,0:T(8,128)(2,1)} %shard_map.95.refs_0_), channel_id=1, source_target_pairs={{0,16},{8,24},{16,32},{24,40},{32,48},{40,56},{48,0},{56,8},{64,80... | collective-permute-start | bytes 811016 | tf_op jit(solution)/shard_map/ppermute | solution.py:359
  19.7 16.0 %collective-permute-start.4 = (bf16[528,256]{1,0:T(8,128)(2,1)S(1)}, bf16[528,256]{1,0:T(8,128)(2,1)S(1)}, u32[]{:S(2)}, u32[]{:S(2)}) collective-permute-start(bf16[528,256]{1,0:T(8,128)(2,1)S(1)} %collective-permute-done.refs_1_), channel_id=1, source_target_pairs={{0,48},{8,56},{16,0},{24,8},{32,16},{40,24},{48,32},{56,40},{64,11... | collective-permute-start | bytes 811016 | tf_op jit(solution)/shard_map/ppermute | solution.py:360
  24.0 11.7 %collective-permute-start.5 = (bf16[528,256]{1,0:T(8,128)(2,1)S(1)}, bf16[528,256]{1,0:T(8,128)(2,1)S(1)}, u32[]{:S(2)}, u32[]{:S(2)}) collective-permute-start(bf16[528,256]{1,0:T(8,128)(2,1)S(1)} %collective-permute-done.refs_1_), channel_id=1, source_target_pairs={{0,16},{8,24},{16,32},{24,40},{32,48},{40,56},{48,0},{56,8},{64,80... | collective-permute-start | bytes 811016 | tf_op jit(solution)/shard_map/ppermute | solution.py:360
  24.5 13.8 %collective-permute-start.6 = (bf16[528,256]{1,0:T(8,128)(2,1)S(1)}, bf16[528,256]{1,0:T(8,128)(2,1)S(1)}, u32[]{:S(2)}, u32[]{:S(2)}) collective-permute-start(bf16[528,256]{1,0:T(8,128)(2,1)S(1)} %collective-permute-done.3.refs_4_), channel_id=1, source_target_pairs={{0,64},{8,72},{16,80},{24,88},{32,96},{40,104},{48,112},{56,120},{... | collective-permute-start | bytes 811016 | tf_op jit(solution)/shard_map/ppermute | solution.py:361
  27.1 11.2 %copy-start.8 = (bf16[528,256]{1,0:T(8,128)(2,1)S(1)}, bf16[528,256]{1,0:T(8,128)(2,1)}, u32[]{:S(2)}) copy-start(bf16[528,256]{1,0:T(8,128)(2,1)} %shard_map.95.refs_0_) | copy-start | bytes 811012
  33.3 5.3 %copy-start.1 = (bf16[16,16,2,32,256]{4,3,2,1,0:T(8,128)(2,1)}, bf16[16,16,2,32,256]{4,3,2,1,0:T(8,128)(2,1)S(1)}, u32[]{:S(2)}) copy-start(bf16[16,16,2,32,256]{4,3,2,1,0:T(8,128)(2,1)S(1)} %get-tuple-element.60.u_ref) | copy-start | bytes 25165828
  38.3 0.7 copy-start.10
  38.3 0.7 copy-start.11
  38.3 0.7 copy-start.12
  38.6 4.3 %collective-permute-start.7 = (bf16[8,528,256]{2,1,0:T(8,128)(2,1)S(1)}, bf16[8,528,256]{2,1,0:T(8,128)(2,1)S(1)}, u32[]{:S(2)}, u32[]{:S(2)}) collective-permute-start(bf16[8,528,256]{2,1,0:T(8,128)(2,1)S(1)} %shard_map.96.refs_0_), channel_id=1, source_target_pairs={{0,8},{8,0},{16,24},{24,16},{32,40},{40,32},{48,56},{56,48},{64,72... | collective-permute-start | bytes 6488072 | tf_op jit(solution)/shard_map/ppermute | solution.py:363
  39.0 4.0 %copy-start.2 = (bf16[16,16,2,32,256]{4,3,2,1,0:T(8,128)(2,1)S(1)}, bf16[16,16,2,32,256]{4,3,2,1,0:T(8,128)(2,1)}, u32[]{:S(2)}) copy-start(bf16[16,16,2,32,256]{4,3,2,1,0:T(8,128)(2,1)} %copy-done.1) | copy-start | bytes 25165828
  43.0 31.0 %copy-start = (bf16[1,2,8,256,256]{4,3,2,1,0:T(8,128)(2,1)S(1)}, bf16[1,2,8,256,256]{4,3,2,1,0:T(8,128)(2,1)}, u32[]{:S(2)}) copy-start(bf16[1,2,8,256,256]{4,3,2,1,0:T(8,128)(2,1)} %param.11) | copy-start | bytes 6291460
  49.3 30.8 %copy-start.5 = (bf16[1,2,256,256]{3,2,1,0:T(8,128)(2,1)S(1)}, bf16[1,2,256,256]{3,2,1,0:T(8,128)(2,1)}, u32[]{:S(2)}) copy-start(bf16[1,2,256,256]{3,2,1,0:T(8,128)(2,1)} %param.7) | copy-start | bytes 786436
  49.3 19.2 %collective-permute-start.8 = (bf16[4,256,256]{2,1,0:T(8,128)(2,1)S(1)}, bf16[4,256,256]{2,1,0:T(8,128)(2,1)S(1)}, u32[]{:S(2)}, u32[]{:S(2)}) collective-permute-start(bf16[4,256,256]{2,1,0:T(8,128)(2,1)S(1)} %get-tuple-element.66), channel_id=1, source_target_pairs={{0,4},{1,5},{2,6},{3,7},{4,0},{5,1},{6,2},{7,3},{8,12},{9,13},{10,... | collective-permute-start | bytes 1572872 | tf_op jit(solution)/shard_map/ppermute | solution.py:439
  51.3 10.3 %collective-permute-start.9 = (bf16[528,256]{1,0:T(8,128)(2,1)S(1)}, bf16[528,256]{1,0:T(8,128)(2,1)S(1)}, u32[]{:S(2)}, u32[]{:S(2)}) collective-permute-start(bf16[528,256]{1,0:T(8,128)(2,1)S(1)} %get-tuple-element.68), channel_id=1, source_target_pairs={{0,1},{1,2},{2,3},{3,0},{4,5},{5,6},{6,7},{7,4},{8,9},{9,10},{10,1... | collective-permute-start | bytes 811016 | tf_op jit(solution)/shard_map/ppermute | solution.py:440
  51.3 17.2 %collective-permute-start.10 = (bf16[528,256]{1,0:T(8,128)(2,1)S(1)}, bf16[528,256]{1,0:T(8,128)(2,1)S(1)}, u32[]{:S(2)}, u32[]{:S(2)}) collective-permute-start(bf16[528,256]{1,0:T(8,128)(2,1)S(1)} %get-tuple-element.69), channel_id=1, source_target_pairs={{0,2},{1,3},{2,0},{3,1},{4,6},{5,7},{6,4},{7,5},{8,10},{9,11},{10,... | collective-permute-start | bytes 811016 | tf_op jit(solution)/shard_map/ppermute | solution.py:440
  56.5 12.0 %collective-permute-start.11 = (bf16[528,256]{1,0:T(8,128)(2,1)S(1)}, bf16[528,256]{1,0:T(8,128)(2,1)S(1)}, u32[]{:S(2)}, u32[]{:S(2)}) collective-permute-start(bf16[528,256]{1,0:T(8,128)(2,1)S(1)} %get-tuple-element.70), channel_id=1, source_target_pairs={{0,3},{1,0},{2,1},{3,2},{4,7},{5,4},{6,5},{7,6},{8,11},{9,8},{10,9... | collective-permute-start | bytes 811016 | tf_op jit(solution)/shard_map/ppermute | solution.py:440
  69.4 10.7 %collective-permute-start.15 = (bf16[272,256]{1,0:T(8,128)(2,1)}, bf16[272,256]{1,0:T(8,128)(2,1)S(1)}, u32[]{:S(2)}, u32[]{:S(2)}) collective-permute-start(bf16[272,256]{1,0:T(8,128)(2,1)} %get-tuple-element.77), channel_id=1, source_target_pairs={{0,4},{1,5},{2,6},{3,7},{4,0},{5,1},{6,2},{7,3},{8,12},{9,13},{10,... | collective-permute-start | bytes 417800 | tf_op jit(solution)/shard_map/ppermute | solution.py:458
  70.4 8.4 %collective-permute-start.12 = (bf16[256,256]{1,0:T(8,128)(2,1)}, bf16[256,256]{1,0:T(8,128)(2,1)S(1)}, u32[]{:S(2)}, u32[]{:S(2)}) collective-permute-start(bf16[256,256]{1,0:T(8,128)(2,1)} %get-tuple-element.72), channel_id=1, source_target_pairs={{0,1},{1,2},{2,3},{3,0},{4,5},{5,6},{6,7},{7,4},{8,9},{9,10},{10,1... | collective-permute-start | bytes 393224 | tf_op jit(solution)/shard_map/ppermute | solution.py:457
  70.4 9.7 %collective-permute-start.13 = (bf16[256,256]{1,0:T(8,128)(2,1)}, bf16[256,256]{1,0:T(8,128)(2,1)S(1)}, u32[]{:S(2)}, u32[]{:S(2)}) collective-permute-start(bf16[256,256]{1,0:T(8,128)(2,1)} %get-tuple-element.73), channel_id=1, source_target_pairs={{0,2},{1,3},{2,0},{3,1},{4,6},{5,7},{6,4},{7,5},{8,10},{9,11},{10,... | collective-permute-start | bytes 393224 | tf_op jit(solution)/shard_map/ppermute | solution.py:457
  73.9 6.2 %collective-permute-start.14 = (bf16[256,256]{1,0:T(8,128)(2,1)}, bf16[256,256]{1,0:T(8,128)(2,1)S(1)}, u32[]{:S(2)}, u32[]{:S(2)}) collective-permute-start(bf16[256,256]{1,0:T(8,128)(2,1)} %get-tuple-element.74), channel_id=1, source_target_pairs={{0,3},{1,0},{2,1},{3,2},{4,7},{5,4},{6,5},{7,6},{8,11},{9,8},{10,9... | collective-permute-start | bytes 393224 | tf_op jit(solution)/shard_map/ppermute | solution.py:457
  73.9 1.6 %copy-start.6 = (bf16[1,16,256,256]{3,2,0,1:T(8,128)(2,1)S(1)}, bf16[1,16,256,256]{3,2,0,1:T(8,128)(2,1)}, u32[]{:S(2)}) copy-start(bf16[1,16,256,256]{3,2,0,1:T(8,128)(2,1)} %all-gather.6.cloned.1.call-done) | copy-start | bytes 6291460
  81.3 8.8 %collective-permute-start.16 = (bf16[528,256]{1,0:T(8,128)(2,1)S(1)}, bf16[528,256]{1,0:T(8,128)(2,1)S(1)}, u32[]{:S(2)}, u32[]{:S(2)}) collective-permute-start(bf16[528,256]{1,0:T(8,128)(2,1)S(1)} %get-tuple-element.85.refs_0_), channel_id=1, source_target_pairs={{0,64},{8,72},{16,80},{24,88},{32,96},{40,104},{48,112},{56,120},{... | collective-permute-start | bytes 811016 | tf_op jit(solution)/shard_map/ppermute | solution.py:358
  83.1 10.9 %collective-permute-start.19 = (bf16[528,256]{1,0:T(8,128)(2,1)S(1)}, bf16[528,256]{1,0:T(8,128)(2,1)S(1)}, u32[]{:S(2)}, u32[]{:S(2)}) collective-permute-start(bf16[528,256]{1,0:T(8,128)(2,1)S(1)} %get-tuple-element.85.refs_0_), channel_id=1, source_target_pairs={{0,32},{8,40},{16,48},{24,56},{32,0},{40,8},{48,16},{56,24},{64,96... | collective-permute-start | bytes 811016 | tf_op jit(solution)/shard_map/ppermute | solution.py:359
  85.8 16.2 %collective-permute-start.17 = (bf16[528,256]{1,0:T(8,128)(2,1)S(1)}, bf16[528,256]{1,0:T(8,128)(2,1)S(1)}, u32[]{:S(2)}, u32[]{:S(2)}) collective-permute-start(bf16[528,256]{1,0:T(8,128)(2,1)S(1)} %get-tuple-element.85.refs_0_), channel_id=1, source_target_pairs={{0,48},{8,56},{16,0},{24,8},{32,16},{40,24},{48,32},{56,40},{64,11... | collective-permute-start | bytes 811016 | tf_op jit(solution)/shard_map/ppermute | solution.py:359
  86.7 15.3 %collective-permute-start.18 = (bf16[528,256]{1,0:T(8,128)(2,1)S(1)}, bf16[528,256]{1,0:T(8,128)(2,1)S(1)}, u32[]{:S(2)}, u32[]{:S(2)}) collective-permute-start(bf16[528,256]{1,0:T(8,128)(2,1)S(1)} %get-tuple-element.85.refs_0_), channel_id=1, source_target_pairs={{0,16},{8,24},{16,32},{24,40},{32,48},{40,56},{48,0},{56,8},{64,80... | collective-permute-start | bytes 811016 | tf_op jit(solution)/shard_map/ppermute | solution.py:359
  90.0 13.0 %collective-permute-start.20 = (bf16[528,256]{1,0:T(8,128)(2,1)S(1)}, bf16[528,256]{1,0:T(8,128)(2,1)S(1)}, u32[]{:S(2)}, u32[]{:S(2)}) collective-permute-start(bf16[528,256]{1,0:T(8,128)(2,1)S(1)} %collective-permute-done.16.refs_1_), channel_id=1, source_target_pairs={{0,48},{8,56},{16,0},{24,8},{32,16},{40,24},{48,32},{56,40},{64,11... | collective-permute-start | bytes 811016 | tf_op jit(solution)/shard_map/ppermute | solution.py:360
  93.5 9.5 %collective-permute-start.21 = (bf16[528,256]{1,0:T(8,128)(2,1)S(1)}, bf16[528,256]{1,0:T(8,128)(2,1)S(1)}, u32[]{:S(2)}, u32[]{:S(2)}) collective-permute-start(bf16[528,256]{1,0:T(8,128)(2,1)S(1)} %collective-permute-done.16.refs_1_), channel_id=1, source_target_pairs={{0,16},{8,24},{16,32},{24,40},{32,48},{40,56},{48,0},{56,8},{64,80... | collective-permute-start | bytes 811016 | tf_op jit(solution)/shard_map/ppermute | solution.py:360
  94.0 12.7 %collective-permute-start.22 = (bf16[528,256]{1,0:T(8,128)(2,1)S(1)}, bf16[528,256]{1,0:T(8,128)(2,1)S(1)}, u32[]{:S(2)}, u32[]{:S(2)}) collective-permute-start(bf16[528,256]{1,0:T(8,128)(2,1)S(1)} %collective-permute-done.19.refs_4_), channel_id=1, source_target_pairs={{0,64},{8,72},{16,80},{24,88},{32,96},{40,104},{48,112},{56,120},{... | collective-permute-start | bytes 811016 | tf_op jit(solution)/shard_map/ppermute | solution.py:361
  102.0 5.0 %copy-start.3 = (bf16[16,16,2,32,256]{4,3,2,1,0:T(8,128)(2,1)}, bf16[16,16,2,32,256]{4,3,2,1,0:T(8,128)(2,1)S(1)}, u32[]{:S(2)}) copy-start(bf16[16,16,2,32,256]{4,3,2,1,0:T(8,128)(2,1)S(1)} %get-tuple-element.84.u_ref) | copy-start | bytes 25165828
  107.0 4.3 %collective-permute-start.23 = (bf16[8,528,256]{2,1,0:T(8,128)(2,1)S(1)}, bf16[8,528,256]{2,1,0:T(8,128)(2,1)S(1)}, u32[]{:S(2)}, u32[]{:S(2)}) collective-permute-start(bf16[8,528,256]{2,1,0:T(8,128)(2,1)S(1)} %shard_map.103.refs_0_), channel_id=1, source_target_pairs={{0,8},{8,0},{16,24},{24,16},{32,40},{40,32},{48,56},{56,48},{64,72... | collective-permute-start | bytes 6488072 | tf_op jit(solution)/shard_map/ppermute | solution.py:363
  107.1 4.2 %copy-start.4 = (bf16[16,16,2,32,256]{4,3,2,1,0:T(8,128)(2,1)S(1)}, bf16[16,16,2,32,256]{4,3,2,1,0:T(8,128)(2,1)}, u32[]{:S(2)}) copy-start(bf16[16,16,2,32,256]{4,3,2,1,0:T(8,128)(2,1)} %copy-done.3) | copy-start | bytes 25165828
  117.6 30.6 %copy-start.9 = (f32[2,256,256]{2,1,0:T(8,128)S(1)}, f32[2,256,256]{2,1,0:T(8,128)}, u32[]{:S(2)}) copy-start(f32[2,256,256]{2,1,0:T(8,128)} %get-tuple-element.104.refs_9_) | copy-start | bytes 1572868
  117.7 19.1 %collective-permute-start.24 = (bf16[4,256,256]{2,1,0:T(8,128)(2,1)S(1)}, bf16[4,256,256]{2,1,0:T(8,128)(2,1)S(1)}, u32[]{:S(2)}, u32[]{:S(2)}) collective-permute-start(bf16[4,256,256]{2,1,0:T(8,128)(2,1)S(1)} %get-tuple-element.89), channel_id=1, source_target_pairs={{0,4},{1,5},{2,6},{3,7},{4,0},{5,1},{6,2},{7,3},{8,12},{9,13},{10,... | collective-permute-start | bytes 1572872 | tf_op jit(solution)/shard_map/ppermute | solution.py:439
  118.5 11.2 %collective-permute-start.25 = (bf16[528,256]{1,0:T(8,128)(2,1)S(1)}, bf16[528,256]{1,0:T(8,128)(2,1)S(1)}, u32[]{:S(2)}, u32[]{:S(2)}) collective-permute-start(bf16[528,256]{1,0:T(8,128)(2,1)S(1)} %get-tuple-element.91), channel_id=1, source_target_pairs={{0,1},{1,2},{2,3},{3,0},{4,5},{5,6},{6,7},{7,4},{8,9},{9,10},{10,1... | collective-permute-start | bytes 811016 | tf_op jit(solution)/shard_map/ppermute | solution.py:440
  118.5 18.2 %collective-permute-start.26 = (bf16[528,256]{1,0:T(8,128)(2,1)S(1)}, bf16[528,256]{1,0:T(8,128)(2,1)S(1)}, u32[]{:S(2)}, u32[]{:S(2)}) collective-permute-start(bf16[528,256]{1,0:T(8,128)(2,1)S(1)} %get-tuple-element.92), channel_id=1, source_target_pairs={{0,2},{1,3},{2,0},{3,1},{4,6},{5,7},{6,4},{7,5},{8,10},{9,11},{10,... | collective-permute-start | bytes 811016 | tf_op jit(solution)/shard_map/ppermute | solution.py:440
  124.7 12.0 %collective-permute-start.27 = (bf16[528,256]{1,0:T(8,128)(2,1)S(1)}, bf16[528,256]{1,0:T(8,128)(2,1)S(1)}, u32[]{:S(2)}, u32[]{:S(2)}) collective-permute-start(bf16[528,256]{1,0:T(8,128)(2,1)S(1)} %get-tuple-element.93), channel_id=1, source_target_pairs={{0,3},{1,0},{2,1},{3,2},{4,7},{5,4},{6,5},{7,6},{8,11},{9,8},{10,9... | collective-permute-start | bytes 811016 | tf_op jit(solution)/shard_map/ppermute | solution.py:440
  137.6 10.6 %collective-permute-start.31 = (bf16[272,256]{1,0:T(8,128)(2,1)}, bf16[272,256]{1,0:T(8,128)(2,1)S(1)}, u32[]{:S(2)}, u32[]{:S(2)}) collective-permute-start(bf16[272,256]{1,0:T(8,128)(2,1)} %get-tuple-element.101), channel_id=1, source_target_pairs={{0,4},{1,5},{2,6},{3,7},{4,0},{5,1},{6,2},{7,3},{8,12},{9,13},{10,... | collective-permute-start | bytes 417800 | tf_op jit(solution)/shard_map/ppermute | solution.py:458
  138.5 8.4 %collective-permute-start.28 = (bf16[256,256]{1,0:T(8,128)(2,1)}, bf16[256,256]{1,0:T(8,128)(2,1)S(1)}, u32[]{:S(2)}, u32[]{:S(2)}) collective-permute-start(bf16[256,256]{1,0:T(8,128)(2,1)} %get-tuple-element.95), channel_id=1, source_target_pairs={{0,1},{1,2},{2,3},{3,0},{4,5},{5,6},{6,7},{7,4},{8,9},{9,10},{10,1... | collective-permute-start | bytes 393224 | tf_op jit(solution)/shard_map/ppermute | solution.py:457
  138.5 9.7 %collective-permute-start.29 = (bf16[256,256]{1,0:T(8,128)(2,1)}, bf16[256,256]{1,0:T(8,128)(2,1)S(1)}, u32[]{:S(2)}, u32[]{:S(2)}) collective-permute-start(bf16[256,256]{1,0:T(8,128)(2,1)} %get-tuple-element.96), channel_id=1, source_target_pairs={{0,2},{1,3},{2,0},{3,1},{4,6},{5,7},{6,4},{7,5},{8,10},{9,11},{10,... | collective-permute-start | bytes 393224 | tf_op jit(solution)/shard_map/ppermute | solution.py:457
  142.0 6.2 %collective-permute-start.30 = (bf16[256,256]{1,0:T(8,128)(2,1)}, bf16[256,256]{1,0:T(8,128)(2,1)S(1)}, u32[]{:S(2)}, u32[]{:S(2)}) collective-permute-start(bf16[256,256]{1,0:T(8,128)(2,1)} %get-tuple-element.97), channel_id=1, source_target_pairs={{0,3},{1,0},{2,1},{3,2},{4,7},{5,4},{6,5},{7,6},{8,11},{9,8},{10,9... | collective-permute-start | bytes 393224 | tf_op jit(solution)/shard_map/ppermute | solution.py:457
  142.0 1.6 %copy-start.7 = (bf16[16,256,256]{2,1,0:T(8,128)(2,1)S(1)}, bf16[16,256,256]{2,1,0:T(8,128)(2,1)}, u32[]{:S(2)}) copy-start(bf16[16,256,256]{2,1,0:T(8,128)(2,1)} %all-gather.4.cloned.1.call-done.panel_ref) | copy-start | bytes 6291460
Sparse Core Ops, SparseCore 0:
  9.6 46.0 all-gather.5
  81.4 41.0 all-gather.3

commit v5 on v4

--- a/solution.py
+++ b/solution.py
@@ -438,6 +438,8 @@
         around, own = around[:-1], around[-1]
         cross = lax.ppermute(cross, "near", flip_x)
         around = [lax.ppermute(part, "near", up_y(turn + 1)) for turn, part in enumerate(around)]
+        near = near_products(panel)
+        stay, near = lax.optimization_barrier((stay, near))
         block = (size, width)
         first, *sends, second, send, sums = pl.pallas_call(
             add_kernel,
@@ -453,9 +455,8 @@
             compiler_params=params(8),
             cost_estimate=cost(0, 3),
         )(stay, cross, own, *around)
-        send, panel = lax.optimization_barrier((send, panel))
         sends = [lax.ppermute(part, "near", up_y(turn + 1)) for turn, part in enumerate(sends)]
-        return (first, *sends, second, lax.ppermute(send, "near", flip_x), sums), panel
+        return (first, *sends, second, lax.ppermute(send, "near", flip_x), sums), near
 
     payload = pl.pallas_call(
         start_kernel,
@@ -466,7 +467,7 @@
         compiler_params=params(60),
     )(x, tiles)
     panel = gather_near(x)
-    far_x, panel = scatter_panel(far_products(payload, far_w, far_u), panel)
+    far_x, near_x = scatter_panel(far_products(payload, far_w, far_u), panel)
     image, sums, z, payload = pl.pallas_call(
         functools.partial(middle_kernel, total_rows=total_rows),
         out_shape=(
@@ -478,10 +479,10 @@
         in_specs=[vmem] * 9,
         out_specs=(vmem,) * 4,
         compiler_params=params(8),
-    )(*far_x, near_products(panel), x)
+    )(*far_x, near_x, x)
     panel = gather_near(z)
     payload, far_w, far_u = lax.optimization_barrier((payload, far_w, far_u))
-    far_z, panel = scatter_panel(far_products(payload, far_w, far_u), panel)
+    far_z, near_z = scatter_panel(far_products(payload, far_w, far_u), panel)
     second_basis, second_image, coefficients = pl.pallas_call(
         functools.partial(last_kernel, total_rows=total_rows),
         out_shape=(
@@ -492,7 +493,7 @@
         in_specs=[vmem] * 11,
         out_specs=(vmem, vmem, vmem),
         compiler_params=params(8),
-    )(*far_z, near_products(panel), x, image, sums)
+    )(*far_z, near_z, x, image, sums)
     return second_basis[None], second_image[None], coefficients
 
 

time: 156 us -> 162 us (1.038)
  Pallas kernels: 45.5 us -> 50.9 us
    pallas_call x2, Pallas kernels: 1.8 us -> 4.16 us  [scatter_panel(): pl.pallas_call(add_kernel, out_shape=(jax.ShapeDtypeStruct(block, f32),)...]
    unnamed x26 -> x34, local copies, waits for them, and re-layouts: 3.51 us -> 4.89 us
where the time goes in v5:
time: 162 us
  starting transfers between devices  50.9 us (31%)
  Pallas kernels  50.9 us (31%)
  waiting for transfers between devices  40.7 us (25%)
  between operations  14.3 us (9%)
  local copies, waits for them, and re-layouts  4.99 us (3%)
    ppermute x12, waiting for transfers between devices, scatter_panel(): lax.ppermute(part, 'near', up_y(turn + 1))  25.7 us
    ppermute x12, starting transfers between devices, scatter_panel(): lax.ppermute(part, 'near', up_y(turn + 1))  18.6 us
    pallas_call x2, Pallas kernels, far_products(): pl.pallas_call(far_kernel, out_shape=(jax.ShapeDtypeStruct((ys, size, wid...  14.2 us
    pallas_call x2, Pallas kernels, load_factors(): pl.pallas_call(load_kernel, out_shape=(pltpu.VMEM(far_w.shape, bf16), plt...  12.3 us
    ppermute x6, starting transfers between devices, gather_panels(): own = [lax.ppermute(payload, 'blk', along_z(turn)) for turn in z_turns[1:]]  10.6 us
    pallas_call x2, Pallas kernels, near_products(): pl.pallas_call(near_kernel, out_shape=jax.ShapeDtypeStruct((per_dev, size...  8.1 us
    ppermute x4, starting transfers between devices, gather_panels(): late = [lax.ppermute(far, 'blk', along_z(turn)) for turn in z_turns[1:3]]  7.74 us
    pallas_call x2, Pallas kernels, far_products(): pl.pallas_call(code_kernel, out_shape=(pltpu.VMEM((targets, n, per_dev *...  7.42 us
  transfers between devices with their start and end apart: 34, of which 18 were waited for; matrix products, arithmetic and copies ran while one was open for 0% of the time, Pallas kernels for 28%

profile of v5, /device:TPU:0, one launch (start us, length us, event | category | flops | bytes accessed | tf_op | source)
XLA Modules:
  0.0 161.9 jit_solution(8671509468238878694)
XLA Ops:
  7.2 0.0 all-gather.6.cloned.1.call-start
  7.2 0.7 all-gather.6.cloned.1.call-update
  7.9 0.0 all-gather.4.cloned.1.call-start
  7.9 2.0 %shard_map.95.refs_0_ = bf16[528,256]{1,0:T(8,128)(2,1)} custom-call(bf16[2,256,256]{2,1,0:T(8,128)(2,1)} %bitcast.40, bf16[2,8,256,256]{3,2,1,0:T(8,128)(2,1)} %bitcast.36), custom_call_target="tpu_custom_call" | custom-call | tf_op jit(solution)/shard_map/pallas_call | solution.py:461
  9.9 3.1 %collective-permute-start = (bf16[528,256]{1,0:T(8,128)(2,1)}, bf16[528,256]{1,0:T(8,128)(2,1)S(1)}, u32[]{:S(2)}, u32[]{:S(2)}) collective-permute-start(bf16[528,256]{1,0:T(8,128)(2,1)} %shard_map.95.refs_0_), channel_id=1, source_target_pairs={{0,64},{8,72},{16,80},{24,88},{32,96},{40,104},{48,112},{56,120},{... | collective-permute-start | bytes 811016 | tf_op jit(solution)/shard_map/ppermute | solution.py:358
  13.0 3.9 %collective-permute-start.3 = (bf16[528,256]{1,0:T(8,128)(2,1)}, bf16[528,256]{1,0:T(8,128)(2,1)S(1)}, u32[]{:S(2)}, u32[]{:S(2)}) collective-permute-start(bf16[528,256]{1,0:T(8,128)(2,1)} %shard_map.95.refs_0_), channel_id=1, source_target_pairs={{0,32},{8,40},{16,48},{24,56},{32,0},{40,8},{48,16},{56,24},{64,96... | collective-permute-start | bytes 811016 | tf_op jit(solution)/shard_map/ppermute | solution.py:359
  16.9 0.7 collective-permute-start.1
  17.6 1.3 collective-permute-start.2
  18.9 0.8 collective-permute-done.refs_1_
  19.7 4.3 %collective-permute-start.4 = (bf16[528,256]{1,0:T(8,128)(2,1)S(1)}, bf16[528,256]{1,0:T(8,128)(2,1)S(1)}, u32[]{:S(2)}, u32[]{:S(2)}) collective-permute-start(bf16[528,256]{1,0:T(8,128)(2,1)S(1)} %collective-permute-done.refs_1_), channel_id=1, source_target_pairs={{0,48},{8,56},{16,0},{24,8},{32,16},{40,24},{48,32},{56,40},{64,11... | collective-permute-start | bytes 811016 | tf_op jit(solution)/shard_map/ppermute | solution.py:360
  24.0 0.5 collective-permute-done.3.refs_4_
  24.5 2.5 %collective-permute-start.6 = (bf16[528,256]{1,0:T(8,128)(2,1)S(1)}, bf16[528,256]{1,0:T(8,128)(2,1)S(1)}, u32[]{:S(2)}, u32[]{:S(2)}) collective-permute-start(bf16[528,256]{1,0:T(8,128)(2,1)S(1)} %collective-permute-done.3.refs_4_), channel_id=1, source_target_pairs={{0,64},{8,72},{16,80},{24,88},{32,96},{40,104},{48,112},{56,120},{... | collective-permute-start | bytes 811016 | tf_op jit(solution)/shard_map/ppermute | solution.py:361
  27.0 0.1 stack.103.order_ref
  27.1 6.2 %shard_map.94 = (bf16[16,16,2,32,256]{4,3,2,1,0:T(8,128)(2,1)S(1)}, bf16[16,16,2,32,256]{4,3,2,1,0:T(8,128)(2,1)S(1)}) custom-call(bf16[16,16,2,32,256]{4,3,2,1,0:T(8,128)(2,1)} %w_ref.1, bf16[16,16,2,32,256]{4,3,2,1,0:T(8,128)(2,1)} %u_ref.2), custom_call_target="tpu_custom_call" | custom-call | bytes 33554432 | tf_op jit(solution)/shard_map/pallas_call | solution.py:375
  33.4 2.3 %collective-permute-done.4.refs_5_ = bf16[528,256]{1,0:T(8,128)(2,1)S(1)} collective-permute-done((bf16[528,256]{1,0:T(8,128)(2,1)S(1)}, bf16[528,256]{1,0:T(8,128)(2,1)S(1)}, u32[]{:S(2)}, u32[]{:S(2)}) %collective-permute-start.4) | collective-permute-done | bytes 270368 | tf_op jit(solution)/shard_map/ppermute | solution.py:360
  35.7 2.6 %collective-permute-done.6.refs_7_ = bf16[528,256]{1,0:T(8,128)(2,1)S(1)} collective-permute-done((bf16[528,256]{1,0:T(8,128)(2,1)S(1)}, bf16[528,256]{1,0:T(8,128)(2,1)S(1)}, u32[]{:S(2)}, u32[]{:S(2)}) %collective-permute-start.6) | collective-permute-done | bytes 270368 | tf_op jit(solution)/shard_map/ppermute | solution.py:361
  38.3 0.3 shard_map.96.refs_0_
  38.6 0.1 collective-permute-start.7
  38.7 0.3 copy-done.14
  39.0 3.7 %shard_map.97 = (bf16[16,8,64,256]{3,2,1,0:T(8,128)(2,1)S(1)}, f32[16,256]{1,0:T(8,128)S(1)}) custom-call(s32[25]{0:T(128)S(1)} %stack.103.order_ref, s32[16,2,16]{2,1,0:T(2,128)S(1)} %bitcast.44, s32[8,16]{1,0:T(8,128)S(1)} %bitcast.48, s32[16]{0:T(128)S(1)} %bitcast.52, bf16[16,16,2,32,256]{4,3,2,1,0:T(8,128)(2,1)S(1)} %get-tuple-element.59.refs_8_.w_ref, ...), custom_call_target="tpu_custom_call" | custom-call | flops 1073741824 | bytes 16777216 | tf_op jit(solution)/shard_map/pallas_call | solution.py:390
  42.7 0.2 collective-permute-done.7.refs_0_
  43.0 7.1 %shard_map.98 = (bf16[4,256,256]{2,1,0:T(8,128)(2,1)}, bf16[4,256,256]{2,1,0:T(8,128)(2,1)S(1)}, bf16[528,256]{1,0:T(8,128)(2,1)}, bf16[528,256]{1,0:T(8,128)(2,...) custom-call(s32[25]{0:T(128)S(1)} %stack.103.order_ref, s32[16,2,16]{2,1,0:T(2,128)S(1)} %bitcast.45, ...), custom_call_target="tpu_custom_call" | custom-call | flops 3221225472 | bytes 20971520 | tf_op jit(solution)/shard_map/pallas_call | solution.py:403
  50.1 0.7 copy-done.12
  50.7 1.9 %collective-permute-start.8 = (bf16[4,256,256]{2,1,0:T(8,128)(2,1)}, bf16[4,256,256]{2,1,0:T(8,128)(2,1)S(1)}, u32[]{:S(2)}, u32[]{:S(2)}) collective-permute-start(bf16[4,256,256]{2,1,0:T(8,128)(2,1)} %get-tuple-element.67), channel_id=1, source_target_pairs={{0,4},{1,5},{2,6},{3,7},{4,0},{5,1},{6,2},{7,3},{8,12},{9,13},{10,... | collective-permute-start | bytes 1572872 | tf_op jit(solution)/shard_map/ppermute | solution.py:439
  52.7 5.2 %collective-permute-start.10 = (bf16[528,256]{1,0:T(8,128)(2,1)}, bf16[528,256]{1,0:T(8,128)(2,1)}, u32[]{:S(2)}, u32[]{:S(2)}) collective-permute-start(bf16[528,256]{1,0:T(8,128)(2,1)} %get-tuple-element.70), channel_id=1, source_target_pairs={{0,2},{1,3},{2,0},{3,1},{4,6},{5,7},{6,4},{7,5},{8,10},{9,11},{10,... | collective-permute-start | bytes 811016 | tf_op jit(solution)/shard_map/ppermute | solution.py:440
  58.0 1.6 copy-done.6
  59.5 4.1 %shard_map.99.refs_7_ = f32[2,256,256]{2,1,0:T(8,128)S(1)} custom-call(s32[25]{0:T(128)S(1)} %stack.103.order_ref, s32[8,16]{1,0:T(8,128)S(1)} %bitcast.49, s32[16]{0:T(128)S(1)} %bitcast.53, bf16[2,8,256,256]{3,2,1,0:T(8,128)(2,1)S(1)} %bitcast.37, bf16[16,256,256]{2,1,0:T(8,128)(2,1)S(1)} %bitcast.43), custom_call_target="tpu_custom_call" | custom-call | flops 536870912 | bytes 5242880 | tf_op jit(solution)/shard_map/pallas_call | solution.py:419
  63.6 6.6 %collective-permute-done.10.a2_ref = bf16[528,256]{1,0:T(8,128)(2,1)} collective-permute-done((bf16[528,256]{1,0:T(8,128)(2,1)}, bf16[528,256]{1,0:T(8,128)(2,1)}, u32[]{:S(2)}, u32[]{:S(2)}) %collective-permute-start.10) | collective-permute-done | bytes 270368 | tf_op jit(solution)/shard_map/ppermute | solution.py:440
  70.2 2.0 %shard_map.100 = (f32[256,256]{1,0:T(8,128)S(1)}, bf16[256,256]{1,0:T(8,128)(2,1)}, bf16[256,256]{1,0:T(8,128)(2,1)}, bf16[256,256]{1,0:T(8,128)(2,1)}, f32[256,...) custom-call(bf16[4,256,256]{2,1,0:T(8,128)(2,1)S(1)} %get-tuple-element.66.stay_ref, ...), custom_call_target="tpu_custom_call" | custom-call | bytes 3145728 | tf_op jit(solution)/shard_map/pallas_call | solution.py:444
  72.2 1.0 collective-permute-start.15
  73.2 3.5 %collective-permute-start.13 = (bf16[256,256]{1,0:T(8,128)(2,1)}, bf16[256,256]{1,0:T(8,128)(2,1)S(1)}, u32[]{:S(2)}, u32[]{:S(2)}) collective-permute-start(bf16[256,256]{1,0:T(8,128)(2,1)} %get-tuple-element.74), channel_id=1, source_target_pairs={{0,2},{1,3},{2,0},{3,1},{4,6},{5,7},{6,4},{7,5},{8,10},{9,11},{10,... | collective-permute-start | bytes 393224 | tf_op jit(solution)/shard_map/ppermute | solution.py:458
  76.7 3.7 %collective-permute-done.12.refs_1_ = bf16[256,256]{1,0:T(8,128)(2,1)S(1)} collective-permute-done((bf16[256,256]{1,0:T(8,128)(2,1)}, bf16[256,256]{1,0:T(8,128)(2,1)S(1)}, u32[]{:S(2)}, u32[]{:S(2)}) %collective-permute-start.12) | collective-permute-done | bytes 131104 | tf_op jit(solution)/shard_map/ppermute | solution.py:458
  80.4 2.5 %collective-permute-done.13.refs_2_ = bf16[256,256]{1,0:T(8,128)(2,1)S(1)} collective-permute-done((bf16[256,256]{1,0:T(8,128)(2,1)}, bf16[256,256]{1,0:T(8,128)(2,1)S(1)}, u32[]{:S(2)}, u32[]{:S(2)}) %collective-permute-start.13) | collective-permute-done | bytes 131104 | tf_op jit(solution)/shard_map/ppermute | solution.py:458
  82.9 0.1 collective-permute-done.14.refs_3_
  82.9 1.1 shard_map.101
  84.1 1.8 %collective-permute-start.16 = (bf16[528,256]{1,0:T(8,128)(2,1)S(1)}, bf16[528,256]{1,0:T(8,128)(2,1)S(1)}, u32[]{:S(2)}, u32[]{:S(2)}) collective-permute-start(bf16[528,256]{1,0:T(8,128)(2,1)S(1)} %get-tuple-element.85.refs_0_), channel_id=1, source_target_pairs={{0,64},{8,72},{16,80},{24,88},{32,96},{40,104},{48,112},{56,120},{... | collective-permute-start | bytes 811016 | tf_op jit(solution)/shard_map/ppermute | solution.py:358
  85.8 2.7 %collective-permute-start.19 = (bf16[528,256]{1,0:T(8,128)(2,1)S(1)}, bf16[528,256]{1,0:T(8,128)(2,1)S(1)}, u32[]{:S(2)}, u32[]{:S(2)}) collective-permute-start(bf16[528,256]{1,0:T(8,128)(2,1)S(1)} %get-tuple-element.85.refs_0_), channel_id=1, source_target_pairs={{0,32},{8,40},{16,48},{24,56},{32,0},{40,8},{48,16},{56,24},{64,96... | collective-permute-start | bytes 811016 | tf_op jit(solution)/shard_map/ppermute | solution.py:359
  88.5 0.9 collective-permute-start.17
  89.4 1.1 collective-permute-start.18
  90.6 2.3 %collective-permute-done.16.refs_1_ = bf16[528,256]{1,0:T(8,128)(2,1)S(1)} collective-permute-done((bf16[528,256]{1,0:T(8,128)(2,1)S(1)}, bf16[528,256]{1,0:T(8,128)(2,1)S(1)}, u32[]{:S(2)}, u32[]{:S(2)}) %collective-permute-start.16) | collective-permute-done | bytes 270368 | tf_op jit(solution)/shard_map/ppermute | solution.py:358
  92.8 3.5 %collective-permute-start.20 = (bf16[528,256]{1,0:T(8,128)(2,1)S(1)}, bf16[528,256]{1,0:T(8,128)(2,1)S(1)}, u32[]{:S(2)}, u32[]{:S(2)}) collective-permute-start(bf16[528,256]{1,0:T(8,128)(2,1)S(1)} %collective-permute-done.16.refs_1_), channel_id=1, source_target_pairs={{0,48},{8,56},{16,0},{24,8},{32,16},{40,24},{48,32},{56,40},{64,11... | collective-permute-start | bytes 811016 | tf_op jit(solution)/shard_map/ppermute | solution.py:360
  96.3 0.4 collective-permute-done.19.refs_4_
  96.7 1.9 %collective-permute-start.22 = (bf16[528,256]{1,0:T(8,128)(2,1)S(1)}, bf16[528,256]{1,0:T(8,128)(2,1)S(1)}, u32[]{:S(2)}, u32[]{:S(2)}) collective-permute-start(bf16[528,256]{1,0:T(8,128)(2,1)S(1)} %collective-permute-done.19.refs_4_), channel_id=1, source_target_pairs={{0,64},{8,72},{16,80},{24,88},{32,96},{40,104},{48,112},{56,120},{... | collective-permute-start | bytes 811016 | tf_op jit(solution)/shard_map/ppermute | solution.py:361
  98.6 6.2 %shard_map.102 = (bf16[16,16,2,32,256]{4,3,2,1,0:T(8,128)(2,1)S(1)}, bf16[16,16,2,32,256]{4,3,2,1,0:T(8,128)(2,1)S(1)}) custom-call(bf16[16,16,2,32,256]{4,3,2,1,0:T(8,128)(2,1)} %w_ref.1, bf16[16,16,2,32,256]{4,3,2,1,0:T(8,128)(2,1)} %u_ref.2), custom_call_target="tpu_custom_call" | custom-call | bytes 33554432 | tf_op jit(solution)/shard_map/pallas_call | solution.py:375
  104.8 1.0 collective-permute-done.20.refs_5_
  105.8 3.7 %collective-permute-done.22.refs_7_ = bf16[528,256]{1,0:T(8,128)(2,1)S(1)} collective-permute-done((bf16[528,256]{1,0:T(8,128)(2,1)S(1)}, bf16[528,256]{1,0:T(8,128)(2,1)S(1)}, u32[]{:S(2)}, u32[]{:S(2)}) %collective-permute-start.22) | collective-permute-done | bytes 270368 | tf_op jit(solution)/shard_map/ppermute | solution.py:361
  109.5 0.3 shard_map.103.refs_0_
  109.8 0.1 collective-permute-start.23
  109.9 3.7 %shard_map.104 = (bf16[16,8,64,256]{3,2,1,0:T(8,128)(2,1)S(1)}, f32[16,256]{1,0:T(8,128)S(1)}) custom-call(s32[25]{0:T(128)S(1)} %stack.103.order_ref, s32[16,2,16]{2,1,0:T(2,128)S(1)} %bitcast.46, s32[8,16]{1,0:T(8,128)S(1)} %bitcast.50, s32[16]{0:T(128)S(1)} %bitcast.54, bf16[16,16,2,32,256]{4,3,2,1,0:T(8,128)(2,1)S(1)} %get-tuple-element.83.refs_8_.w_ref, ...), custom_call_target="tpu_custom_call" | custom-call | flops 1073741824 | bytes 16777216 | tf_op jit(solution)/shard_map/pallas_call | solution.py:390
  113.6 0.5 collective-permute-done.23.refs_0_
  114.1 7.1 %shard_map.105 = (bf16[4,256,256]{2,1,0:T(8,128)(2,1)}, bf16[4,256,256]{2,1,0:T(8,128)(2,1)S(1)}, bf16[528,256]{1,0:T(8,128)(2,1)}, bf16[528,256]{1,0:T(8,128)(2...) custom-call(s32[25]{0:T(128)S(1)} %stack.103.order_ref, s32[16,2,16]{2,1,0:T(2,128)S(1)} %bitcast.47, ...), custom_call_target="tpu_custom_call" | custom-call | flops 3221225472 | bytes 20971520 | tf_op jit(solution)/shard_map/pallas_call | solution.py:403
  121.3 0.7 copy-done.10
  122.0 0.6 collective-permute-start.24
  122.6 6.3 %collective-permute-start.26 = (bf16[528,256]{1,0:T(8,128)(2,1)}, bf16[528,256]{1,0:T(8,128)(2,1)}, u32[]{:S(2)}, u32[]{:S(2)}) collective-permute-start(bf16[528,256]{1,0:T(8,128)(2,1)} %get-tuple-element.94), channel_id=1, source_target_pairs={{0,2},{1,3},{2,0},{3,1},{4,6},{5,7},{6,4},{7,5},{8,10},{9,11},{10,... | collective-permute-start | bytes 811016 | tf_op jit(solution)/shard_map/ppermute | solution.py:440
  128.9 1.6 copy-done.7
  130.5 4.0 %shard_map.106.refs_7_ = f32[2,256,256]{2,1,0:T(8,128)S(1)} custom-call(s32[25]{0:T(128)S(1)} %stack.103.order_ref, s32[8,16]{1,0:T(8,128)S(1)} %bitcast.51, s32[16]{0:T(128)S(1)} %bitcast.55, bf16[2,8,256,256]{3,2,1,0:T(8,128)(2,1)S(1)} %bitcast.38, bf16[16,256,256]{2,1,0:T(8,128)(2,1)S(1)} %copy-done.7), custom_call_target="tpu_custom_call" | custom-call | flops 536870912 | bytes 5242880 | tf_op jit(solution)/shard_map/pallas_call | solution.py:419
  134.6 6.7 %collective-permute-done.26.a2_ref = bf16[528,256]{1,0:T(8,128)(2,1)} collective-permute-done((bf16[528,256]{1,0:T(8,128)(2,1)}, bf16[528,256]{1,0:T(8,128)(2,1)}, u32[]{:S(2)}, u32[]{:S(2)}) %collective-permute-start.26) | collective-permute-done | bytes 270368 | tf_op jit(solution)/shard_map/ppermute | solution.py:440
  141.3 2.2 %shard_map.107 = (f32[256,256]{1,0:T(8,128)S(1)}, bf16[256,256]{1,0:T(8,128)(2,1)}, bf16[256,256]{1,0:T(8,128)(2,1)}, bf16[256,256]{1,0:T(8,128)(2,1)}, f32[256,...) custom-call(bf16[4,256,256]{2,1,0:T(8,128)(2,1)S(1)} %get-tuple-element.90.stay_ref, ...), custom_call_target="tpu_custom_call" | custom-call | bytes 3145728 | tf_op jit(solution)/shard_map/pallas_call | solution.py:444
  143.5 0.8 collective-permute-start.31
  144.3 3.5 %collective-permute-start.29 = (bf16[256,256]{1,0:T(8,128)(2,1)}, bf16[256,256]{1,0:T(8,128)(2,1)S(1)}, u32[]{:S(2)}, u32[]{:S(2)}) collective-permute-start(bf16[256,256]{1,0:T(8,128)(2,1)} %get-tuple-element.98), channel_id=1, source_target_pairs={{0,2},{1,3},{2,0},{3,1},{4,6},{5,7},{6,4},{7,5},{8,10},{9,11},{10,... | collective-permute-start | bytes 393224 | tf_op jit(solution)/shard_map/ppermute | solution.py:458
  147.8 3.7 %collective-permute-done.28.refs_1_ = bf16[256,256]{1,0:T(8,128)(2,1)S(1)} collective-permute-done((bf16[256,256]{1,0:T(8,128)(2,1)}, bf16[256,256]{1,0:T(8,128)(2,1)S(1)}, u32[]{:S(2)}, u32[]{:S(2)}) %collective-permute-start.28) | collective-permute-done | bytes 131104 | tf_op jit(solution)/shard_map/ppermute | solution.py:458
  151.4 2.5 %collective-permute-done.29.refs_2_ = bf16[256,256]{1,0:T(8,128)(2,1)S(1)} collective-permute-done((bf16[256,256]{1,0:T(8,128)(2,1)}, bf16[256,256]{1,0:T(8,128)(2,1)S(1)}, u32[]{:S(2)}, u32[]{:S(2)}) %collective-permute-start.29) | collective-permute-done | bytes 131104 | tf_op jit(solution)/shard_map/ppermute | solution.py:458
  153.9 0.1 collective-permute-done.30.refs_3_
  154.0 1.0 shard_map.108
  (56 shorter events, 0.1 us)
Async XLA Ops:
  7.2 50.8 %all-gather.6.cloned.1.call-start = ((), (), s32[]{:S(2)}) async-start(), calls=%async_computation.1 | async-start | bytes 2359296 | tf_op jit(solution)/shard_map/all_gather | solution.py:434
  7.9 121.0 %all-gather.4.cloned.1.call-start = ((), (), s32[]{:S(2)}) async-start(), calls=%async_computation | async-start | bytes 2359296 | tf_op jit(solution)/shard_map/all_gather | solution.py:434
  9.9 9.8 %collective-permute-start = (bf16[528,256]{1,0:T(8,128)(2,1)}, bf16[528,256]{1,0:T(8,128)(2,1)S(1)}, u32[]{:S(2)}, u32[]{:S(2)}) collective-permute-start(bf16[528,256]{1,0:T(8,128)(2,1)} %shard_map.95.refs_0_), channel_id=1, source_target_pairs={{0,64},{8,72},{16,80},{24,88},{32,96},{40,104},{48,112},{56,120},{... | collective-permute-start | bytes 811016 | tf_op jit(solution)/shard_map/ppermute | solution.py:358
  13.0 11.5 %collective-permute-start.3 = (bf16[528,256]{1,0:T(8,128)(2,1)}, bf16[528,256]{1,0:T(8,128)(2,1)S(1)}, u32[]{:S(2)}, u32[]{:S(2)}) collective-permute-start(bf16[528,256]{1,0:T(8,128)(2,1)} %shard_map.95.refs_0_), channel_id=1, source_target_pairs={{0,32},{8,40},{16,48},{24,56},{32,0},{40,8},{48,16},{56,24},{64,96... | collective-permute-start | bytes 811016 | tf_op jit(solution)/shard_map/ppermute | solution.py:359
  16.9 16.4 %collective-permute-start.1 = (bf16[528,256]{1,0:T(8,128)(2,1)}, bf16[528,256]{1,0:T(8,128)(2,1)S(1)}, u32[]{:S(2)}, u32[]{:S(2)}) collective-permute-start(bf16[528,256]{1,0:T(8,128)(2,1)} %shard_map.95.refs_0_), channel_id=1, source_target_pairs={{0,48},{8,56},{16,0},{24,8},{32,16},{40,24},{48,32},{56,40},{64,11... | collective-permute-start | bytes 811016 | tf_op jit(solution)/shard_map/ppermute | solution.py:359
  17.6 15.7 %collective-permute-start.2 = (bf16[528,256]{1,0:T(8,128)(2,1)}, bf16[528,256]{1,0:T(8,128)(2,1)S(1)}, u32[]{:S(2)}, u32[]{:S(2)}) collective-permute-start(bf16[528,256]{1,0:T(8,128)(2,1)} %shard_map.95.refs_0_), channel_id=1, source_target_pairs={{0,16},{8,24},{16,32},{24,40},{32,48},{40,56},{48,0},{56,8},{64,80... | collective-permute-start | bytes 811016 | tf_op jit(solution)/shard_map/ppermute | solution.py:359
  19.7 16.0 %collective-permute-start.4 = (bf16[528,256]{1,0:T(8,128)(2,1)S(1)}, bf16[528,256]{1,0:T(8,128)(2,1)S(1)}, u32[]{:S(2)}, u32[]{:S(2)}) collective-permute-start(bf16[528,256]{1,0:T(8,128)(2,1)S(1)} %collective-permute-done.refs_1_), channel_id=1, source_target_pairs={{0,48},{8,56},{16,0},{24,8},{32,16},{40,24},{48,32},{56,40},{64,11... | collective-permute-start | bytes 811016 | tf_op jit(solution)/shard_map/ppermute | solution.py:360
  24.0 11.7 %collective-permute-start.5 = (bf16[528,256]{1,0:T(8,128)(2,1)S(1)}, bf16[528,256]{1,0:T(8,128)(2,1)S(1)}, u32[]{:S(2)}, u32[]{:S(2)}) collective-permute-start(bf16[528,256]{1,0:T(8,128)(2,1)S(1)} %collective-permute-done.refs_1_), channel_id=1, source_target_pairs={{0,16},{8,24},{16,32},{24,40},{32,48},{40,56},{48,0},{56,8},{64,80... | collective-permute-start | bytes 811016 | tf_op jit(solution)/shard_map/ppermute | solution.py:360
  24.5 13.8 %collective-permute-start.6 = (bf16[528,256]{1,0:T(8,128)(2,1)S(1)}, bf16[528,256]{1,0:T(8,128)(2,1)S(1)}, u32[]{:S(2)}, u32[]{:S(2)}) collective-permute-start(bf16[528,256]{1,0:T(8,128)(2,1)S(1)} %collective-permute-done.3.refs_4_), channel_id=1, source_target_pairs={{0,64},{8,72},{16,80},{24,88},{32,96},{40,104},{48,112},{56,120},{... | collective-permute-start | bytes 811016 | tf_op jit(solution)/shard_map/ppermute | solution.py:361
  27.1 11.2 %copy-start.8 = (bf16[528,256]{1,0:T(8,128)(2,1)S(1)}, bf16[528,256]{1,0:T(8,128)(2,1)}, u32[]{:S(2)}) copy-start(bf16[528,256]{1,0:T(8,128)(2,1)} %shard_map.95.refs_0_) | copy-start | bytes 811012
  33.3 5.3 %copy-start.1 = (bf16[16,16,2,32,256]{4,3,2,1,0:T(8,128)(2,1)}, bf16[16,16,2,32,256]{4,3,2,1,0:T(8,128)(2,1)S(1)}, u32[]{:S(2)}) copy-start(bf16[16,16,2,32,256]{4,3,2,1,0:T(8,128)(2,1)S(1)} %get-tuple-element.60.u_ref) | copy-start | bytes 25165828
  38.3 0.7 copy-start.14
  38.3 0.7 copy-start.15
  38.3 0.7 copy-start.16
  38.6 4.3 %collective-permute-start.7 = (bf16[8,528,256]{2,1,0:T(8,128)(2,1)S(1)}, bf16[8,528,256]{2,1,0:T(8,128)(2,1)S(1)}, u32[]{:S(2)}, u32[]{:S(2)}) collective-permute-start(bf16[8,528,256]{2,1,0:T(8,128)(2,1)S(1)} %shard_map.96.refs_0_), channel_id=1, source_target_pairs={{0,8},{8,0},{16,24},{24,16},{32,40},{40,32},{48,56},{56,48},{64,72... | collective-permute-start | bytes 6488072 | tf_op jit(solution)/shard_map/ppermute | solution.py:363
  39.0 4.0 %copy-start.2 = (bf16[16,16,2,32,256]{4,3,2,1,0:T(8,128)(2,1)S(1)}, bf16[16,16,2,32,256]{4,3,2,1,0:T(8,128)(2,1)}, u32[]{:S(2)}) copy-start(bf16[16,16,2,32,256]{4,3,2,1,0:T(8,128)(2,1)} %copy-done.1) | copy-start | bytes 25165828
  43.0 15.0 %copy-start = (bf16[1,2,8,256,256]{4,3,2,1,0:T(8,128)(2,1)S(1)}, bf16[1,2,8,256,256]{4,3,2,1,0:T(8,128)(2,1)}, u32[]{:S(2)}) copy-start(bf16[1,2,8,256,256]{4,3,2,1,0:T(8,128)(2,1)} %param.11) | copy-start | bytes 6291460
  50.0 0.7 copy-start.12
  50.7 32.2 %copy-start.5 = (bf16[1,2,256,256]{3,2,1,0:T(8,128)(2,1)S(1)}, bf16[1,2,256,256]{3,2,1,0:T(8,128)(2,1)}, u32[]{:S(2)}) copy-start(bf16[1,2,256,256]{3,2,1,0:T(8,128)(2,1)} %param.7) | copy-start | bytes 786436
  50.7 19.5 %collective-permute-start.8 = (bf16[4,256,256]{2,1,0:T(8,128)(2,1)}, bf16[4,256,256]{2,1,0:T(8,128)(2,1)S(1)}, u32[]{:S(2)}, u32[]{:S(2)}) collective-permute-start(bf16[4,256,256]{2,1,0:T(8,128)(2,1)} %get-tuple-element.67), channel_id=1, source_target_pairs={{0,4},{1,5},{2,6},{3,7},{4,0},{5,1},{6,2},{7,3},{8,12},{9,13},{10,... | collective-permute-start | bytes 1572872 | tf_op jit(solution)/shard_map/ppermute | solution.py:439
  52.7 10.9 %collective-permute-start.9 = (bf16[528,256]{1,0:T(8,128)(2,1)}, bf16[528,256]{1,0:T(8,128)(2,1)}, u32[]{:S(2)}, u32[]{:S(2)}) collective-permute-start(bf16[528,256]{1,0:T(8,128)(2,1)} %get-tuple-element.69), channel_id=1, source_target_pairs={{0,1},{1,2},{2,3},{3,0},{4,5},{5,6},{6,7},{7,4},{8,9},{9,10},{10,1... | collective-permute-start | bytes 811016 | tf_op jit(solution)/shard_map/ppermute | solution.py:440
  52.7 17.5 %collective-permute-start.10 = (bf16[528,256]{1,0:T(8,128)(2,1)}, bf16[528,256]{1,0:T(8,128)(2,1)}, u32[]{:S(2)}, u32[]{:S(2)}) collective-permute-start(bf16[528,256]{1,0:T(8,128)(2,1)} %get-tuple-element.70), channel_id=1, source_target_pairs={{0,2},{1,3},{2,0},{3,1},{4,6},{5,7},{6,4},{7,5},{8,10},{9,11},{10,... | collective-permute-start | bytes 811016 | tf_op jit(solution)/shard_map/ppermute | solution.py:440
  57.9 12.3 %collective-permute-start.11 = (bf16[528,256]{1,0:T(8,128)(2,1)}, bf16[528,256]{1,0:T(8,128)(2,1)}, u32[]{:S(2)}, u32[]{:S(2)}) collective-permute-start(bf16[528,256]{1,0:T(8,128)(2,1)} %get-tuple-element.71), channel_id=1, source_target_pairs={{0,3},{1,0},{2,1},{3,2},{4,7},{5,4},{6,5},{7,6},{8,11},{9,8},{10,9... | collective-permute-start | bytes 811016 | tf_op jit(solution)/shard_map/ppermute | solution.py:440
  57.9 1.6 copy-start.6
  59.5 10.7 %copy-start.13 = (bf16[528,256]{1,0:T(8,128)(2,1)S(1)}, bf16[528,256]{1,0:T(8,128)(2,1)}, u32[]{:S(2)}) copy-start(bf16[528,256]{1,0:T(8,128)(2,1)} %copy-done.12) | copy-start | bytes 811012
  72.2 10.7 %collective-permute-start.15 = (bf16[272,256]{1,0:T(8,128)(2,1)}, bf16[272,256]{1,0:T(8,128)(2,1)S(1)}, u32[]{:S(2)}, u32[]{:S(2)}) collective-permute-start(bf16[272,256]{1,0:T(8,128)(2,1)} %get-tuple-element.77), channel_id=1, source_target_pairs={{0,4},{1,5},{2,6},{3,7},{4,0},{5,1},{6,2},{7,3},{8,12},{9,13},{10,... | collective-permute-start | bytes 417800 | tf_op jit(solution)/shard_map/ppermute | solution.py:459
  73.2 7.2 %collective-permute-start.12 = (bf16[256,256]{1,0:T(8,128)(2,1)}, bf16[256,256]{1,0:T(8,128)(2,1)S(1)}, u32[]{:S(2)}, u32[]{:S(2)}) collective-permute-start(bf16[256,256]{1,0:T(8,128)(2,1)} %get-tuple-element.73), channel_id=1, source_target_pairs={{0,1},{1,2},{2,3},{3,0},{4,5},{5,6},{6,7},{7,4},{8,9},{9,10},{10,1... | collective-permute-start | bytes 393224 | tf_op jit(solution)/shard_map/ppermute | solution.py:458
  73.2 9.7 %collective-permute-start.13 = (bf16[256,256]{1,0:T(8,128)(2,1)}, bf16[256,256]{1,0:T(8,128)(2,1)S(1)}, u32[]{:S(2)}, u32[]{:S(2)}) collective-permute-start(bf16[256,256]{1,0:T(8,128)(2,1)} %get-tuple-element.74), channel_id=1, source_target_pairs={{0,2},{1,3},{2,0},{3,1},{4,6},{5,7},{6,4},{7,5},{8,10},{9,11},{10,... | collective-permute-start | bytes 393224 | tf_op jit(solution)/shard_map/ppermute | solution.py:458
  76.7 6.2 %collective-permute-start.14 = (bf16[256,256]{1,0:T(8,128)(2,1)}, bf16[256,256]{1,0:T(8,128)(2,1)S(1)}, u32[]{:S(2)}, u32[]{:S(2)}) collective-permute-start(bf16[256,256]{1,0:T(8,128)(2,1)} %get-tuple-element.75), channel_id=1, source_target_pairs={{0,3},{1,0},{2,1},{3,2},{4,7},{5,4},{6,5},{7,6},{8,11},{9,8},{10,9... | collective-permute-start | bytes 393224 | tf_op jit(solution)/shard_map/ppermute | solution.py:458
  84.1 8.8 %collective-permute-start.16 = (bf16[528,256]{1,0:T(8,128)(2,1)S(1)}, bf16[528,256]{1,0:T(8,128)(2,1)S(1)}, u32[]{:S(2)}, u32[]{:S(2)}) collective-permute-start(bf16[528,256]{1,0:T(8,128)(2,1)S(1)} %get-tuple-element.85.refs_0_), channel_id=1, source_target_pairs={{0,64},{8,72},{16,80},{24,88},{32,96},{40,104},{48,112},{56,120},{... | collective-permute-start | bytes 811016 | tf_op jit(solution)/shard_map/ppermute | solution.py:358
  85.8 10.9 %collective-permute-start.19 = (bf16[528,256]{1,0:T(8,128)(2,1)S(1)}, bf16[528,256]{1,0:T(8,128)(2,1)S(1)}, u32[]{:S(2)}, u32[]{:S(2)}) collective-permute-start(bf16[528,256]{1,0:T(8,128)(2,1)S(1)} %get-tuple-element.85.refs_0_), channel_id=1, source_target_pairs={{0,32},{8,40},{16,48},{24,56},{32,0},{40,8},{48,16},{56,24},{64,96... | collective-permute-start | bytes 811016 | tf_op jit(solution)/shard_map/ppermute | solution.py:359
  88.5 16.3 %collective-permute-start.17 = (bf16[528,256]{1,0:T(8,128)(2,1)S(1)}, bf16[528,256]{1,0:T(8,128)(2,1)S(1)}, u32[]{:S(2)}, u32[]{:S(2)}) collective-permute-start(bf16[528,256]{1,0:T(8,128)(2,1)S(1)} %get-tuple-element.85.refs_0_), channel_id=1, source_target_pairs={{0,48},{8,56},{16,0},{24,8},{32,16},{40,24},{48,32},{56,40},{64,11... | collective-permute-start | bytes 811016 | tf_op jit(solution)/shard_map/ppermute | solution.py:359
  89.4 15.3 %collective-permute-start.18 = (bf16[528,256]{1,0:T(8,128)(2,1)S(1)}, bf16[528,256]{1,0:T(8,128)(2,1)S(1)}, u32[]{:S(2)}, u32[]{:S(2)}) collective-permute-start(bf16[528,256]{1,0:T(8,128)(2,1)S(1)} %get-tuple-element.85.refs_0_), channel_id=1, source_target_pairs={{0,16},{8,24},{16,32},{24,40},{32,48},{40,56},{48,0},{56,8},{64,80... | collective-permute-start | bytes 811016 | tf_op jit(solution)/shard_map/ppermute | solution.py:359
  92.8 13.0 %collective-permute-start.20 = (bf16[528,256]{1,0:T(8,128)(2,1)S(1)}, bf16[528,256]{1,0:T(8,128)(2,1)S(1)}, u32[]{:S(2)}, u32[]{:S(2)}) collective-permute-start(bf16[528,256]{1,0:T(8,128)(2,1)S(1)} %collective-permute-done.16.refs_1_), channel_id=1, source_target_pairs={{0,48},{8,56},{16,0},{24,8},{32,16},{40,24},{48,32},{56,40},{64,11... | collective-permute-start | bytes 811016 | tf_op jit(solution)/shard_map/ppermute | solution.py:360
  96.3 9.5 %collective-permute-start.21 = (bf16[528,256]{1,0:T(8,128)(2,1)S(1)}, bf16[528,256]{1,0:T(8,128)(2,1)S(1)}, u32[]{:S(2)}, u32[]{:S(2)}) collective-permute-start(bf16[528,256]{1,0:T(8,128)(2,1)S(1)} %collective-permute-done.16.refs_1_), channel_id=1, source_target_pairs={{0,16},{8,24},{16,32},{24,40},{32,48},{40,56},{48,0},{56,8},{64,80... | collective-permute-start | bytes 811016 | tf_op jit(solution)/shard_map/ppermute | solution.py:360
  96.7 12.8 %collective-permute-start.22 = (bf16[528,256]{1,0:T(8,128)(2,1)S(1)}, bf16[528,256]{1,0:T(8,128)(2,1)S(1)}, u32[]{:S(2)}, u32[]{:S(2)}) collective-permute-start(bf16[528,256]{1,0:T(8,128)(2,1)S(1)} %collective-permute-done.19.refs_4_), channel_id=1, source_target_pairs={{0,64},{8,72},{16,80},{24,88},{32,96},{40,104},{48,112},{56,120},{... | collective-permute-start | bytes 811016 | tf_op jit(solution)/shard_map/ppermute | solution.py:361
  104.8 5.0 %copy-start.3 = (bf16[16,16,2,32,256]{4,3,2,1,0:T(8,128)(2,1)}, bf16[16,16,2,32,256]{4,3,2,1,0:T(8,128)(2,1)S(1)}, u32[]{:S(2)}) copy-start(bf16[16,16,2,32,256]{4,3,2,1,0:T(8,128)(2,1)S(1)} %get-tuple-element.84.u_ref) | copy-start | bytes 25165828
  109.8 4.3 %collective-permute-start.23 = (bf16[8,528,256]{2,1,0:T(8,128)(2,1)S(1)}, bf16[8,528,256]{2,1,0:T(8,128)(2,1)S(1)}, u32[]{:S(2)}, u32[]{:S(2)}) collective-permute-start(bf16[8,528,256]{2,1,0:T(8,128)(2,1)S(1)} %shard_map.103.refs_0_), channel_id=1, source_target_pairs={{0,8},{8,0},{16,24},{24,16},{32,40},{40,32},{48,56},{56,48},{64,72... | collective-permute-start | bytes 6488072 | tf_op jit(solution)/shard_map/ppermute | solution.py:363
  109.9 4.2 %copy-start.4 = (bf16[16,16,2,32,256]{4,3,2,1,0:T(8,128)(2,1)S(1)}, bf16[16,16,2,32,256]{4,3,2,1,0:T(8,128)(2,1)}, u32[]{:S(2)}) copy-start(bf16[16,16,2,32,256]{4,3,2,1,0:T(8,128)(2,1)} %copy-done.3) | copy-start | bytes 25165828
  114.1 39.8 %copy-start.9 = (f32[2,256,256]{2,1,0:T(8,128)S(1)}, f32[2,256,256]{2,1,0:T(8,128)}, u32[]{:S(2)}) copy-start(f32[2,256,256]{2,1,0:T(8,128)} %get-tuple-element.104.refs_9_) | copy-start | bytes 1572868
  121.2 0.7 copy-start.10
  122.0 19.3 %collective-permute-start.24 = (bf16[4,256,256]{2,1,0:T(8,128)(2,1)}, bf16[4,256,256]{2,1,0:T(8,128)(2,1)}, u32[]{:S(2)}, u32[]{:S(2)}) collective-permute-start(bf16[4,256,256]{2,1,0:T(8,128)(2,1)} %get-tuple-element.91), channel_id=1, source_target_pairs={{0,4},{1,5},{2,6},{3,7},{4,0},{5,1},{6,2},{7,3},{8,12},{9,13},{10,... | collective-permute-start | bytes 1572872 | tf_op jit(solution)/shard_map/ppermute | solution.py:439
  122.6 12.0 %collective-permute-start.25 = (bf16[528,256]{1,0:T(8,128)(2,1)}, bf16[528,256]{1,0:T(8,128)(2,1)}, u32[]{:S(2)}, u32[]{:S(2)}) collective-permute-start(bf16[528,256]{1,0:T(8,128)(2,1)} %get-tuple-element.93), channel_id=1, source_target_pairs={{0,1},{1,2},{2,3},{3,0},{4,5},{5,6},{6,7},{7,4},{8,9},{9,10},{10,1... | collective-permute-start | bytes 811016 | tf_op jit(solution)/shard_map/ppermute | solution.py:440
  122.6 18.7 %collective-permute-start.26 = (bf16[528,256]{1,0:T(8,128)(2,1)}, bf16[528,256]{1,0:T(8,128)(2,1)}, u32[]{:S(2)}, u32[]{:S(2)}) collective-permute-start(bf16[528,256]{1,0:T(8,128)(2,1)} %get-tuple-element.94), channel_id=1, source_target_pairs={{0,2},{1,3},{2,0},{3,1},{4,6},{5,7},{6,4},{7,5},{8,10},{9,11},{10,... | collective-permute-start | bytes 811016 | tf_op jit(solution)/shard_map/ppermute | solution.py:440
  128.9 12.4 %collective-permute-start.27 = (bf16[528,256]{1,0:T(8,128)(2,1)}, bf16[528,256]{1,0:T(8,128)(2,1)}, u32[]{:S(2)}, u32[]{:S(2)}) collective-permute-start(bf16[528,256]{1,0:T(8,128)(2,1)} %get-tuple-element.95), channel_id=1, source_target_pairs={{0,3},{1,0},{2,1},{3,2},{4,7},{5,4},{6,5},{7,6},{8,11},{9,8},{10,9... | collective-permute-start | bytes 811016 | tf_op jit(solution)/shard_map/ppermute | solution.py:440
  128.9 1.6 copy-start.7
  130.5 10.8 %copy-start.11 = (bf16[528,256]{1,0:T(8,128)(2,1)S(1)}, bf16[528,256]{1,0:T(8,128)(2,1)}, u32[]{:S(2)}) copy-start(bf16[528,256]{1,0:T(8,128)(2,1)} %copy-done.10) | copy-start | bytes 811012
  143.5 10.5 %collective-permute-start.31 = (bf16[272,256]{1,0:T(8,128)(2,1)}, bf16[272,256]{1,0:T(8,128)(2,1)S(1)}, u32[]{:S(2)}, u32[]{:S(2)}) collective-permute-start(bf16[272,256]{1,0:T(8,128)(2,1)} %get-tuple-element.101), channel_id=1, source_target_pairs={{0,4},{1,5},{2,6},{3,7},{4,0},{5,1},{6,2},{7,3},{8,12},{9,13},{10,... | collective-permute-start | bytes 417800 | tf_op jit(solution)/shard_map/ppermute | solution.py:459
  144.3 7.2 %collective-permute-start.28 = (bf16[256,256]{1,0:T(8,128)(2,1)}, bf16[256,256]{1,0:T(8,128)(2,1)S(1)}, u32[]{:S(2)}, u32[]{:S(2)}) collective-permute-start(bf16[256,256]{1,0:T(8,128)(2,1)} %get-tuple-element.97), channel_id=1, source_target_pairs={{0,1},{1,2},{2,3},{3,0},{4,5},{5,6},{6,7},{7,4},{8,9},{9,10},{10,1... | collective-permute-start | bytes 393224 | tf_op jit(solution)/shard_map/ppermute | solution.py:458
  144.3 9.7 %collective-permute-start.29 = (bf16[256,256]{1,0:T(8,128)(2,1)}, bf16[256,256]{1,0:T(8,128)(2,1)S(1)}, u32[]{:S(2)}, u32[]{:S(2)}) collective-permute-start(bf16[256,256]{1,0:T(8,128)(2,1)} %get-tuple-element.98), channel_id=1, source_target_pairs={{0,2},{1,3},{2,0},{3,1},{4,6},{5,7},{6,4},{7,5},{8,10},{9,11},{10,... | collective-permute-start | bytes 393224 | tf_op jit(solution)/shard_map/ppermute | solution.py:458
  147.8 6.2 %collective-permute-start.30 = (bf16[256,256]{1,0:T(8,128)(2,1)}, bf16[256,256]{1,0:T(8,128)(2,1)S(1)}, u32[]{:S(2)}, u32[]{:S(2)}) collective-permute-start(bf16[256,256]{1,0:T(8,128)(2,1)} %get-tuple-element.99), channel_id=1, source_target_pairs={{0,3},{1,0},{2,1},{3,2},{4,7},{5,4},{6,5},{7,6},{8,11},{9,8},{10,9... | collective-permute-start | bytes 393224 | tf_op jit(solution)/shard_map/ppermute | solution.py:458
Sparse Core Ops, SparseCore 0:
  9.6 46.0 all-gather.5
  84.2 41.0 all-gather.3
